TPU v7x, 32 devices: a whole 2x2x4 slice. The times are simulated.
32 devices in a mesh: seq: 8 (over z, y), head: 4 (over x, core).
Axes of the slice: x: 2, y: 2, z: 4, core: 2. Of those that a mesh axis runs over, the one named last changes fastest.
Arguments:
- query_vectors: bfloat16 [16384, 1024], P('seq', 'head'), may hold values from -6 to 6
- key_vectors: bfloat16 [16384, 128], P('seq'), may hold values from -6 to 6
- value_vectors: bfloat16 [16384, 128], P('seq'), may hold values from -6 to 6
- output_grad: bfloat16 [16384, 1024], P('seq', 'head'), may hold values from -48 to 48
- random_blocks: int32 [128, 3], P('seq'), may hold values from 0 to 127, as said below
- global_blocks: int32 [2], replicated, may hold values from 0 to 127
Outputs:
- query_grad: bfloat16 [16384, 1024], P('seq', 'head')
- key_grad: bfloat16 [16384, 128], P('seq')
- value_grad: bfloat16 [16384, 128], P('seq')
Inputs may be any that keep to these rules, and one draw needn't show every extreme that they name: `random_blocks`: take the query blocks in aligned runs of 16 and the key blocks in aligned runs of 16: all entries of one run of query blocks that fall into one run of key blocks name the same key block.
All inputs are finite; a program needn't handle non-finite values.
Results may differ from a plain program's by a relative error of at most 0.012.
Values may be sent and summed in bfloat16 or wider, within the bound.
No kernel may reach another device: no remote copies, remote signals or barrier semaphores. Data moves between devices by JAX's collectives and lax.ppermute only.
A program may use at most 128 MiB of HBM per device.

v0:
```python
import jax
import jax.numpy as jnp
from jax import lax
from jax.sharding import PartitionSpec as P

DH = 128
BLOCK = 128
R = 3
G = 2


def with_halo(value, sides, width):
    for axis, dim in sides:
        size, length = (lax.axis_size(axis), value.shape[dim])
        up = [(i, (i + 1) % size) for i in range(size - 1)]
        down = [(j, i) for i, j in up]
        last = lax.slice_in_dim(value, length - width, length, axis=dim)
        first = lax.slice_in_dim(value, 0, width, axis=dim)
        before = lax.ppermute(last, axis, up)
        after = lax.ppermute(first, axis, down)
        value = jnp.concatenate([before, value, after], axis=dim)
    return value


def from_root(value, axis, source):
    kept = jnp.where(lax.axis_index(axis) == source, value, 0).astype(value.dtype)
    return lax.psum(kept, axis)


def from_behind(block, axis, distance):
    devices = range(lax.axis_size(axis))
    route = [(i - distance, i) for i in devices if i - distance in devices]
    return lax.ppermute(block, axis, route)


def softmax_rows(scores):
    largest = jnp.max(scores, axis=-1, keepdims=True)
    powers = jnp.exp(scores - largest)
    return powers / jnp.sum(powers, axis=-1, keepdims=True)


def body(query_vectors, key_vectors, value_vectors, output_grad, random_blocks, global_blocks):
    seq_count = lax.axis_size("seq")
    seq_index = lax.axis_index("seq")
    rows_dev = query_vectors.shape[0]
    blocks_dev = rows_dev // BLOCK
    heads_dev = query_vectors.shape[1] // DH
    factor = float(DH) ** (-0.5)
    pair_width = 2 * DH
    listed = 3 + R + G
    group_size = 4
    rounds = blocks_dev // group_size
    key_value = jnp.concatenate([key_vectors, value_vectors], axis=1)
    pair_blocks = key_value.reshape(blocks_dev, BLOCK, pair_width)
    owners = random_blocks // blocks_dev
    within = random_blocks % blocks_dev
    peer_ids = jnp.arange(seq_count, dtype=jnp.int32)
    matched = owners[:, :, None] == peer_ids[None, None, :]
    wanted = jnp.max(jnp.where(matched, within[:, :, None], -1), axis=(0, 1))
    requested = lax.all_to_all(
        wanted.reshape(seq_count, 1), "seq", split_axis=0, concat_axis=0, tiled=True
    )[:, 0]
    served = pair_blocks[jnp.clip(requested, 0, blocks_dev - 1)]
    row_share = BLOCK // lax.axis_size("head")
    quarter = lax.dynamic_slice_in_dim(served, lax.axis_index("head") * row_share, row_share, 1)
    arrived = lax.all_to_all(quarter, "seq", split_axis=0, concat_axis=0, tiled=True)
    fetched = lax.all_gather(arrived, "head", axis=1, tiled=True)
    extended = with_halo(key_value, (("seq", 0),), BLOCK)
    extended = extended.reshape(blocks_dev + 2, BLOCK, pair_width)
    global_list = []
    for global_slot in range(G):
        target = global_blocks[global_slot]
        fragment = lax.dynamic_index_in_dim(pair_blocks, target % blocks_dev, 0, keepdims=False)
        global_list.append(from_root(fragment, "seq", target // blocks_dev))
    global_pairs = jnp.stack(global_list)
    first_block = seq_index * blocks_dev
    total_blocks = seq_count * blocks_dev
    query_blocks = query_vectors.reshape(blocks_dev, BLOCK, heads_dev, DH)
    grad_blocks = output_grad.reshape(blocks_dev, BLOCK, heads_dev, DH)

    def advance(totals, position):
        window_acc, random_acc, global_acc = totals
        offset = position * group_size
        beside_all = lax.dynamic_slice_in_dim(extended, offset, group_size + 2, 0)
        window_panels = jnp.stack(
            [
                beside_all[0:group_size],
                beside_all[1 : group_size + 1],
                beside_all[2 : group_size + 2],
            ],
            axis=1,
        )
        owner_rows = lax.dynamic_slice_in_dim(owners, offset, group_size, 0)
        remote_panels = fetched[owner_rows]
        global_part = jnp.broadcast_to(global_pairs[None], (group_size, G, BLOCK, pair_width))
        panels = jnp.concatenate([window_panels, remote_panels, global_part], axis=1)
        panels = panels.reshape(group_size, listed * BLOCK, pair_width)
        key_row_matrix = panels[:, :, :DH]
        value_row_matrix = panels[:, :, DH:]
        query_row_matrix = lax.dynamic_slice_in_dim(query_blocks, offset, group_size, 0)
        gradient_rows = lax.dynamic_slice_in_dim(grad_blocks, offset, group_size, 0)
        block_ids = first_block + offset + jnp.arange(group_size, dtype=jnp.int32)
        allowed = jnp.concatenate(
            [
                (block_ids > 0)[:, None],
                jnp.ones((group_size, 1), dtype=jnp.bool_),
                (block_ids < total_blocks - 1)[:, None],
                jnp.ones((group_size, R + G), dtype=jnp.bool_),
            ],
            axis=1,
        )
        visible = jnp.repeat(allowed, BLOCK, axis=1)
        scores = (
            jnp.einsum(
                "awst,axt->aswx",
                query_row_matrix,
                key_row_matrix,
                preferred_element_type=jnp.float32,
            )
            * factor
        )
        scores = jnp.where(visible[:, None, None, :], scores, -jnp.inf)
        attention = softmax_rows(scores)
        attention_reduced = attention.astype(jnp.bfloat16)
        outputs = jnp.einsum(
            "uwsn,unj->uswj",
            attention_reduced,
            value_row_matrix,
            preferred_element_type=jnp.float32,
        )
        row_delta = jnp.sum(gradient_rows.astype(jnp.float32) * outputs, axis=-1)
        prob_grad = jnp.einsum(
            "awst,axt->aswx", gradient_rows, value_row_matrix, preferred_element_type=jnp.float32
        )
        score_gradient = (
            attention * (prob_grad - jnp.transpose(row_delta, (0, 2, 1))[..., None])
        ).astype(jnp.bfloat16)
        query_part = (
            jnp.einsum(
                "uwsn,unj->uswj", score_gradient, key_row_matrix, preferred_element_type=jnp.float32
            )
            * factor
        ).astype(jnp.bfloat16)
        key_part = (
            jnp.einsum(
                "uwva,uvwp->uap",
                score_gradient,
                query_row_matrix,
                preferred_element_type=jnp.float32,
            )
            * factor
        )
        value_part = jnp.einsum(
            "uwva,uvwp->uap", attention_reduced, gradient_rows, preferred_element_type=jnp.float32
        )
        gradients = jnp.concatenate([key_part, value_part], axis=-1).reshape(
            group_size, listed, BLOCK, pair_width
        )
        spread = jnp.zeros((group_size + 2, BLOCK, pair_width), dtype=jnp.float32)
        spread = spread.at[0:group_size].add(gradients[:, 0])
        spread = spread.at[1 : group_size + 1].add(gradients[:, 1])
        spread = spread.at[2 : group_size + 2].add(gradients[:, 2])
        updated = lax.dynamic_slice_in_dim(window_acc, offset, group_size + 2, 0) + spread
        window_acc = lax.dynamic_update_slice_in_dim(window_acc, updated, offset, 0)
        onehot = (owner_rows[:, :, None] == peer_ids[None, None, :]).astype(jnp.float32)
        random_acc = random_acc + jnp.einsum(
            "brn,brxc->nxc", onehot, gradients[:, 3 : 3 + R], precision=lax.Precision.HIGHEST
        )
        global_acc = global_acc + jnp.sum(gradients[:, 3 + R :], axis=0)
        return (
            (window_acc, random_acc, global_acc),
            query_part.reshape(group_size, BLOCK, heads_dev * DH),
        )

    start_totals = (
        jnp.zeros((blocks_dev + 2, BLOCK, pair_width), dtype=jnp.float32),
        jnp.zeros((seq_count, BLOCK, pair_width), dtype=jnp.float32),
        jnp.zeros((G, BLOCK, pair_width), dtype=jnp.float32),
    )
    (window_acc, random_acc, global_acc), query_parts = lax.scan(
        advance, start_totals, jnp.arange(rounds, dtype=jnp.int32)
    )
    query_grad = query_parts.reshape(rows_dev, heads_dev * DH)
    into_last = from_behind(window_acc[0].astype(jnp.bfloat16), "seq", -1).astype(jnp.float32)
    into_first = from_behind(window_acc[blocks_dev + 1].astype(jnp.bfloat16), "seq", 1).astype(
        jnp.float32
    )
    local_sum = window_acc[1 : blocks_dev + 1]
    local_sum = local_sum.at[blocks_dev - 1].add(into_last)
    local_sum = local_sum.at[0].add(into_first)
    global_total_sum = lax.psum(global_acc, "seq")
    block_range = jnp.arange(blocks_dev, dtype=jnp.int32)
    owned_indicator = (
        (global_blocks[None, :] // blocks_dev == seq_index)
        & (global_blocks[None, :] % blocks_dev == block_range[:, None])
    ).astype(jnp.float32)
    local_sum = local_sum + jnp.einsum(
        "ar,rdi->adi", owned_indicator, global_total_sum, precision=lax.Precision.HIGHEST
    )
    served_hot = (requested[None, :] == block_range[:, None]).astype(jnp.float32)
    returned = lax.all_to_all(
        random_acc.astype(jnp.bfloat16), "seq", split_axis=0, concat_axis=0, tiled=True
    ).astype(random_acc.dtype)
    local_sum = local_sum + jnp.einsum(
        "je,exc->jxc", served_hot, returned, precision=lax.Precision.HIGHEST
    )
    finished = lax.psum(local_sum.astype(jnp.bfloat16), "head")
    finished = finished.reshape(rows_dev, pair_width)
    return (query_grad, finished[:, :DH], finished[:, DH:])


def solution(mesh):
    return jax.shard_map(
        body,
        mesh=mesh,
        in_specs=(
            P("seq", "head"),
            P("seq", None),
            P("seq", None),
            P("seq", "head"),
            P("seq", None),
            P(),
        ),
        out_specs=(P("seq", "head"), P("seq", None), P("seq", None)),
        check_vma=False,
    )
```

profile of v0, /device:TPU:5, one launch (start us, length us, event | category | flops | bytes accessed | tf_op | source)
XLA Modules:
  0.0 393.9 jit_solution(7123273942941622758)
XLA Ops:
  9.0 5.8 %all-to-all-start = ((s32[8,1,1]{2,1,0:T(1,128)}), s32[8,1,1]{2,1,0:T(1,128)S(1)}, u32[]{:S(2)}, u32[]{:S(2)}) async-start(s32[8,1,1]{2,1,0:T(1,128)} %copy.161), calls=%async_computation | async-start | bytes 8192 | tf_op jit(solution)/shard_map/all_to_all | solution.py:60
  17.9 3.1 collective-permute-start
  34.5 5.4 %all-to-all-start.1 = ((bf16[8,32,256]{2,1,0:T(8,128)(2,1)}), bf16[8,32,256]{2,1,0:T(8,128)(2,1)S(1)}, u32[]{:S(2)}, u32[]{:S(2)}) async-start(bf16[8,32,256]{2,1,0:T(8,128)(2,1)} %constant_dynamic-slice_fusion.3), calls=%async_computation.1 | async-start | bytes 262144 | tf_op jit(solution)/shard_map/all_to_all | solution.py:66
  40.1 59.3 %all-reduce.10.cloned.1.call-done = (bf16[1,128,256]{2,1,0:T(8,128)(2,1)}, bf16[1,128,256]{2,1,0:T(8,128)(2,1)}) async-done(((bf16[1,128,256]{2,1,0:T(8,128)(2,1)}, bf16[1,128,256]{2,1,0:T(8,128)(2,1)}), (bf16[1,128,256]{2,1,0:T(8,128)(2,1)}, bf16[1,128,256]{2,1,0:T(8,128)(2,1)})) %all-reduce.10.cloned.1.call-update) | async-done | bytes 131088 | tf_op jit(solution)/shard_map/psum | solution.py:27
  100.2 10.1 %all_gather.3 = bf16[8,128,256]{2,1,0:T(8,128)(2,1)} all-gather(bf16[8,32,256]{2,1,0:T(8,128)(2,1)S(1)} %all-to-all-done.1), channel_id=1, replica_groups=mesh['seq'=8,'head'=4] {'head'}, dimensions={1}, use_global_device_ids=true | all-gather | bytes 655360 | tf_op jit(solution)/shard_map/all_gather | solution.py:67
  112.0 146.1 %while.25 = (s32[]{:T(128)}, f32[18,128,256]{1,2,0:T(8,128)}, f32[8,128,256]{2,0,1:T(8,128)}, f32[2,128,256]{1,0,2:T(2,128)S(1)}, bf16[4,4,128,256]{3,2,1,0:T(8,...) while((s32[]{:T(128)}, f32[18,128,256]{1,2,0:T(8,128)}, ...), condition=%wide.region_8.9_spmd.clone, body=%wide.region_3.8_spmd.clone.sunk | while | flops 1664484608 | bytes 137012368 | solution.py:180
  124.7 3.0 copy.238
  127.8 2.9 slice_reduce_fusion.2
  131.8 7.1 %fusion.102 = (f32[4,1,128,256]{2,1,3,0:T(1,128)S(1)}, f32[4,1,128,256]{2,1,3,0:T(1,128)S(1)}, f32[4,1,128,256]{2,1,3,0:T(1,128)}) fusion(f32[4,8,128,256]{2,1,3,0:T(8,128)} %bitcast.196), kind=kLoop, calls=%fused_computation.110.clone.1 | loop fusion | bytes 3145728 | tf_op jit(solution)/shard_map/while/body/eval_jaxpr/slice | solution.py:162
  141.0 4.1 %fusion.104 = f32[8,128,256]{2,0,1:T(8,128)} fusion(f32[4,3,128,256]{3,0,1,2:T(4,128)} %copy.239, f32[8,128,256]{2,0,1:T(8,128)} %get-tuple-element.561, pred[]{:T(512)S(6)} %compare.58, s32[4,3]{0,1:T(4,128)S(1)} %copy.240), kind=kOutput, calls=%fused_computation.21.clone.1 | convolution fusion | flops 38273120 | bytes 3670065 | tf_op jit(solution)/shard_map/while/body/eval_jaxpr/brn,brxc->nxc/dot_general | solution.py:166
  161.0 3.0 copy.238
  168.1 7.1 %fusion.102 = (f32[4,1,128,256]{2,1,3,0:T(1,128)S(1)}, f32[4,1,128,256]{2,1,3,0:T(1,128)S(1)}, f32[4,1,128,256]{2,1,3,0:T(1,128)}) fusion(f32[4,8,128,256]{2,1,3,0:T(8,128)} %bitcast.196), kind=kLoop, calls=%fused_computation.110.clone.1 | loop fusion | bytes 3145728 | tf_op jit(solution)/shard_map/while/body/eval_jaxpr/slice | solution.py:162
  177.3 4.3 %fusion.104 = f32[8,128,256]{2,0,1:T(8,128)} fusion(f32[4,3,128,256]{3,0,1,2:T(4,128)} %copy.239, f32[8,128,256]{2,0,1:T(8,128)} %get-tuple-element.561, pred[]{:T(512)S(6)} %compare.58, s32[4,3]{0,1:T(4,128)S(1)} %copy.240), kind=kOutput, calls=%fused_computation.21.clone.1 | convolution fusion | flops 38273120 | bytes 3670065 | tf_op jit(solution)/shard_map/while/body/eval_jaxpr/brn,brxc->nxc/dot_general | solution.py:166
  197.6 3.0 copy.238
  204.7 7.1 %fusion.102 = (f32[4,1,128,256]{2,1,3,0:T(1,128)S(1)}, f32[4,1,128,256]{2,1,3,0:T(1,128)S(1)}, f32[4,1,128,256]{2,1,3,0:T(1,128)}) fusion(f32[4,8,128,256]{2,1,3,0:T(8,128)} %bitcast.196), kind=kLoop, calls=%fused_computation.110.clone.1 | loop fusion | bytes 3145728 | tf_op jit(solution)/shard_map/while/body/eval_jaxpr/slice | solution.py:162
  213.9 4.3 %fusion.104 = f32[8,128,256]{2,0,1:T(8,128)} fusion(f32[4,3,128,256]{3,0,1,2:T(4,128)} %copy.239, f32[8,128,256]{2,0,1:T(8,128)} %get-tuple-element.561, pred[]{:T(512)S(6)} %compare.58, s32[4,3]{0,1:T(4,128)S(1)} %copy.240), kind=kOutput, calls=%fused_computation.21.clone.1 | convolution fusion | flops 38273120 | bytes 3670065 | tf_op jit(solution)/shard_map/while/body/eval_jaxpr/brn,brxc->nxc/dot_general | solution.py:166
  234.2 3.0 copy.238
  237.3 2.9 slice_reduce_fusion.2
  241.3 7.1 %fusion.102 = (f32[4,1,128,256]{2,1,3,0:T(1,128)S(1)}, f32[4,1,128,256]{2,1,3,0:T(1,128)S(1)}, f32[4,1,128,256]{2,1,3,0:T(1,128)}) fusion(f32[4,8,128,256]{2,1,3,0:T(8,128)} %bitcast.196), kind=kLoop, calls=%fused_computation.110.clone.1 | loop fusion | bytes 3145728 | tf_op jit(solution)/shard_map/while/body/eval_jaxpr/slice | solution.py:162
  250.5 4.3 %fusion.104 = f32[8,128,256]{2,0,1:T(8,128)} fusion(f32[4,3,128,256]{3,0,1,2:T(4,128)} %copy.239, f32[8,128,256]{2,0,1:T(8,128)} %get-tuple-element.561, pred[]{:T(512)S(6)} %compare.58, s32[4,3]{0,1:T(4,128)S(1)} %copy.240), kind=kOutput, calls=%fused_computation.21.clone.1 | convolution fusion | flops 38273120 | bytes 3670065 | tf_op jit(solution)/shard_map/while/body/eval_jaxpr/brn,brxc->nxc/dot_general | solution.py:166
  260.6 4.6 %all-to-all-start.2 = ((bf16[8,128,256]{2,1,0:T(8,128)(2,1)}), bf16[8,128,256]{2,1,0:T(8,128)(2,1)S(1)}, u32[]{:S(2)}, u32[]{:S(2)}) async-start(bf16[8,128,256]{2,1,0:T(8,128)(2,1)} %copy.220), calls=%async_computation.2 | async-start | bytes 1048576 | tf_op jit(solution)/shard_map/all_to_all | solution.py:201
  276.5 4.2 %collective-permute-start.3 = (bf16[128,256]{1,0:T(8,128)(2,1)S(1)}, bf16[128,256]{1,0:T(8,128)(2,1)S(1)}, u32[]{:S(2)}, u32[]{:S(2)}) collective-permute-start(bf16[128,256]{1,0:T(8,128)(2,1)S(1)} %get-tuple-element.423), channel_id=1, source_target_pairs={{0,4},{4,8},{8,12},{12,16},{16,20},{20,24},{24,28},{1,5},{5,9},{9,... | collective-permute-start | bytes 196616 | tf_op jit(solution)/shard_map/ppermute | solution.py:33
  287.5 55.6 %all-reduce.6.cloned.1.call-done = f32[2,128,256]{2,0,1:T(2,128)} async-done(((f32[2,128,256]{2,0,1:T(2,128)}), f32[2,128,256]{2,0,1:T(2,128)}) %all-reduce.6.cloned.1.call-update) | async-done | bytes 262160 | tf_op jit(solution)/shard_map/psum | solution.py:191
  347.5 37.6 %all-reduce.8.cloned.1.call-done = bf16[2048,256]{1,0:T(8,128)(2,1)} async-done(((bf16[2048,256]{1,0:T(8,128)(2,1)}), bf16[2048,256]{1,0:T(8,128)(2,1)}) %all-reduce.8.cloned.1.call-update) | async-done | bytes 1048592 | tf_op jit(solution)/shard_map/psum | solution.py:207
  (271 shorter events, 122.5 us)
Async XLA Ops:
  7.2 16.0 %copy-start.9 = (s32[2]{0:T(128)S(1)}, s32[2]{0:T(128)}, u32[]{:S(2)}) copy-start(s32[2]{0:T(128)} %param.23) | copy-start | bytes 28
  7.2 22.9 %copy-start.7 = (bf16[2048,256]{1,0:T(8,128)(2,1)S(1)}, bf16[2048,256]{1,0:T(8,128)(2,1)}, u32[]{:S(2)}) copy-start(bf16[2048,256]{1,0:T(8,128)(2,1)} %param.18) | copy-start | bytes 3145732
  9.0 23.4 %all-to-all-start = ((s32[8,1,1]{2,1,0:T(1,128)}), s32[8,1,1]{2,1,0:T(1,128)S(1)}, u32[]{:S(2)}, u32[]{:S(2)}) async-start(s32[8,1,1]{2,1,0:T(1,128)} %copy.161), calls=%async_computation | async-start | bytes 8192 | tf_op jit(solution)/shard_map/all_to_all | solution.py:60
  14.8 84.5 %all-reduce.10.cloned.1.call-start = ((), (), s32[]{:S(2)}) async-start(), calls=%async_computation.5 | async-start | bytes 262144 | tf_op jit(solution)/shard_map/psum | solution.py:27
  15.9 15.4 %copy-start.8 = (bf16[2048,256]{1,0:T(8,128)(2,1)S(1)}, bf16[2048,256]{1,0:T(8,128)(2,1)}, u32[]{:S(2)}) copy-start(bf16[2048,256]{1,0:T(8,128)(2,1)} %param.21) | copy-start | bytes 3145732
  17.9 22.1 %collective-permute-start = (bf16[128,256]{1,0:T(8,128)(2,1)}, bf16[128,256]{1,0:T(8,128)(2,1)S(1)}, u32[]{:S(2)}, u32[]{:S(2)}) collective-permute-start(bf16[128,256]{1,0:T(8,128)(2,1)} %get-tuple-element.429), channel_id=1, source_target_pairs={{0,4},{4,8},{8,12},{12,16},{16,20},{20,24},{24,28},{1,5},{5,9},{9,... | collective-permute-start | bytes 196616 | tf_op jit(solution)/shard_map/ppermute | solution.py:19
  20.9 19.0 %collective-permute-start.1 = (bf16[128,256]{1,0:T(8,128)(2,1)}, bf16[128,256]{1,0:T(8,128)(2,1)S(1)}, u32[]{:S(2)}, u32[]{:S(2)}) collective-permute-start(bf16[128,256]{1,0:T(8,128)(2,1)} %get-tuple-element.430), channel_id=1, source_target_pairs={{4,0},{8,4},{12,8},{16,12},{20,16},{24,20},{28,24},{5,1},{9,5},{13... | collective-permute-start | bytes 196616 | tf_op jit(solution)/shard_map/ppermute | solution.py:20
  34.5 65.7 %all-to-all-start.1 = ((bf16[8,32,256]{2,1,0:T(8,128)(2,1)}), bf16[8,32,256]{2,1,0:T(8,128)(2,1)S(1)}, u32[]{:S(2)}, u32[]{:S(2)}) async-start(bf16[8,32,256]{2,1,0:T(8,128)(2,1)} %constant_dynamic-slice_fusion.3), calls=%async_computation.1 | async-start | bytes 262144 | tf_op jit(solution)/shard_map/all_to_all | solution.py:66
  112.0 5.0 %copy-start.5 = (bf16[18,128,256]{2,1,0:T(8,128)(2,1)}, bf16[18,128,256]{2,1,0:T(8,128)(2,1)S(1)}, u32[]{:S(2)}) copy-start(bf16[18,128,256]{2,1,0:T(8,128)(2,1)S(1)} %get-tuple-element.589) | copy-start | bytes 3538948 | tf_op jit(solution)/shard_map/while
  130.7 8.1 %copy-start = (f32[128,8,8,128]{3,2,1,0:T(8,128)S(1)}, f32[128,8,8,128]{3,2,1,0:T(8,128)}, u32[]{:S(2)}) copy-start(f32[128,8,8,128]{3,2,1,0:T(8,128)} %copy.238) | copy-start | bytes 12582916 | tf_op jit(solution)/shard_map/while
  148.3 5.0 %copy-start.5 = (bf16[18,128,256]{2,1,0:T(8,128)(2,1)}, bf16[18,128,256]{2,1,0:T(8,128)(2,1)S(1)}, u32[]{:S(2)}) copy-start(bf16[18,128,256]{2,1,0:T(8,128)(2,1)S(1)} %get-tuple-element.589) | copy-start | bytes 3538948 | tf_op jit(solution)/shard_map/while
  167.0 8.1 %copy-start = (f32[128,8,8,128]{3,2,1,0:T(8,128)S(1)}, f32[128,8,8,128]{3,2,1,0:T(8,128)}, u32[]{:S(2)}) copy-start(f32[128,8,8,128]{3,2,1,0:T(8,128)} %copy.238) | copy-start | bytes 12582916 | tf_op jit(solution)/shard_map/while
  184.9 5.0 %copy-start.5 = (bf16[18,128,256]{2,1,0:T(8,128)(2,1)}, bf16[18,128,256]{2,1,0:T(8,128)(2,1)S(1)}, u32[]{:S(2)}) copy-start(bf16[18,128,256]{2,1,0:T(8,128)(2,1)S(1)} %get-tuple-element.589) | copy-start | bytes 3538948 | tf_op jit(solution)/shard_map/while
  203.7 8.1 %copy-start = (f32[128,8,8,128]{3,2,1,0:T(8,128)S(1)}, f32[128,8,8,128]{3,2,1,0:T(8,128)}, u32[]{:S(2)}) copy-start(f32[128,8,8,128]{3,2,1,0:T(8,128)} %copy.238) | copy-start | bytes 12582916 | tf_op jit(solution)/shard_map/while
  221.5 5.0 %copy-start.5 = (bf16[18,128,256]{2,1,0:T(8,128)(2,1)}, bf16[18,128,256]{2,1,0:T(8,128)(2,1)S(1)}, u32[]{:S(2)}) copy-start(bf16[18,128,256]{2,1,0:T(8,128)(2,1)S(1)} %get-tuple-element.589) | copy-start | bytes 3538948 | tf_op jit(solution)/shard_map/while
  240.2 8.1 %copy-start = (f32[128,8,8,128]{3,2,1,0:T(8,128)S(1)}, f32[128,8,8,128]{3,2,1,0:T(8,128)}, u32[]{:S(2)}) copy-start(f32[128,8,8,128]{3,2,1,0:T(8,128)} %copy.238) | copy-start | bytes 12582916 | tf_op jit(solution)/shard_map/while
  258.1 7.0 %copy-start.4 = (f32[18,128,256]{1,2,0:T(8,128)S(1)}, f32[18,128,256]{1,2,0:T(8,128)}, u32[]{:S(2)}) copy-start(f32[18,128,256]{1,2,0:T(8,128)} %get-tuple-element.283) | copy-start | bytes 7077892
  260.6 25.0 %all-to-all-start.2 = ((bf16[8,128,256]{2,1,0:T(8,128)(2,1)}), bf16[8,128,256]{2,1,0:T(8,128)(2,1)S(1)}, u32[]{:S(2)}, u32[]{:S(2)}) async-start(bf16[8,128,256]{2,1,0:T(8,128)(2,1)} %copy.220), calls=%async_computation.2 | async-start | bytes 1048576 | tf_op jit(solution)/shard_map/all_to_all | solution.py:201
  265.1 78.0 %all-reduce.6.cloned.1.call-start = ((), (), s32[]{:S(2)}) async-start(), calls=%async_computation.3 | async-start | bytes 524288 | tf_op jit(solution)/shard_map/psum | solution.py:191
  269.0 11.7 %collective-permute-start.2 = (bf16[128,256]{1,0:T(8,128)(2,1)S(1)}, bf16[128,256]{1,0:T(8,128)(2,1)S(1)}, u32[]{:S(2)}, u32[]{:S(2)}) collective-permute-start(bf16[128,256]{1,0:T(8,128)(2,1)S(1)} %get-tuple-element.424), channel_id=1, source_target_pairs={{4,0},{8,4},{12,8},{16,12},{20,16},{24,20},{28,24},{5,1},{9,5},{13... | collective-permute-start | bytes 196616 | tf_op jit(solution)/shard_map/ppermute | solution.py:33
  274.2 11.3 %copy-start.11 = (s32[8]{0:T(128)S(1)}, s32[8]{0:T(128)}, u32[]{:S(2)}) copy-start(s32[8]{0:T(128)} %get-tuple-element.382) | copy-start | bytes 100
  274.2 110.9 %all-reduce.8.cloned.1.call-start = ((), (), s32[]{:S(2)}) async-start(), calls=%async_computation.4 | async-start | bytes 2097152 | tf_op jit(solution)/shard_map/psum | solution.py:207
  276.5 66.6 %copy-start.12 = (s32[2]{0:T(128)S(1)}, s32[2]{0:T(128)}, u32[]{:S(2)}) copy-start(s32[2]{0:T(128)} %and_select_fusion) | copy-start | bytes 28
  276.5 7.1 %collective-permute-start.3 = (bf16[128,256]{1,0:T(8,128)(2,1)S(1)}, bf16[128,256]{1,0:T(8,128)(2,1)S(1)}, u32[]{:S(2)}, u32[]{:S(2)}) collective-permute-start(bf16[128,256]{1,0:T(8,128)(2,1)S(1)} %get-tuple-element.423), channel_id=1, source_target_pairs={{0,4},{4,8},{8,12},{12,16},{16,20},{20,24},{24,28},{1,5},{5,9},{9,... | collective-permute-start | bytes 196616 | tf_op jit(solution)/shard_map/ppermute | solution.py:33
  (17 other events, 45.8 us)
Sparse Core Ops, SparseCore 0:
  29.7 69.5 all-reduce.9
  274.3 68.7 all-reduce.5
  347.6 37.4 all-reduce.7
where the time goes:
time: 397 us; the launch traced here: 394 us
  waiting for transfers between devices  153 us (39%)
  local copies, waits for them, and re-layouts  108 us (27%)
  matrix products  40.7 us (10%)
  other arithmetic  32.2 us (8%)
  starting transfers between devices  27.3 us (7%)
  between operations  19.1 us (5%)
  blocking collectives  10.1 us (3%)
    psum x1, waiting for transfers between devices, from_root(): return lax.psum(kept, axis)  59.3 us
    psum x1, waiting for transfers between devices, body(): global_total_sum = lax.psum(global_acc, 'seq')  55.6 us
    psum x1, waiting for transfers between devices, body(): finished = lax.psum(local_sum.astype(jnp.bfloat16), 'head')  37.6 us
    while x80, local copies, waits for them, and re-layouts  30.7 us
    slice x4, local copies, waits for them, and re-layouts, advance(): spread = spread.at[2:group_size + 2].add(gradients[:, 2])  28.2 us
    dot_general x4, matrix products, advance(): jnp.einsum('brn,brxc->nxc', onehot, gradients[:, 3:3 + R], precision=lax....  17.1 us
    reduce_sum x4, other arithmetic, advance(): global_acc = global_acc + jnp.sum(gradients[:, 3 + R:], axis=0)  11.8 us
    all_gather x1, blocking collectives, body(): fetched = lax.all_gather(arrived, 'head', axis=1, tiled=True)  10.1 us
  transfers between devices with their start and end apart: 10, of which 3 were waited for; matrix products, arithmetic and copies ran while one was open for 7% of the time, Pallas kernels for 0%

commit v1 on v0

v1 whole, which is shorter than its diff:
```python
import functools
import math

import jax
import jax.numpy as jnp
from jax import lax
from jax.experimental import pallas as pl
from jax.experimental.pallas import tpu as pltpu
from jax.sharding import PartitionSpec as P

DH = 128
BLOCK = 128
R = 3
G = 2
WINDOW = 3
LISTED = WINDOW + R + G
PER_STEP = 2
VMEM_LIMIT = 56 * 1024 * 1024
MASKED = -1e30
FACTOR = float(DH) ** -0.5
LOG2E = math.log2(math.e)

NT = (((1,), (1,)), ((), ()))
NN = (((1,), (0,)), ((), ()))


def mm(a, b, dims):
    return lax.dot_general(a, b, dims, preferred_element_type=jnp.float32)


def stack_heads(rows):
    heads = rows.shape[1] // DH
    return jnp.concatenate([rows[:, h * DH : (h + 1) * DH] for h in range(heads)], axis=0)


def serve_kernel(requested, k_ref, v_ref, out_ref):
    half = BLOCK // 2
    core = lax.rem(lax.axis_index("head"), 2)
    last = k_ref.shape[0] // BLOCK - 1

    def one(j, carry):
        start = pl.multiple_of(jnp.clip(requested[j], 0, last) * BLOCK + core * half, half)
        out_ref[j, 0] = k_ref[pl.ds(start, half), :]
        out_ref[j, 1] = v_ref[pl.ds(start, half), :]
        return carry

    lax.fori_loop(0, out_ref.shape[0], one, 0)


def attend_kernel(
    owners,
    q_ref,
    g_ref,
    k_ref,
    v_ref,
    before_ref,
    after_ref,
    mine_ref,
    other_ref,
    glob_mine_ref,
    glob_other_ref,
    ds_ref,
    pw_ref,
    keep_ref,
    send_ref,
    k_all,
    v_all,
    acc,
):
    blocks = k_ref.shape[0] // BLOCK
    peers = mine_ref.shape[0]
    half = BLOCK // 2
    core = lax.rem(lax.axis_index("head"), 2)
    seq_index = lax.axis_index("seq")
    step = pl.program_id(0)
    first_random = blocks + 2
    first_global = first_random + peers
    halo_slot = peers + G

    @pl.when(step == 0)
    def _():
        for all_ref, own_ref, which in ((k_all, k_ref, 0), (v_all, v_ref, 1)):
            all_ref[0] = before_ref[which]
            all_ref[blocks + 1] = after_ref[which]
            all_ref[1 : blocks + 1] = own_ref[...].reshape(blocks, BLOCK, DH)
            for j in range(peers):
                all_ref[first_random + j, pl.ds(core * half, half), :] = mine_ref[j, which]
                all_ref[first_random + j, pl.ds((1 - core) * half, half), :] = other_ref[j, which]
            for j in range(G):
                all_ref[first_global + j, pl.ds(core * half, half), :] = glob_mine_ref[j, which]
                all_ref[first_global + j, pl.ds((1 - core) * half, half), :] = glob_other_ref[j, which]
        acc[...] = jnp.zeros_like(acc)

    for u in range(PER_STEP):
        b = step * PER_STEP + u
        q = stack_heads(q_ref[u * BLOCK : (u + 1) * BLOCK, :])
        g = stack_heads(g_ref[u * BLOCK : (u + 1) * BLOCK, :])
        places = [owners[b * R + r] for r in range(R)]

        def listed(all_ref):
            parts = [all_ref[pl.ds(b, WINDOW)].reshape(WINDOW * BLOCK, DH)]
            parts += [all_ref[first_random + o] for o in places]
            parts += [all_ref[first_global + j] for j in range(G)]
            return jnp.concatenate(parts, axis=0)

        s = mm(listed(k_all), q, NT)
        dp = mm(listed(v_all), g, NT)
        no_left = jnp.logical_and(seq_index == 0, b == 0)
        no_right = jnp.logical_and(seq_index == lax.axis_size("seq") - 1, b == blocks - 1)
        left = jnp.where(no_left, MASKED, 0.0)
        right = jnp.where(no_right, MASKED, 0.0)
        spans = [(0, 1, left), (1, 2, None), (2, 3, right), (3, LISTED, None)]
        m = None
        for lo, hi, bias in spans:
            t = jnp.max(s[lo * BLOCK : hi * BLOCK], axis=0, keepdims=True)
            if bias is not None:
                t = t + bias
            m = t if m is None else jnp.maximum(m, t)
        scale = FACTOR * LOG2E
        mc = m * scale
        parts = []
        for lo, hi, bias in spans:
            off = mc if bias is None else mc - bias
            parts.append(jnp.exp2(s[lo * BLOCK : hi * BLOCK] * scale - off))
        e = jnp.concatenate(parts, axis=0)
        l = jnp.sum(e, axis=0, keepdims=True)
        d = jnp.sum(e * dp, axis=0, keepdims=True)
        inv = 1.0 / l
        delta = d * inv
        p = e * inv
        pb = p.astype(jnp.bfloat16)
        ds = (p * (dp - delta)).astype(jnp.bfloat16)
        ds_ref[u] = ds
        pw_ref[u] = pb[: WINDOW * BLOCK]
        tail = WINDOW * BLOCK
        dk = mm(ds[tail:], q, NN)
        dv = mm(pb[tail:], g, NN)
        for i in range(R + G):
            slot = places[i] if i < R else peers + i - R
            acc[slot, 0] += dk[i * BLOCK : (i + 1) * BLOCK]
            acc[slot, 1] += dv[i * BLOCK : (i + 1) * BLOCK]

        if u == 0:

            @pl.when(b == 0)
            def _():
                acc[halo_slot, 0] = mm(ds[:BLOCK], q, NN)
                acc[halo_slot, 1] = mm(pb[:BLOCK], g, NN)

        if u == PER_STEP - 1:

            @pl.when(b == blocks - 1)
            def _():
                acc[halo_slot + 1, 0] = mm(ds[2 * BLOCK : 3 * BLOCK], q, NN)
                acc[halo_slot + 1, 1] = mm(pb[2 * BLOCK : 3 * BLOCK], g, NN)

    @pl.when(step == pl.num_programs(0) - 1)
    def _():
        for which, f in ((0, FACTOR), (1, 1.0)):
            keep_ref[:, which] = acc[:, which, pl.ds(core * half, half), :] * f
            send_ref[:, which] = (acc[:, which, pl.ds((1 - core) * half, half), :] * f).astype(jnp.bfloat16)


def window_kernel(
    owners,
    q_ref,
    g_ref,
    k_ref,
    before_ref,
    after_ref,
    mine_ref,
    other_ref,
    glob_mine_ref,
    glob_other_ref,
    ds_ref,
    pw_ref,
    dq_ref,
    keep_ref,
    send_ref,
    kt_all,
    acc,
):
    blocks = k_ref.shape[0] // BLOCK
    peers = mine_ref.shape[0]
    half = BLOCK // 2
    core = lax.rem(lax.axis_index("head"), 2)
    step = pl.program_id(0)
    first_random = blocks + 2
    first_global = first_random + peers

    @pl.when(step == 0)
    def _():
        kt_all[0] = before_ref[0].T
        kt_all[blocks + 1] = after_ref[0].T

        def own(j, carry):
            kt_all[j + 1] = k_ref[pl.ds(pl.multiple_of(j * BLOCK, BLOCK), BLOCK), :].T
            return carry

        lax.fori_loop(0, blocks, own, 0)

        def joined(a, b):
            low = jnp.where(core == 0, a, b)
            high = jnp.where(core == 0, b, a)
            return jnp.concatenate([low, high], axis=0).T

        def fetched(j, carry):
            kt_all[first_random + j] = joined(mine_ref[j, 0], other_ref[j, 0])
            return carry

        lax.fori_loop(0, peers, fetched, 0)
        for j in range(G):
            kt_all[first_global + j] = joined(glob_mine_ref[j, 0], glob_other_ref[j, 0])
        acc[...] = jnp.zeros_like(acc)

    for u in range(PER_STEP):
        b = step * PER_STEP + u
        q = stack_heads(q_ref[u * BLOCK : (u + 1) * BLOCK, :])
        g = stack_heads(g_ref[u * BLOCK : (u + 1) * BLOCK, :])
        parts = [kt_all[b + w] for w in range(WINDOW)]
        parts += [kt_all[first_random + owners[b * R + r]] for r in range(R)]
        parts += [kt_all[first_global + j] for j in range(G)]
        ds = ds_ref[u]
        dqt = mm(jnp.concatenate(parts, axis=1), ds, NN) * FACTOR
        heads = q_ref.shape[1] // DH
        for h in range(heads):
            dq_ref[u * BLOCK : (u + 1) * BLOCK, h * DH : (h + 1) * DH] = (
                dqt[:, h * BLOCK : (h + 1) * BLOCK].T.astype(jnp.bfloat16)
            )
        dk = mm(ds[: WINDOW * BLOCK], q, NN).reshape(WINDOW, BLOCK, DH)
        dv = mm(pw_ref[u], g, NN).reshape(WINDOW, BLOCK, DH)
        acc[pl.ds(b, WINDOW), 0] += dk
        acc[pl.ds(b, WINDOW), 1] += dv

    @pl.when(step == pl.num_programs(0) - 1)
    def _():
        for which, f in ((0, FACTOR), (1, 1.0)):
            keep_ref[:, which] = acc[1 : blocks + 1, which, pl.ds(core * half, half), :] * f
            send_ref[:, which] = (
                acc[1 : blocks + 1, which, pl.ds((1 - core) * half, half), :] * f
            ).astype(jnp.bfloat16)


def whole(shape):
    return pl.BlockSpec(shape, lambda i, *_: (0,) * len(shape))


def partners(size, stride):
    return [(i, i ^ stride) for i in range(size)]


def body(query_vectors, key_vectors, value_vectors, output_grad, random_blocks, global_blocks):
    seq_count = lax.axis_size("seq")
    seq_index = lax.axis_index("seq")
    head_count = lax.axis_size("head")
    head_index = lax.axis_index("head")
    rows_dev, columns = query_vectors.shape
    blocks = rows_dev // BLOCK
    half = BLOCK // 2
    steps = blocks // PER_STEP
    stacked = PER_STEP * BLOCK
    lanes = columns // DH * BLOCK
    bf16 = jnp.bfloat16
    core = head_index % 2
    core_pairs = partners(head_count, 1)
    slots = seq_count + G + 2

    owners = random_blocks // blocks
    within = random_blocks % blocks
    peer_ids = jnp.arange(seq_count, dtype=jnp.int32)
    matched = owners[:, :, None] == peer_ids[None, None, :]
    wanted = jnp.max(jnp.where(matched, within[:, :, None], -1), axis=(0, 1))
    requested = lax.all_to_all(
        wanted.reshape(seq_count, 1), "seq", split_axis=0, concat_axis=0, tiled=True
    )[:, 0]
    owner_list = owners.reshape(-1)

    up = [(i, i + 1) for i in range(seq_count - 1)]
    down = [(i + 1, i) for i in range(seq_count - 1)]
    last = jnp.stack([key_vectors[-BLOCK:], value_vectors[-BLOCK:]])
    first = jnp.stack([key_vectors[:BLOCK], value_vectors[:BLOCK]])
    before = lax.ppermute(last, "seq", up)
    after = lax.ppermute(first, "seq", down)

    def half_block(index):
        start = index * BLOCK + core * half
        return jnp.stack(
            [lax.dynamic_slice_in_dim(a, start, half, 0) for a in (key_vectors, value_vectors)]
        )

    global_part = jnp.stack([half_block(global_blocks[j] % blocks) for j in range(G)])
    spread = lax.all_to_all(
        jnp.broadcast_to(global_part[None], (seq_count,) + global_part.shape),
        "seq",
        split_axis=0,
        concat_axis=0,
        tiled=True,
    )
    glob_mine = jnp.stack(
        [
            lax.dynamic_index_in_dim(spread[:, j], global_blocks[j] // blocks, 0, keepdims=False)
            for j in range(G)
        ]
    )
    glob_other = lax.ppermute(glob_mine, "head", core_pairs)

    vmem = pl.BlockSpec(memory_space=pltpu.VMEM)
    served = pl.pallas_call(
        serve_kernel,
        out_shape=jax.ShapeDtypeStruct((seq_count, 2, half, DH), bf16),
        in_specs=[pl.BlockSpec(memory_space=pltpu.SMEM), vmem, vmem],
        out_specs=vmem,
        name="serve",
    )(requested, key_vectors, value_vectors)
    mine = lax.all_to_all(served, "seq", split_axis=0, concat_axis=0, tiled=True)
    other = lax.ppermute(mine, "head", core_pairs)

    block_rows = pl.BlockSpec((stacked, columns), lambda i, *_: (i, 0))
    fetched_specs = [
        whole(before.shape),
        whole(after.shape),
        whole(mine.shape),
        whole(other.shape),
        whole(glob_mine.shape),
        whole(glob_other.shape),
    ]
    fetched = (before, after, mine, other, glob_mine, glob_other)
    ds_spec = pl.BlockSpec((PER_STEP, LISTED * BLOCK, lanes), lambda i, *_: (i, 0, 0))
    pw_spec = pl.BlockSpec((PER_STEP, WINDOW * BLOCK, lanes), lambda i, *_: (i, 0, 0))
    piece = (slots, 2, half, DH)
    all_blocks = blocks + 2 + seq_count + G
    unit = 2 * blocks * lanes * LISTED * BLOCK * DH
    params = pltpu.CompilerParams(
        dimension_semantics=("arbitrary",), vmem_limit_bytes=VMEM_LIMIT
    )
    ds, pw, keep, send = pl.pallas_call(
        attend_kernel,
        out_shape=(
            jax.ShapeDtypeStruct((blocks, LISTED * BLOCK, lanes), bf16),
            jax.ShapeDtypeStruct((blocks, WINDOW * BLOCK, lanes), bf16),
            jax.ShapeDtypeStruct(piece, jnp.float32),
            jax.ShapeDtypeStruct(piece, bf16),
        ),
        grid_spec=pltpu.PrefetchScalarGridSpec(
            num_scalar_prefetch=1,
            grid=(steps,),
            in_specs=[block_rows, block_rows, whole(key_vectors.shape), whole(value_vectors.shape)]
            + fetched_specs,
            out_specs=(ds_spec, pw_spec, whole(piece), whole(piece)),
            scratch_shapes=[
                pltpu.VMEM((all_blocks, BLOCK, DH), bf16),
                pltpu.VMEM((all_blocks, BLOCK, DH), bf16),
                pltpu.VMEM((slots, 2, BLOCK, DH), jnp.float32),
            ],
        ),
        compiler_params=params,
        cost_estimate=pl.CostEstimate(
            flops=4 * unit, bytes_accessed=16 << 20, transcendentals=blocks * lanes * LISTED * BLOCK
        ),
        name="attend",
    )(owner_list, query_vectors, output_grad, key_vectors, value_vectors, *fetched)

    piece_w = (blocks, 2, half, DH)
    query_grad, keep_w, send_w = pl.pallas_call(
        window_kernel,
        out_shape=(
            jax.ShapeDtypeStruct(query_vectors.shape, bf16),
            jax.ShapeDtypeStruct(piece_w, jnp.float32),
            jax.ShapeDtypeStruct(piece_w, bf16),
        ),
        grid_spec=pltpu.PrefetchScalarGridSpec(
            num_scalar_prefetch=1,
            grid=(steps,),
            in_specs=[block_rows, block_rows, whole(key_vectors.shape)]
            + fetched_specs
            + [ds_spec, pw_spec],
            out_specs=(block_rows, whole(piece_w), whole(piece_w)),
            scratch_shapes=[
                pltpu.VMEM((all_blocks, BLOCK, DH), bf16),
                pltpu.VMEM((blocks + 2, 2, BLOCK, DH), jnp.float32),
            ],
        ),
        compiler_params=params,
        cost_estimate=pl.CostEstimate(flops=2 * unit, bytes_accessed=16 << 20, transcendentals=0),
        name="window",
    )(owner_list, query_vectors, output_grad, key_vectors, *fetched, ds, pw)

    def reduced(kept, sent):
        total = kept + lax.ppermute(sent, "head", core_pairs).astype(jnp.float32)
        stride = 2
        while stride < head_count:
            size = total.shape[2] // 2
            bit = (head_index // stride) % 2
            away = lax.dynamic_slice_in_dim(total, (1 - bit) * size, size, 2).astype(bf16)
            home = lax.dynamic_slice_in_dim(total, bit * size, size, 2)
            total = home + lax.ppermute(away, "head", partners(head_count, stride)).astype(
                jnp.float32
            )
            stride *= 2
        return total

    shared = reduced(keep, send)
    share = shared.shape[2]
    shared_low = shared.astype(bf16)
    terms = jnp.concatenate(
        [
            shared_low[:seq_count].reshape(seq_count, 2, share, DH),
            jnp.broadcast_to(
                shared_low[seq_count : seq_count + G].reshape(1, 2 * G, share, DH),
                (seq_count, 2 * G, share, DH),
            ),
        ],
        axis=1,
    )
    returned = lax.all_to_all(terms, "seq", split_axis=0, concat_axis=0, tiled=True).astype(
        jnp.float32
    )
    into_last = lax.ppermute(shared_low[seq_count + G], "seq", down).astype(jnp.float32)
    into_first = lax.ppermute(shared_low[seq_count + G + 1], "seq", up).astype(jnp.float32)
    total = reduced(keep_w, send_w)
    block_range = jnp.arange(blocks, dtype=jnp.int32)
    served_hot = (requested[None, :] == block_range[:, None]).astype(jnp.float32)
    total = total + jnp.einsum(
        "je,ewrd->jwrd", served_hot, returned[:, :2], precision=lax.Precision.HIGHEST
    )
    global_sum = jnp.sum(returned[:, 2:], axis=0).reshape(G, 2, share, DH)
    owned = (global_blocks[None, :] == seq_index * blocks + block_range[:, None]).astype(jnp.float32)
    for j in range(G):
        total = total + owned[:, j][:, None, None, None] * global_sum[j][None]
    total = total.at[blocks - 1].add(into_last)
    total = total.at[0].add(into_first)

    held = total.astype(bf16)
    stride = head_count // 2
    while stride >= 1:
        there = lax.ppermute(held, "head", partners(head_count, stride))
        bit = (head_index // stride) % 2
        low = jnp.where(bit == 0, held, there)
        high = jnp.where(bit == 0, there, held)
        held = jnp.concatenate([low, high], axis=2)
        stride //= 2
    return (
        query_grad,
        held[:, 0].reshape(rows_dev, DH),
        held[:, 1].reshape(rows_dev, DH),
    )


def solution(mesh):
    return jax.shard_map(
        body,
        mesh=mesh,
        in_specs=(
            P("seq", "head"),
            P("seq", None),
            P("seq", None),
            P("seq", "head"),
            P("seq", None),
            P(),
        ),
        out_specs=(P("seq", "head"), P("seq", None), P("seq", None)),
        check_vma=False,
    )
```

time: 397 us -> 123 us (0.31)
  waiting for transfers between devices: 153 us -> 14.3 us
  local copies, waits for them, and re-layouts: 108 us -> 6.11 us
  Pallas kernels: 0 us -> 40.5 us
  matrix products: 40.7 us -> 0.34 us
  other arithmetic: 32.2 us -> 6.95 us
  between operations: 19.1 us -> 6.16 us
  starting transfers between devices: 27.3 us -> 37.1 us
    psum x3 -> x0, waiting for transfers between devices: 153 us -> none  [the longest x1 59.3 us: from_root(): return lax.psum(kept, axis)]
    pallas_call x0 -> x3, Pallas kernels: none -> 40.5 us  [the longest x1 24.8 us: body(): pl.pallas_call(attend_kernel, out_shape=(jax.ShapeDtypeStruct((blocks, LI...]
    dot_general x30 -> x1, matrix products: 40.7 us -> 0.34 us  [body(): jnp.einsum('je,ewrd->jwrd', served_hot, returned[:, :2], precision=lax.Pr...]
    while x84 -> x0, local copies, waits for them, and re-layouts: 38.4 us -> none
    slice x12 -> x6, local copies, waits for them, and re-layouts: 35.7 us -> 1.42 us  [the longest x1 1.34 us: body(): global_blocks[j] % blocks]
    reduce_sum x4 -> x1, other arithmetic: 11.8 us -> 0.04 us  [body(): global_sum = jnp.sum(returned[:, 2:], axis=0).reshape(G, 2, share, DH)]
    ppermute x4 -> x12, starting transfers between devices: 11.4 us -> 22.8 us  [the longest x1 3.96 us: body(): glob_other = lax.ppermute(glob_mine, 'head', core_pairs)]
    all_gather x1 -> x0, blocking collectives: 10.1 us -> none  [body(): fetched = lax.all_gather(arrived, 'head', axis=1, tiled=True)]
  transfers between devices with their start and end apart: 10 -> 15, of which waited for: 3 -> 6; matrix products, arithmetic and copies ran while one was open for 7% -> 6% of each run, Pallas kernels for 0% -> 11%
where the time goes in v1:
time: 123 us; the launch traced here: 121 us
  Pallas kernels  40.5 us (33%)
  starting transfers between devices  37.1 us (30%)
  waiting for transfers between devices  14.3 us (12%)
  blocking collectives  9.69 us (8%)
  other arithmetic  6.95 us (6%)
  between operations  6.16 us (5%)
  local copies, waits for them, and re-layouts  6.11 us (5%)
    pallas_call x1, Pallas kernels, body(): pl.pallas_call(attend_kernel, out_shape=(jax.ShapeDtypeStruct((blocks, LI...  24.8 us
    pallas_call x1, Pallas kernels, body(): pl.pallas_call(window_kernel, out_shape=(jax.ShapeDtypeStruct(query_vecto...  13.7 us
    all_to_all x1, blocking collectives, body(): lax.all_to_all(wanted.reshape(seq_count, 1), 'seq', split_axis=0, concat_...  9.69 us
    ppermute x2, waiting for transfers between devices, body(): there = lax.ppermute(held, 'head', partners(head_count, stride))  7.91 us
    all_to_all x1, starting transfers between devices, body(): lax.all_to_all(jnp.broadcast_to(global_part[None], (seq_count,) + global_...  5.48 us
    all_to_all x1, starting transfers between devices, body(): lax.all_to_all(served, 'seq', split_axis=0, concat_axis=0, tiled=True)  4.51 us
    all_to_all x1, starting transfers between devices, body(): lax.all_to_all(terms, 'seq', split_axis=0, concat_axis=0, tiled=True)  4.36 us
    all_to_all x1, waiting for transfers between devices, body(): lax.all_to_all(terms, 'seq', split_axis=0, concat_axis=0, tiled=True)  4.17 us
  transfers between devices with their start and end apart: 15, of which 6 were waited for; matrix products, arithmetic and copies ran while one was open for 6% of the time, Pallas kernels for 11%

profile of v1, /device:TPU:5, one launch (start us, length us, event | category | flops | bytes accessed | tf_op | source)
XLA Modules:
  0.0 121.2 jit_solution(2746642950627330864)
XLA Ops:
  1.5 9.7 %all_to_all.24 = s32[8,1,1]{2,1,0:T(1,128)S(1)} all-to-all(s32[8,1,1]{2,1,0:T(1,128)S(1)} %copy.32), channel_id=1, replica_groups=mesh['seq'=8,'head'=4] {'seq'}, dimensions={0} | all-to-all | bytes 64 | tf_op jit(solution)/shard_map/all_to_all | solution.py:273
  12.0 2.0 %serve.1 = bf16[8,2,64,128]{3,2,1,0:T(8,128)(2,1)} custom-call(s32[8]{0:T(128)} %reduce.4.requested, bf16[2048,128]{1,0:T(8,128)(2,1)} %k_ref.5, bf16[2048,128]{1,0:T(8,128)(2,1)} %v_ref.3), custom_call_target="tpu_custom_call" | custom-call | tf_op jit(solution)/shard_map/serve/pallas_call | solution.py:308
  14.0 4.5 %all-to-all-start.1 = ((bf16[8,2,64,128]{3,2,1,0:T(8,128)(2,1)}), bf16[8,2,64,128]{3,2,1,0:T(8,128)(2,1)S(1)}, u32[]{:S(2)}, u32[]{:S(2)}) async-start(bf16[8,2,64,128]{3,2,1,0:T(8,128)(2,1)} %serve.1), calls=%async_computation.1 | async-start | bytes 524288 | tf_op jit(solution)/shard_map/all_to_all | solution.py:315
  18.5 1.3 %fusion.13 = (s32[1]{0:T(128)}, s32[1]{0:T(128)}) fusion(s32[2]{0:T(128)} %param.15), kind=kLoop, calls=%fused_computation.62 | loop fusion | bytes 16 | tf_op jit(solution)/shard_map/slice | solution.py:291
  24.5 0.9 broadcast_in_dim.20
  25.4 5.5 %all-to-all-start.2 = ((bf16[8,2,2,64,128]{4,3,2,1,0:T(8,128)(2,1)}), bf16[8,2,2,64,128]{4,3,2,1,0:T(8,128)(2,1)S(1)}, u32[]{:S(2)}, u32[]{:S(2)}) async-start(bf16[8,2,2,64,128]{4,3,2,1,0:T(8,128)(2,1)} %broadcast_in_dim.20), calls=%async_computation.2 | async-start | bytes 1048576 | tf_op jit(solution)/shard_map/all_to_all | solution.py:292
  31.7 3.1 %collective-permute-start = (bf16[2,128,128]{2,1,0:T(8,128)(2,1)S(1)}, bf16[2,128,128]{2,1,0:T(8,128)(2,1)S(1)}, u32[]{:S(2)}, u32[]{:S(2)}) collective-permute-start(bf16[2,128,128]{2,1,0:T(8,128)(2,1)S(1)} %pad_maximum_fusion.3), channel_id=1, source_target_pairs={{0,4},{4,8},{8,12},{12,16},{16,20},{20,24},{24,28},{1,5},{5,9},{9,... | collective-permute-start | bytes 196616 | tf_op jit(solution)/shard_map/ppermute | solution.py:282
  34.8 2.2 %collective-permute-start.1 = (bf16[2,128,128]{2,1,0:T(8,128)(2,1)S(1)}, bf16[2,128,128]{2,1,0:T(8,128)(2,1)S(1)}, u32[]{:S(2)}, u32[]{:S(2)}) collective-permute-start(bf16[2,128,128]{2,1,0:T(8,128)(2,1)S(1)} %pad_maximum_fusion.4), channel_id=1, source_target_pairs={{4,0},{8,4},{12,8},{16,12},{20,16},{24,20},{28,24},{5,1},{9,5},{13... | collective-permute-start | bytes 196616 | tf_op jit(solution)/shard_map/ppermute | solution.py:283
  38.3 3.6 %collective-permute-start.2 = (bf16[8,2,64,128]{3,2,1,0:T(8,128)(2,1)S(1)}, bf16[8,2,64,128]{3,2,1,0:T(8,128)(2,1)S(1)}, u32[]{:S(2)}, u32[]{:S(2)}) collective-permute-start(bf16[8,2,64,128]{3,2,1,0:T(8,128)(2,1)S(1)} %all-to-all-done.1.mine_ref), channel_id=1, source_target_pairs={{0,1},{1,0},{2,3},{3,2},{4,5},{5,4},{6,7},{7,6},{8,9},{9,8},{10,11... | collective-permute-start | bytes 786440 | tf_op jit(solution)/shard_map/ppermute | solution.py:316
  42.3 4.0 %collective-permute-start.3 = (bf16[2,2,64,128]{3,2,1,0:T(8,128)(2,1)S(1)}, bf16[2,2,64,128]{3,2,1,0:T(8,128)(2,1)S(1)}, u32[]{:S(2)}, u32[]{:S(2)}) collective-permute-start(bf16[2,2,64,128]{3,2,1,0:T(8,128)(2,1)S(1)} %pad_maximum_fusion.6.glob_mine_ref), channel_id=1, source_target_pairs={{0,1},{1,0},{2,3},{3,2},{4,5},{5,4},{6,7},{7,6},{8,9},{9,8},{10,11... | collective-permute-start | bytes 196616 | tf_op jit(solution)/shard_map/ppermute | solution.py:305
  48.4 24.8 %attend.1 = (bf16[16,1024,256]{2,1,0:T(8,128)(2,1)}, bf16[16,384,256]{2,1,0:T(8,128)(2,1)}, f32[12,2,64,128]{3,2,1,0:T(8,128)}, bf16[12,2,64,128]{3,2,1,0:T(8,128)(2,1)}) custom-call(s32[48]{0:T(128)} %reshape.110.owners, bf16[2048,256]{1,0:T(8,128)(2,1)} %q_ref.3, bf16[2048,256]{1,0:T(8,128)(2,1)} %g_ref.3, bf16[2048,128]{1,0:T(8,128)(2,1)} %k_ref.5, ...), custom_call_target="tpu_custom_call" | custom-call | flops 4294967296 | bytes 16777216 | tf_op jit(solution)/shard_map/attend/pallas_call | solution.py:336
  73.4 1.8 %collective-permute-done.6 = bf16[12,2,64,128]{3,2,1,0:T(8,128)(2,1)S(1)} collective-permute-done((bf16[12,2,64,128]{3,2,1,0:T(8,128)(2,1)}, bf16[12,2,64,128]{3,2,1,0:T(8,128)(2,1)S(1)}, u32[]{:S(2)}, u32[]{:S(2)}) %collective-permute-start.6) | collective-permute-done | bytes 393248 | tf_op jit(solution)/shard_map/ppermute | solution.py:389
  75.2 1.2 %convert_add_fusion.1 = f32[12,2,64,128]{3,2,1,0:T(8,128)S(1)} fusion(f32[12,2,64,128]{3,2,1,0:T(8,128)} %get-tuple-element.39, bf16[12,2,64,128]{3,2,1,0:T(8,128)(2,1)S(1)} %collective-permute-done.6), kind=kLoop, calls=%fused_computation.3 | loop fusion | flops 393216 | bytes 1966080 | tf_op jit(solution)/shard_map/add | solution.py:389
  76.5 1.3 %collective-permute-start.7 = (bf16[12,2,32,128]{3,2,1,0:T(8,128)(2,1)S(1)}, bf16[12,2,32,128]{3,2,1,0:T(8,128)(2,1)S(1)}, u32[]{:S(2)}, u32[]{:S(2)}) collective-permute-start(bf16[12,2,32,128]{3,2,1,0:T(8,128)(2,1)S(1)} %dynamic-slice_convert_fusion.1), channel_id=1, source_target_pairs={{0,2},{1,3},{2,0},{3,1},{4,6},{5,7},{6,4},{7,5},{8,10},{9,11},{10,... | collective-permute-start | bytes 589832 | tf_op jit(solution)/shard_map/ppermute | solution.py:396
  77.8 13.7 %window.1 = (bf16[2048,256]{1,0:T(8,128)(2,1)}, f32[16,2,64,128]{3,2,1,0:T(8,128)}, bf16[16,2,64,128]{3,2,1,0:T(8,128)(2,1)}) custom-call(s32[48]{0:T(128)} %reshape.110.owners, bf16[2048,256]{1,0:T(8,128)(2,1)} %q_ref.3, bf16[2048,256]{1,0:T(8,128)(2,1)} %g_ref.3, bf16[2048,128]{1,0:T(8,128)(2,1)} %k_ref.5, bf16[2,128,128]{2,1,0:T(8,128)(2,1)} %copy-done.3, ...), custom_call_target="tpu_custom_call" | custom-call | flops 2147483648 | bytes 16777216 | tf_op jit(solution)/shard_map/window/pallas_call | solution.py:364
  92.9 4.4 %all-to-all-start.3 = ((bf16[8,6,32,128]{3,2,1,0:T(8,128)(2,1)}), bf16[8,6,32,128]{3,2,1,0:T(8,128)(2,1)S(1)}, u32[]{:S(2)}, u32[]{:S(2)}) async-start(bf16[8,6,32,128]{3,2,1,0:T(8,128)(2,1)} %pad_maximum_fusion.2), calls=%async_computation.3 | async-start | bytes 786432 | tf_op jit(solution)/shard_map/all_to_all | solution.py:415
  97.3 1.4 %convert_add_fusion = f32[16,2,64,128]{3,2,1,0:T(8,128)S(1)} fusion(f32[16,2,64,128]{3,2,1,0:T(8,128)} %get-tuple-element.37, bf16[16,2,64,128]{3,2,1,0:T(8,128)(2,1)S(1)} %collective-permute-done.4), kind=kLoop, calls=%fused_computation.2 | loop fusion | flops 524288 | bytes 2621440 | tf_op jit(solution)/shard_map/add | solution.py:389
  99.0 3.1 %collective-permute-start.9 = (bf16[2,32,128]{2,1,0:T(8,128)(2,1)S(1)}, bf16[2,32,128]{2,1,0:T(8,128)(2,1)S(1)}, u32[]{:S(2)}, u32[]{:S(2)}) collective-permute-start(bf16[2,32,128]{2,1,0:T(8,128)(2,1)S(1)} %get-tuple-element.57), channel_id=1, source_target_pairs={{0,4},{4,8},{8,12},{12,16},{16,20},{20,24},{24,28},{1,5},{5,9},{9,... | collective-permute-start | bytes 49160 | tf_op jit(solution)/shard_map/ppermute | solution.py:419
  102.1 2.2 %collective-permute-start.8 = (bf16[2,32,128]{2,1,0:T(8,128)(2,1)S(1)}, bf16[2,32,128]{2,1,0:T(8,128)(2,1)S(1)}, u32[]{:S(2)}, u32[]{:S(2)}) collective-permute-start(bf16[2,32,128]{2,1,0:T(8,128)(2,1)S(1)} %get-tuple-element.58), channel_id=1, source_target_pairs={{4,0},{8,4},{12,8},{16,12},{20,16},{24,20},{28,24},{5,1},{9,5},{13... | collective-permute-start | bytes 49160 | tf_op jit(solution)/shard_map/ppermute | solution.py:418
  104.3 4.2 %all-to-all-done.3 = bf16[8,6,32,128]{3,2,1,0:T(8,128)(2,1)S(1)} async-done(((bf16[8,6,32,128]{3,2,1,0:T(8,128)(2,1)}), bf16[8,6,32,128]{3,2,1,0:T(8,128)(2,1)S(1)}, u32[]{:S(2)}, u32[]{:S(2)}) %all-to-all-start.3) | async-done | bytes 393248 | tf_op jit(solution)/shard_map/all_to_all | solution.py:415
  109.6 6.4 %collective-permute-done.10 = bf16[16,2,32,128]{3,2,1,0:T(8,128)(2,1)S(1)} collective-permute-done((bf16[16,2,32,128]{3,2,1,0:T(8,128)(2,1)S(1)}, bf16[16,2,32,128]{3,2,1,0:T(8,128)(2,1)S(1)}, u32[]{:S(2)}, u32[]{:S(2)}) %collective-permute-start.10) | collective-permute-done | bytes 262176 | tf_op jit(solution)/shard_map/ppermute | solution.py:436
  116.1 2.1 %collective-permute-start.11 = (bf16[16,2,64,128]{3,2,1,0:T(8,128)(2,1)S(1)}, bf16[16,2,64,128]{3,2,1,0:T(8,128)(2,1)S(1)}, u32[]{:S(2)}, u32[]{:S(2)}) collective-permute-start(bf16[16,2,64,128]{3,2,1,0:T(8,128)(2,1)S(1)} %pad_maximum_fusion.1), channel_id=1, source_target_pairs={{0,1},{1,0},{2,3},{3,2},{4,5},{5,4},{6,7},{7,6},{8,9},{9,8},{10,11... | collective-permute-start | bytes 1572872 | tf_op jit(solution)/shard_map/ppermute | solution.py:436
  118.3 1.5 %collective-permute-done.11 = bf16[16,2,64,128]{3,2,1,0:T(8,128)(2,1)S(1)} collective-permute-done((bf16[16,2,64,128]{3,2,1,0:T(8,128)(2,1)S(1)}, bf16[16,2,64,128]{3,2,1,0:T(8,128)(2,1)S(1)}, u32[]{:S(2)}, u32[]{:S(2)}) %collective-permute-start.11) | collective-permute-done | bytes 524320 | tf_op jit(solution)/shard_map/ppermute | solution.py:436
  120.1 1.1 pad_maximum_fusion
  (70 shorter events, 9.2 us)
Async XLA Ops:
  14.0 10.5 %all-to-all-start.1 = ((bf16[8,2,64,128]{3,2,1,0:T(8,128)(2,1)}), bf16[8,2,64,128]{3,2,1,0:T(8,128)(2,1)S(1)}, u32[]{:S(2)}, u32[]{:S(2)}) async-start(bf16[8,2,64,128]{3,2,1,0:T(8,128)(2,1)} %serve.1), calls=%async_computation.1 | async-start | bytes 524288 | tf_op jit(solution)/shard_map/all_to_all | solution.py:315
  24.5 22.7 %copy-start = (bf16[8,2,64,128]{3,2,1,0:T(8,128)(2,1)}, bf16[8,2,64,128]{3,2,1,0:T(8,128)(2,1)S(1)}, u32[]{:S(2)}) copy-start(bf16[8,2,64,128]{3,2,1,0:T(8,128)(2,1)S(1)} %all-to-all-done.1.mine_ref) | copy-start | bytes 786436
  25.4 16.8 %all-to-all-start.2 = ((bf16[8,2,2,64,128]{4,3,2,1,0:T(8,128)(2,1)}), bf16[8,2,2,64,128]{4,3,2,1,0:T(8,128)(2,1)S(1)}, u32[]{:S(2)}, u32[]{:S(2)}) async-start(bf16[8,2,2,64,128]{4,3,2,1,0:T(8,128)(2,1)} %broadcast_in_dim.20), calls=%async_computation.2 | async-start | bytes 1048576 | tf_op jit(solution)/shard_map/all_to_all | solution.py:292
  31.7 15.2 %collective-permute-start = (bf16[2,128,128]{2,1,0:T(8,128)(2,1)S(1)}, bf16[2,128,128]{2,1,0:T(8,128)(2,1)S(1)}, u32[]{:S(2)}, u32[]{:S(2)}) collective-permute-start(bf16[2,128,128]{2,1,0:T(8,128)(2,1)S(1)} %pad_maximum_fusion.3), channel_id=1, source_target_pairs={{0,4},{4,8},{8,12},{12,16},{16,20},{20,24},{24,28},{1,5},{5,9},{9,... | collective-permute-start | bytes 196616 | tf_op jit(solution)/shard_map/ppermute | solution.py:282
  34.8 12.1 %collective-permute-start.1 = (bf16[2,128,128]{2,1,0:T(8,128)(2,1)S(1)}, bf16[2,128,128]{2,1,0:T(8,128)(2,1)S(1)}, u32[]{:S(2)}, u32[]{:S(2)}) collective-permute-start(bf16[2,128,128]{2,1,0:T(8,128)(2,1)S(1)} %pad_maximum_fusion.4), channel_id=1, source_target_pairs={{4,0},{8,4},{12,8},{16,12},{20,16},{24,20},{28,24},{5,1},{9,5},{13... | collective-permute-start | bytes 196616 | tf_op jit(solution)/shard_map/ppermute | solution.py:283
  38.3 35.0 %copy-start.6 = (s32[2]{0:T(128)S(1)}, s32[2]{0:T(128)}, u32[]{:S(2)}) copy-start(s32[2]{0:T(128)} %param.15) | copy-start | bytes 28
  38.3 8.6 %collective-permute-start.2 = (bf16[8,2,64,128]{3,2,1,0:T(8,128)(2,1)S(1)}, bf16[8,2,64,128]{3,2,1,0:T(8,128)(2,1)S(1)}, u32[]{:S(2)}, u32[]{:S(2)}) collective-permute-start(bf16[8,2,64,128]{3,2,1,0:T(8,128)(2,1)S(1)} %all-to-all-done.1.mine_ref), channel_id=1, source_target_pairs={{0,1},{1,0},{2,3},{3,2},{4,5},{5,4},{6,7},{7,6},{8,9},{9,8},{10,11... | collective-permute-start | bytes 786440 | tf_op jit(solution)/shard_map/ppermute | solution.py:316
  42.3 4.9 %copy-start.2 = (bf16[2,2,64,128]{3,2,1,0:T(8,128)(2,1)}, bf16[2,2,64,128]{3,2,1,0:T(8,128)(2,1)S(1)}, u32[]{:S(2)}) copy-start(bf16[2,2,64,128]{3,2,1,0:T(8,128)(2,1)S(1)} %pad_maximum_fusion.6.glob_mine_ref) | copy-start | bytes 196612
  42.3 4.9 %collective-permute-start.3 = (bf16[2,2,64,128]{3,2,1,0:T(8,128)(2,1)S(1)}, bf16[2,2,64,128]{3,2,1,0:T(8,128)(2,1)S(1)}, u32[]{:S(2)}, u32[]{:S(2)}) collective-permute-start(bf16[2,2,64,128]{3,2,1,0:T(8,128)(2,1)S(1)} %pad_maximum_fusion.6.glob_mine_ref), channel_id=1, source_target_pairs={{0,1},{1,0},{2,3},{3,2},{4,5},{5,4},{6,7},{7,6},{8,9},{9,8},{10,11... | collective-permute-start | bytes 196616 | tf_op jit(solution)/shard_map/ppermute | solution.py:305
  46.9 0.6 copy-start.3
  46.9 0.7 copy-start.4
  47.0 0.8 copy-start.1
  47.7 0.6 copy-start.5
  73.2 2.0 %collective-permute-start.6 = (bf16[12,2,64,128]{3,2,1,0:T(8,128)(2,1)}, bf16[12,2,64,128]{3,2,1,0:T(8,128)(2,1)S(1)}, u32[]{:S(2)}, u32[]{:S(2)}) collective-permute-start(bf16[12,2,64,128]{3,2,1,0:T(8,128)(2,1)} %get-tuple-element.40), channel_id=1, source_target_pairs={{0,1},{1,0},{2,3},{3,2},{4,5},{5,4},{6,7},{7,6},{8,9},{9,8},{10,11... | collective-permute-start | bytes 1179656 | tf_op jit(solution)/shard_map/ppermute | solution.py:389
  76.5 15.5 %collective-permute-start.7 = (bf16[12,2,32,128]{3,2,1,0:T(8,128)(2,1)S(1)}, bf16[12,2,32,128]{3,2,1,0:T(8,128)(2,1)S(1)}, u32[]{:S(2)}, u32[]{:S(2)}) collective-permute-start(bf16[12,2,32,128]{3,2,1,0:T(8,128)(2,1)S(1)} %dynamic-slice_convert_fusion.1), channel_id=1, source_target_pairs={{0,2},{1,3},{2,0},{3,1},{4,6},{5,7},{6,4},{7,5},{8,10},{9,11},{10,... | collective-permute-start | bytes 589832 | tf_op jit(solution)/shard_map/ppermute | solution.py:396
  77.8 30.8 %copy-start.7 = (s32[8]{0:T(128)S(1)}, s32[8]{0:T(128)}, u32[]{:S(2)}) copy-start(s32[8]{0:T(128)} %reduce.4.requested) | copy-start | bytes 100
  91.5 5.8 %collective-permute-start.4 = (bf16[16,2,64,128]{3,2,1,0:T(8,128)(2,1)}, bf16[16,2,64,128]{3,2,1,0:T(8,128)(2,1)S(1)}, u32[]{:S(2)}, u32[]{:S(2)}) collective-permute-start(bf16[16,2,64,128]{3,2,1,0:T(8,128)(2,1)} %get-tuple-element.38), channel_id=1, source_target_pairs={{0,1},{1,0},{2,3},{3,2},{4,5},{5,4},{6,7},{7,6},{8,9},{9,8},{10,11... | collective-permute-start | bytes 1572872 | tf_op jit(solution)/shard_map/ppermute | solution.py:389
  92.9 15.6 %all-to-all-start.3 = ((bf16[8,6,32,128]{3,2,1,0:T(8,128)(2,1)}), bf16[8,6,32,128]{3,2,1,0:T(8,128)(2,1)S(1)}, u32[]{:S(2)}, u32[]{:S(2)}) async-start(bf16[8,6,32,128]{3,2,1,0:T(8,128)(2,1)} %pad_maximum_fusion.2), calls=%async_computation.3 | async-start | bytes 786432 | tf_op jit(solution)/shard_map/all_to_all | solution.py:415
  98.7 10.2 %collective-permute-start.5 = (bf16[16,2,32,128]{3,2,1,0:T(8,128)(2,1)S(1)}, bf16[16,2,32,128]{3,2,1,0:T(8,128)(2,1)S(1)}, u32[]{:S(2)}, u32[]{:S(2)}) collective-permute-start(bf16[16,2,32,128]{3,2,1,0:T(8,128)(2,1)S(1)} %dynamic-slice_convert_fusion), channel_id=1, source_target_pairs={{0,2},{1,3},{2,0},{3,1},{4,6},{5,7},{6,4},{7,5},{8,10},{9,11},{10,... | collective-permute-start | bytes 786440 | tf_op jit(solution)/shard_map/ppermute | solution.py:396
  99.0 10.2 %collective-permute-start.9 = (bf16[2,32,128]{2,1,0:T(8,128)(2,1)S(1)}, bf16[2,32,128]{2,1,0:T(8,128)(2,1)S(1)}, u32[]{:S(2)}, u32[]{:S(2)}) collective-permute-start(bf16[2,32,128]{2,1,0:T(8,128)(2,1)S(1)} %get-tuple-element.57), channel_id=1, source_target_pairs={{0,4},{4,8},{8,12},{12,16},{16,20},{20,24},{24,28},{1,5},{5,9},{9,... | collective-permute-start | bytes 49160 | tf_op jit(solution)/shard_map/ppermute | solution.py:419
  102.1 7.1 %collective-permute-start.8 = (bf16[2,32,128]{2,1,0:T(8,128)(2,1)S(1)}, bf16[2,32,128]{2,1,0:T(8,128)(2,1)S(1)}, u32[]{:S(2)}, u32[]{:S(2)}) collective-permute-start(bf16[2,32,128]{2,1,0:T(8,128)(2,1)S(1)} %get-tuple-element.58), channel_id=1, source_target_pairs={{4,0},{8,4},{12,8},{16,12},{20,16},{24,20},{28,24},{5,1},{9,5},{13... | collective-permute-start | bytes 49160 | tf_op jit(solution)/shard_map/ppermute | solution.py:418
  109.3 6.7 %collective-permute-start.10 = (bf16[16,2,32,128]{3,2,1,0:T(8,128)(2,1)S(1)}, bf16[16,2,32,128]{3,2,1,0:T(8,128)(2,1)S(1)}, u32[]{:S(2)}, u32[]{:S(2)}) collective-permute-start(bf16[16,2,32,128]{3,2,1,0:T(8,128)(2,1)S(1)} %convert_element_type.39), channel_id=1, source_target_pairs={{0,2},{1,3},{2,0},{3,1},{4,6},{5,7},{6,4},{7,5},{8,10},{9,11},{10,... | collective-permute-start | bytes 786440 | tf_op jit(solution)/shard_map/ppermute | solution.py:436
  116.1 3.7 %collective-permute-start.11 = (bf16[16,2,64,128]{3,2,1,0:T(8,128)(2,1)S(1)}, bf16[16,2,64,128]{3,2,1,0:T(8,128)(2,1)S(1)}, u32[]{:S(2)}, u32[]{:S(2)}) collective-permute-start(bf16[16,2,64,128]{3,2,1,0:T(8,128)(2,1)S(1)} %pad_maximum_fusion.1), channel_id=1, source_target_pairs={{0,1},{1,0},{2,3},{3,2},{4,5},{5,4},{6,7},{7,6},{8,9},{9,8},{10,11... | collective-permute-start | bytes 1572872 | tf_op jit(solution)/shard_map/ppermute | solution.py:436

commit v2 on v0

v2 whole, which is shorter than its diff:
```python
import functools
import math

import jax
import jax.numpy as jnp
from jax import lax
from jax.experimental import pallas as pl
from jax.experimental.pallas import tpu as pltpu
from jax.sharding import PartitionSpec as P

DH = 128
BLOCK = 128
HALF = BLOCK // 2
R = 3
G = 2
WINDOW = 3
FAR = R + G
LISTED = WINDOW + FAR
MIB = 1024 * 1024
MASKED = -1e30
FACTOR = float(DH) ** -0.5
SCALE = FACTOR * math.log2(math.e)
FOLD = 8

NT = (((1,), (1,)), ((), ()))
NN = (((1,), (0,)), ((), ()))


def mm(a, b, dims):
    return lax.dot_general(a, b, dims, preferred_element_type=jnp.float32)


def stack_heads(ref, u):
    rows = ref[u * BLOCK : (u + 1) * BLOCK, :]
    return jnp.concatenate(
        [rows[:, h * DH : (h + 1) * DH] for h in range(rows.shape[1] // DH)], axis=0
    )


def fold(x):
    return jnp.sum(x.reshape(x.shape[0] // FOLD, FOLD, x.shape[1]), axis=0)


def panel(k, v, q, g):
    s = mm(k, q, NT)
    dp = mm(v, g, NT)
    top = jnp.max(s, axis=0, keepdims=True) * SCALE
    e = jnp.exp2(s * SCALE - top)
    return top, e, dp, fold(e), fold(e * dp)


def places():
    head_index = lax.axis_index("head")
    return lax.rem(head_index, 2), lax.div(head_index, 2)


def ask_kernel(global_blocks, random_ref, k_ref, v_ref, out_ref, low_ref, high_ref, rows, sems):
    tokens = k_ref.shape[0]
    blocks = tokens // BLOCK
    share = BLOCK // lax.axis_size("head")
    core, column = places()
    marks = 2 * G * share
    edges, copies = [], []

    def begin(group, src, dst):
        group.append(pltpu.make_async_copy(src, dst, sems.at[len(edges) + len(copies)]))
        group[-1].start()

    for which, ref in ((0, k_ref), (1, v_ref)):
        for j in range(G):
            start = lax.rem(global_blocks[j], blocks) * BLOCK + core * HALF + column * share
            start = pl.multiple_of(start, share)
            begin(copies, ref.at[pl.ds(start, share), :], rows.at[2 * j + which])
    odd = lax.rem(lax.axis_index("seq"), 2)
    for which, ref in ((0, k_ref), (1, v_ref)):
        for edge_ref, at in ((low_ref, (1 - odd) * (tokens - BLOCK)), (high_ref, odd * (tokens - BLOCK))):
            start = pl.multiple_of(at, BLOCK)
            begin(edges, ref.at[pl.ds(start, BLOCK), :], edge_ref.at[which])
    wanted = random_ref[...]

    def mark(j, carry):
        within = wanted - j * blocks
        mine = jnp.logical_and(within >= 0, within < blocks)
        top = jnp.max(jnp.where(mine, within, -1).astype(jnp.float32))
        out_ref[j, marks:, :] = jnp.full((16, DH), top, jnp.float32).astype(jnp.bfloat16)
        return carry

    peers = out_ref.shape[0]
    lax.fori_loop(0, peers, mark, 0, unroll=min(peers, 8))
    for copy in copies:
        copy.wait()
    for i in range(2 * G):
        out_ref[:, i * share : (i + 1) * share, :] = jnp.broadcast_to(
            rows[i][None], (peers, share, DH)
        )
    for copy in edges:
        copy.wait()


def serve_kernel(global_blocks, asked_ref, k_ref, v_ref, out_ref, glob_ref, requested_ref, sems):
    blocks = k_ref.shape[0] // BLOCK
    share = BLOCK // lax.axis_size("head")
    core, _ = places()
    marks = 2 * G * share
    peers = out_ref.shape[0]
    many = min(peers, 8)

    def copy(j, start, which, ref):
        return pltpu.make_async_copy(
            ref.at[pl.ds(start, HALF), :], out_ref.at[j, which], sems.at[j, which]
        )

    def begin(j, carry):
        wanted = jnp.max(asked_ref[j, marks:, :].astype(jnp.float32)).astype(jnp.int32)
        requested_ref[j] = wanted
        start = pl.multiple_of(jnp.clip(wanted, 0, blocks - 1) * BLOCK + core * HALF, HALF)
        copy(j, start, 0, k_ref).start()
        copy(j, start, 1, v_ref).start()
        return carry

    lax.fori_loop(0, peers, begin, 0, unroll=many)
    for j in range(G):
        owner = lax.div(global_blocks[j], blocks)
        for which in range(2):
            at = (2 * j + which) * share
            glob_ref[j, which] = asked_ref[owner, at : at + share, :]

    def end(j, carry):
        copy(j, 0, 0, k_ref).wait()
        copy(j, 0, 1, v_ref).wait()
        return carry

    lax.fori_loop(0, peers, end, 0, unroll=many)


def glob_kernel(*refs):
    *part_refs, out_ref = refs
    share = part_refs[0].shape[2]
    core, column = places()
    for m, ref in enumerate(part_refs):
        at = (core ^ (m & 1)) * HALF + (column ^ (m >> 1)) * share
        out_ref[:, :, pl.ds(pl.multiple_of(at, share), share), :] = ref[...]


def split_kernel(count, keep_ref, got_ref, out_ref, *send_refs):
    share = out_ref.shape[2]
    _, column = places()
    own = pl.ds(pl.multiple_of(column * share, share), share)
    out_ref[...] = keep_ref[:, :, own, :] + got_ref[:, :, own, :].astype(jnp.float32)
    for m in range(1, count):
        there = pl.ds(pl.multiple_of((column ^ m) * share, share), share)
        send_refs[m - 1][...] = (
            keep_ref[:, :, there, :] + got_ref[:, :, there, :].astype(jnp.float32)
        ).astype(jnp.bfloat16)


def terms_kernel(keep_ref, *refs):
    *got_refs, terms_ref = refs
    peers, _, share, _ = terms_ref.shape
    me = lax.axis_index("seq")

    def total(slot, n=1):
        x = keep_ref[slot : slot + n]
        for ref in got_refs:
            x = x + ref[slot : slot + n].astype(jnp.float32)
        return x.astype(jnp.bfloat16)

    terms_ref[:, :2] = total(0, peers)
    glob = total(peers, G).reshape(1, 2 * G, share, DH)
    terms_ref[:, 2 : 2 + 2 * G] = jnp.broadcast_to(glob, (peers, 2 * G, share, DH))
    to_last = total(peers + G)[0]
    to_first = total(peers + G + 1)[0]

    def halo(j, carry):
        terms_ref[j, 2 + 2 * G :] = jnp.where(j > me, to_first, to_last)
        return carry

    lax.fori_loop(0, peers, halo, 0, unroll=min(peers, 8))


def settle_kernel(requested, global_blocks, back_ref, keep_ref, *refs):
    *got_refs, out_ref, acc = refs
    blocks = keep_ref.shape[0]
    peers, _, share, _ = back_ref.shape
    seq_index = lax.axis_index("seq")
    x = keep_ref[...]
    for ref in got_refs:
        x = x + ref[...].astype(jnp.float32)
    acc[...] = x
    halo = slice(2 + 2 * G, 4 + 2 * G)

    @pl.when(seq_index > 0)
    def _():
        acc[0] += back_ref[jnp.maximum(seq_index - 1, 0), halo].astype(jnp.float32)

    @pl.when(seq_index < peers - 1)
    def _():
        acc[blocks - 1] += back_ref[jnp.minimum(seq_index + 1, peers - 1), halo].astype(jnp.float32)

    def one(j, carry):
        wanted = requested[j]

        @pl.when(wanted >= 0)
        def _():
            acc[wanted] += back_ref[j, :2].astype(jnp.float32)

        return carry

    lax.fori_loop(0, peers, one, 0)
    for j in range(G):

        @pl.when(lax.div(global_blocks[j], blocks) == seq_index)
        def _():
            rows = back_ref[:, 2 + 2 * j : 4 + 2 * j].astype(jnp.float32)
            acc[lax.rem(global_blocks[j], blocks)] += jnp.sum(rows, axis=0)

    out_ref[...] = acc[...].astype(jnp.bfloat16)


def join_kernel(count, *refs):
    *got_refs, dk_ref, dv_ref, dk, dv = refs
    blocks, _, share, _ = got_refs[0].shape
    core, column = places()
    for m in range(count):
        for c in range(2):
            at = (core ^ c) * HALF + (column ^ m) * share
            rows = pl.ds(pl.multiple_of(at, share), share)
            ref = got_refs[2 * m + c]
            dk[:, rows, :] = ref[:, 0]
            dv[:, rows, :] = ref[:, 1]
    dk_ref[...] = dk[...].reshape(dk_ref.shape)
    dv_ref[...] = dv[...].reshape(dv_ref.shape)


def edge_places(blocks):
    odd = lax.rem(lax.axis_index("seq"), 2)
    return (1 - odd) * (blocks + 1), odd * (blocks + 1)


def fill_window(k_ref, v_ref, low_ref, high_ref, k_all, v_all):
    rows = k_ref.shape[0]
    low, high = (pl.ds(pl.multiple_of(i * BLOCK, BLOCK), BLOCK) for i in edge_places(rows // BLOCK))
    for to, own, which in ((k_all, k_ref, 0), (v_all, v_ref, 1)):
        to[low, :] = low_ref[which]
        to[high, :] = high_ref[which]
        to[BLOCK : BLOCK + rows] = own[...]


def near_kernel(q_ref, g_ref, k_ref, v_ref, low_ref, high_ref, st_ref, k_all, v_all):
    step = pl.program_id(0)
    blocks = k_ref.shape[0] // BLOCK
    seq_index = lax.axis_index("seq")
    per = st_ref.shape[0]

    @pl.when(step == 0)
    def _():
        fill_window(k_ref, v_ref, low_ref, high_ref, k_all, v_all)

    for u in range(per):
        b = step * per + u
        q = stack_heads(q_ref, u)
        g = stack_heads(g_ref, u)
        no_left = jnp.logical_and(seq_index == 0, b == 0)
        no_right = jnp.logical_and(seq_index == lax.axis_size("seq") - 1, b == blocks - 1)
        biases = (jnp.where(no_left, MASKED, 0.0), None, jnp.where(no_right, MASKED, 0.0))
        for w in range(WINDOW):
            rows = pl.ds(pl.multiple_of((b + w) * BLOCK, BLOCK), BLOCK)
            top, _, _, l, d = panel(k_all[rows, :], v_all[rows, :], q, g)
            if biases[w] is not None:
                top = top + biases[w]
            st_ref[u, w : w + 1] = top
            st_ref[u, WINDOW + w : WINDOW + w + 1] = jnp.sum(l, axis=0, keepdims=True)
            st_ref[u, 2 * WINDOW + w : 2 * WINDOW + w + 1] = jnp.sum(d, axis=0, keepdims=True)


def far_kernel(
    random_blocks, q_ref, g_ref, mine_ref, other_ref, glob_ref, st_ref, low_ref, high_ref,
    ds_ref, fd_ref, keep_ref, send_ref, k_all, v_all, acc,
):
    step = pl.program_id(0)
    peers = mine_ref.shape[0]
    per = ds_ref.shape[0]
    blocks = per * pl.num_programs(0)
    core = lax.rem(lax.axis_index("head"), 2)
    own, opp = pl.ds(core * HALF, HALF), pl.ds((1 - core) * HALF, HALF)

    @pl.when(step == 0)
    def _():
        for to, which in ((k_all, 0), (v_all, 1)):
            to[:peers, own, :] = mine_ref[:, which]
            to[:peers, opp, :] = other_ref[:, which]
            to[peers:] = glob_ref[:, which]
        acc[...] = jnp.zeros_like(acc)

    for u in range(per):
        b = step * per + u
        q = stack_heads(q_ref, u)
        g = stack_heads(g_ref, u)
        slots = [lax.div(random_blocks[b, r], blocks) for r in range(R)] + [peers + j for j in range(G)]
        parts = [panel(k_all[i], v_all[i], q, g) for i in slots]
        near = [[st_ref[u, i * WINDOW + w : i * WINDOW + w + 1] for w in range(WINDOW)] for i in range(3)]
        top = functools.reduce(jnp.maximum, near[0] + [x[0] for x in parts])
        near_weight = [jnp.exp2(t - top) for t in near[0]]
        weight = [jnp.exp2(x[0] - top) for x in parts]
        l = jnp.sum(sum(w * x[3] for w, x in zip(weight, parts)), axis=0, keepdims=True)
        d = jnp.sum(sum(w * x[4] for w, x in zip(weight, parts)), axis=0, keepdims=True)
        l = l + sum(w * x for w, x in zip(near_weight, near[1]))
        d = d + sum(w * x for w, x in zip(near_weight, near[2]))
        inv = 1.0 / l
        delta = d * inv
        for w in range(WINDOW):
            fd_ref[u, w : w + 1] = near[0][w]
            fd_ref[u, WINDOW + w : WINDOW + w + 1] = near_weight[w] * inv
        fd_ref[u, 2 * WINDOW : 2 * WINDOW + 1] = delta
        for i in range(FAR):
            _, e, dp, _, _ = parts[i]
            p = e * (weight[i] * inv)
            ds = (p * (dp - delta)).astype(jnp.bfloat16)
            ds_ref[u, i * BLOCK : (i + 1) * BLOCK] = ds
            acc[slots[i], 0] += mm(ds, q, NN)
            acc[slots[i], 1] += mm(p.astype(jnp.bfloat16), g, NN)

        def halo(slot, w, swap):
            odd = lax.rem(lax.axis_index("seq"), 2) == swap
            s = mm(jnp.where(odd, low_ref[0], high_ref[0]), q, NT)
            dp = mm(jnp.where(odd, low_ref[1], high_ref[1]), g, NT)
            p = jnp.exp2(s * SCALE - jnp.max(s, axis=0, keepdims=True) * SCALE) * (near_weight[w] * inv)
            ds = (p * (dp - delta)).astype(jnp.bfloat16)
            acc[slot, 0] = mm(ds, q, NN)
            acc[slot, 1] = mm(p.astype(jnp.bfloat16), g, NN)

        if u == 0:
            pl.when(step == 0)(functools.partial(halo, peers + G, 0, 1))
        if u == per - 1:
            pl.when(step == pl.num_programs(0) - 1)(
                functools.partial(halo, peers + G + 1, WINDOW - 1, 0)
            )

    @pl.when(step == pl.num_programs(0) - 1)
    def _():
        for which, f in ((0, FACTOR), (1, 1.0)):
            keep_ref[:, which] = acc[:, which, own, :] * f
            send_ref[:, which] = (acc[:, which, opp, :] * f).astype(jnp.bfloat16)


def window_kernel(
    q_ref, g_ref, k_ref, v_ref, low_ref, high_ref, fd_ref, ds_ref, keep_ref, send_ref, k_all, v_all, acc
):
    step = pl.program_id(0)
    per = ds_ref.shape[0]
    core = lax.rem(lax.axis_index("head"), 2)
    own, opp = pl.ds(core * HALF, HALF), pl.ds((1 - core) * HALF, HALF)

    @pl.when(step == 0)
    def _():
        fill_window(k_ref, v_ref, low_ref, high_ref, k_all, v_all)
        acc[...] = jnp.zeros_like(acc)

    for u in range(per):
        b = step * per + u
        q = stack_heads(q_ref, u)
        g = stack_heads(g_ref, u)
        delta = fd_ref[u, 2 * WINDOW : 2 * WINDOW + 1]
        ds, pb = [], []
        for w in range(WINDOW):
            rows = pl.ds(pl.multiple_of((b + w) * BLOCK, BLOCK), BLOCK)
            s = mm(k_all[rows, :], q, NT)
            dp = mm(v_all[rows, :], g, NT)
            top = fd_ref[u, w : w + 1]
            top = jnp.where(top < MASKED / 2, 0.0, top)
            p = jnp.exp2(s * SCALE - top) * fd_ref[u, WINDOW + w : WINDOW + w + 1]
            ds.append((p * (dp - delta)).astype(jnp.bfloat16))
            ds_ref[u, w * BLOCK : (w + 1) * BLOCK] = ds[w]
            pb.append(p.astype(jnp.bfloat16))
        shape = (WINDOW, BLOCK, DH)
        acc[pl.ds(b, WINDOW), 0] += mm(jnp.concatenate(ds, axis=0), q, NN).reshape(shape)
        acc[pl.ds(b, WINDOW), 1] += mm(jnp.concatenate(pb, axis=0), g, NN).reshape(shape)

    @pl.when(step == pl.num_programs(0) - 1)
    def _():
        for which, f in ((0, FACTOR), (1, 1.0)):
            keep_ref[:, which] = acc[1:-1, which, own, :] * f
            send_ref[:, which] = (acc[1:-1, which, opp, :] * f).astype(jnp.bfloat16)


def queries_kernel(
    random_blocks, k_ref, low_ref, high_ref, mine_ref, other_ref, glob_ref,
    dsw_ref, dsf_ref, dq_ref, kt_all,
):
    blocks = k_ref.shape[0] // BLOCK
    peers = mine_ref.shape[0]
    per = dsw_ref.shape[0]
    core = lax.rem(lax.axis_index("head"), 2)
    step = pl.program_id(0)
    first_random = blocks + 2
    first_global = first_random + peers

    @pl.when(step == 0)
    def _():
        at_low, at_high = edge_places(blocks)
        kt_all[at_low] = low_ref[0].T
        kt_all[at_high] = high_ref[0].T

        def own(j, carry):
            kt_all[j + 1] = k_ref[pl.ds(pl.multiple_of(j * BLOCK, BLOCK), BLOCK), :].T
            return carry

        lax.fori_loop(0, blocks, own, 0)

        def joined(a, b):
            low = jnp.where(core == 0, a, b)
            high = jnp.where(core == 0, b, a)
            return jnp.concatenate([low, high], axis=0).T

        def fetched(j, carry):
            kt_all[first_random + j] = joined(mine_ref[j, 0], other_ref[j, 0])
            return carry

        lax.fori_loop(0, peers, fetched, 0)
        for j in range(G):
            kt_all[first_global + j] = glob_ref[j, 0].T

    for u in range(per):
        b = step * per + u
        near = [kt_all[b + w] for w in range(WINDOW)]
        far = [kt_all[first_random + lax.div(random_blocks[b, r], blocks)] for r in range(R)]
        far += [kt_all[first_global + j] for j in range(G)]
        dqt = mm(jnp.concatenate(near, axis=1), dsw_ref[u], NN)
        dqt = (dqt + mm(jnp.concatenate(far, axis=1), dsf_ref[u], NN)) * FACTOR
        for h in range(dq_ref.shape[1] // DH):
            dq_ref[u * BLOCK : (u + 1) * BLOCK, h * DH : (h + 1) * DH] = (
                dqt[:, h * BLOCK : (h + 1) * BLOCK].T.astype(jnp.bfloat16)
            )


def whole(a):
    return pl.BlockSpec(a.shape, lambda i, *_: (0,) * len(a.shape))


def per_block(per, *rest):
    return pl.BlockSpec((per,) + rest, lambda i, *_: (i,) + (0,) * len(rest))


def partners(size, stride):
    return [(i, i ^ stride) for i in range(size)]


def body(query_vectors, key_vectors, value_vectors, output_grad, random_blocks, global_blocks):
    seq_count = lax.axis_size("seq")
    head_count = lax.axis_size("head")
    rows_dev, columns = query_vectors.shape
    blocks = rows_dev // BLOCK
    per = math.gcd(blocks, 4)
    steps = blocks // per
    lanes = columns // DH * BLOCK
    bf16 = jnp.bfloat16
    f32 = jnp.float32
    sds = jax.ShapeDtypeStruct
    core_pairs = partners(head_count, 1)
    limit = (16 + seq_count // 2) * MIB
    params = pltpu.CompilerParams(dimension_semantics=("arbitrary",), vmem_limit_bytes=limit)
    unit = 2 * blocks * lanes * BLOCK * DH

    vmem = pl.BlockSpec(memory_space=pltpu.VMEM)
    smem = pl.BlockSpec(memory_space=pltpu.SMEM)
    hbm = pl.BlockSpec(memory_space=pltpu.HBM)
    small = pltpu.CompilerParams(vmem_limit_bytes=limit)
    large = pltpu.CompilerParams(vmem_limit_bytes=60 * MIB)
    share = BLOCK // head_count
    columns_count = head_count // 2

    edge = (2, BLOCK, DH)
    asking, to_low, to_high = pl.pallas_call(
        ask_kernel,
        out_shape=(
            sds((seq_count, 2 * G * share + 16, DH), bf16),
            sds(edge, bf16),
            sds(edge, bf16),
        ),
        in_specs=[smem, vmem, hbm, hbm],
        out_specs=(vmem, vmem, vmem),
        scratch_shapes=[
            pltpu.VMEM((2 * G, share, DH), bf16),
            pltpu.SemaphoreType.DMA((2 * G + 4,)),
        ],
        compiler_params=large,
        name="ask",
    )(global_blocks, random_blocks.T, key_vectors, value_vectors)
    asked = lax.all_to_all(asking, "seq", split_axis=0, concat_axis=0, tiled=True)

    low_pairs = [(i, i ^ 1) for i in range(seq_count)]
    high_pairs = [(i, i + 1 if i % 2 else i - 1) for i in range(1, seq_count - 1)]
    low = lax.ppermute(to_low, "seq", low_pairs)
    high = lax.ppermute(to_high, "seq", high_pairs)
    asked, low, high = lax.optimization_barrier((asked, low, high))

    served, glob_part, requested = pl.pallas_call(
        serve_kernel,
        out_shape=(
            sds((seq_count, 2, HALF, DH), bf16),
            sds((G, 2, share, DH), bf16),
            sds((seq_count,), jnp.int32),
        ),
        in_specs=[smem, vmem, hbm, hbm],
        out_specs=(vmem, vmem, smem),
        scratch_shapes=[pltpu.SemaphoreType.DMA((seq_count, 2))],
        compiler_params=large,
        name="serve",
    )(global_blocks, asked, key_vectors, value_vectors)
    mine = lax.all_to_all(served, "seq", split_axis=0, concat_axis=0, tiled=True)
    glob_parts = [glob_part] + [
        lax.ppermute(glob_part, "head", partners(head_count, m)) for m in range(1, head_count)
    ]
    glob = pl.pallas_call(
        glob_kernel,
        out_shape=sds((G, 2, BLOCK, DH), bf16),
        in_specs=[vmem] * head_count,
        out_specs=vmem,
        compiler_params=large,
        name="glob",
    )(*glob_parts)

    rows_spec = pl.BlockSpec((per * BLOCK, columns), lambda i, *_: (i, 0))
    near_spec = per_block(per, WINDOW * BLOCK, lanes)
    far_spec = per_block(per, FAR * BLOCK, lanes)
    st_spec = per_block(per, 2 * FOLD, lanes)
    fd_spec = per_block(per, FOLD, lanes)
    near_shape = sds((blocks, WINDOW * BLOCK, lanes), bf16)
    far_shape = sds((blocks, FAR * BLOCK, lanes), bf16)

    nearby = (key_vectors, value_vectors, low, high)
    window_scratch = [pltpu.VMEM(((blocks + 2) * BLOCK, DH), bf16)] * 2
    st = pl.pallas_call(
        near_kernel,
        out_shape=sds((blocks, 2 * FOLD, lanes), f32),
        grid=(steps,),
        in_specs=[rows_spec, rows_spec] + [whole(a) for a in nearby],
        out_specs=st_spec,
        scratch_shapes=window_scratch,
        compiler_params=large,
        cost_estimate=pl.CostEstimate(
            flops=2 * WINDOW * unit, bytes_accessed=4 * MIB, transcendentals=blocks * lanes * WINDOW * BLOCK
        ),
        name="near",
    )(query_vectors, output_grad, *nearby)
    mine, st, glob = lax.optimization_barrier((mine, st, glob))
    other = lax.ppermute(mine, "head", core_pairs)
    fetched = (mine, other, glob)
    slots = seq_count + G + 2
    piece = (slots, 2, HALF, DH)
    dsf, fd, keep, send = pl.pallas_call(
        far_kernel,
        out_shape=(far_shape, sds((blocks, FOLD, lanes), f32), sds(piece, f32), sds(piece, bf16)),
        grid_spec=pltpu.PrefetchScalarGridSpec(
            num_scalar_prefetch=1,
            grid=(steps,),
            in_specs=[rows_spec, rows_spec] + [whole(a) for a in fetched] + [st_spec, whole(low), whole(high)],
            out_specs=(far_spec, fd_spec, whole(sds(piece, f32)), whole(sds(piece, bf16))),
            scratch_shapes=[pltpu.VMEM((seq_count + G, BLOCK, DH), bf16)] * 2
            + [pltpu.VMEM((slots, 2, BLOCK, DH), f32)],
        ),
        compiler_params=params,
        cost_estimate=pl.CostEstimate(
            flops=4 * FAR * unit, bytes_accessed=8 * MIB, transcendentals=blocks * lanes * FAR * BLOCK
        ),
        name="far",
    )(random_blocks, query_vectors, output_grad, *fetched, st, low, high)

    piece_w = (blocks, 2, HALF, DH)
    dsw, keep_w, send_w = pl.pallas_call(
        window_kernel,
        out_shape=(near_shape, sds(piece_w, f32), sds(piece_w, bf16)),
        grid=(steps,),
        in_specs=[rows_spec, rows_spec] + [whole(a) for a in nearby] + [fd_spec],
        out_specs=(near_spec, whole(sds(piece_w, f32)), whole(sds(piece_w, bf16))),
        scratch_shapes=window_scratch + [pltpu.VMEM((blocks + 2, 2, BLOCK, DH), f32)],
        compiler_params=params,
        cost_estimate=pl.CostEstimate(flops=2 * WINDOW * unit, bytes_accessed=8 * MIB, transcendentals=0),
        name="window",
    )(query_vectors, output_grad, *nearby, fd)

    query_grad = pl.pallas_call(
        queries_kernel,
        out_shape=sds(query_vectors.shape, bf16),
        grid_spec=pltpu.PrefetchScalarGridSpec(
            num_scalar_prefetch=1,
            grid=(steps,),
            in_specs=[whole(a) for a in (key_vectors, low, high) + fetched] + [near_spec, far_spec],
            out_specs=rows_spec,
            scratch_shapes=[pltpu.VMEM((blocks + 2 + slots, BLOCK, DH), bf16)],
        ),
        compiler_params=params,
        cost_estimate=pl.CostEstimate(flops=LISTED * unit, bytes_accessed=8 * MIB, transcendentals=0),
        name="queries",
    )(random_blocks, key_vectors, low, high, *fetched, dsw, dsf)

    others = [m << 1 for m in range(1, columns_count)]

    def reduced(kept, sent, name):
        got = lax.ppermute(sent, "head", core_pairs)
        part = (kept.shape[0], 2, share, DH)
        home, *away = pl.pallas_call(
            functools.partial(split_kernel, columns_count),
            out_shape=(sds(part, f32),) + (sds(part, bf16),) * len(others),
            in_specs=[vmem, vmem],
            out_specs=(vmem,) * (1 + len(others)),
            compiler_params=small,
            name=name,
        )(kept, got)
        return [home] + [
            lax.ppermute(a, "head", partners(head_count, m)) for a, m in zip(away, others)
        ]

    parts = reduced(keep, send, "split_far")
    parts[-1], send_w = lax.optimization_barrier((parts[-1], send_w))
    parts_w = reduced(keep_w, send_w, "split_window")
    terms = pl.pallas_call(
        terms_kernel,
        out_shape=sds((seq_count, 4 + 2 * G, share, DH), bf16),
        in_specs=[vmem] * len(parts),
        out_specs=vmem,
        compiler_params=small,
        name="terms",
    )(*parts)
    back = lax.all_to_all(terms, "seq", split_axis=0, concat_axis=0, tiled=True)
    back, query_grad = lax.optimization_barrier((back, query_grad))
    held = pl.pallas_call(
        settle_kernel,
        out_shape=sds((blocks, 2, share, DH), bf16),
        in_specs=[smem, smem] + [vmem] * (1 + len(parts_w)),
        out_specs=vmem,
        scratch_shapes=[pltpu.VMEM((blocks, 2, share, DH), f32)],
        compiler_params=small,
        name="settle",
    )(requested, global_blocks, back, *parts_w)

    rows = [held] + [lax.ppermute(held, "head", partners(head_count, m)) for m in others]
    pieces = []
    for a in rows:
        pieces += [a, lax.ppermute(a, "head", core_pairs)]
    key_grad, value_grad = pl.pallas_call(
        functools.partial(join_kernel, columns_count),
        out_shape=(sds(key_vectors.shape, bf16),) * 2,
        in_specs=[vmem] * len(pieces),
        out_specs=(vmem, vmem),
        scratch_shapes=[pltpu.VMEM((blocks, BLOCK, DH), bf16)] * 2,
        compiler_params=small,
        name="join",
    )(*pieces)
    return query_grad, key_grad, value_grad


def solution(mesh):
    return jax.shard_map(
        body,
        mesh=mesh,
        in_specs=(
            P("seq", "head"),
            P("seq", None),
            P("seq", None),
            P("seq", "head"),
            P("seq", None),
            P(),
        ),
        out_specs=(P("seq", "head"), P("seq", None), P("seq", None)),
        check_vma=False,
    )
```

time: 397 us -> 104 us (0.26)
  waiting for transfers between devices: 153 us -> 13.9 us
  local copies, waits for them, and re-layouts: 108 us -> 17 us
  matrix products: 40.7 us -> 0 us
  Pallas kernels: 0 us -> 38.8 us
  other arithmetic: 32.2 us -> 0 us
  between operations: 19.1 us -> 0.82 us
  blocking collectives: 10.1 us -> 0 us
  starting transfers between devices: 27.3 us -> 31.8 us
    psum x3 -> x0, waiting for transfers between devices: 153 us -> none  [the longest x1 59.3 us: from_root(): return lax.psum(kept, axis)]
    dot_general x30 -> x0, matrix products: 40.7 us -> none  [the longest x4 17.1 us: advance(): jnp.einsum('brn,brxc->nxc', onehot, gradients[:, 3:3 + R], precision=lax....]
    pallas_call x0 -> x12, Pallas kernels: none -> 38.8 us  [the longest x1 12.7 us: body(): pl.pallas_call(far_kernel, out_shape=(far_shape, sds((blocks, FOLD, lanes...]
    while x84 -> x0, local copies, waits for them, and re-layouts: 38.4 us -> none
    slice x12 -> x0, local copies, waits for them, and re-layouts: 35.7 us -> none  [the longest x4 28.2 us: advance(): spread = spread.at[2:group_size + 2].add(gradients[:, 2])]
    unnamed x16 -> x55, local copies, waits for them, and re-layouts: 2.01 us -> 17 us
    ppermute x4 -> x13, waiting for transfers between devices: 0.01 us -> 13.9 us  [the longest x1 5.05 us: body(): lax.ppermute(held, 'head', partners(head_count, m))]
    reduce_sum x4 -> x0, other arithmetic: 11.8 us -> none  [advance(): global_acc = global_acc + jnp.sum(gradients[:, 3 + R:], axis=0)]
  transfers between devices with their start and end apart: 10 -> 16, of which waited for: 3 -> 6; matrix products, arithmetic and copies ran while one was open for 7% -> 0% of each run, Pallas kernels for 0% -> 17%
where the time goes in v2:
time: 104 us; the launch traced here: 102 us
  Pallas kernels  38.8 us (37%)
  starting transfers between devices  31.8 us (31%)
  local copies, waits for them, and re-layouts  17 us (16%)
  waiting for transfers between devices  13.9 us (13%)
    unnamed x55, local copies, waits for them, and re-layouts  17 us
    pallas_call x1, Pallas kernels, body(): pl.pallas_call(far_kernel, out_shape=(far_shape, sds((blocks, FOLD, lanes...  12.7 us
    all_to_all x1, starting transfers between devices, body(): lax.all_to_all(served, 'seq', split_axis=0, concat_axis=0, tiled=True)  6 us
    all_to_all x1, starting transfers between devices, body(): lax.all_to_all(asking, 'seq', split_axis=0, concat_axis=0, tiled=True)  5.79 us
    pallas_call x1, Pallas kernels, body(): pl.pallas_call(queries_kernel, out_shape=sds(query_vectors.shape, bf16),...  5.68 us
    all_to_all x1, starting transfers between devices, body(): back = lax.all_to_all(terms, 'seq', split_axis=0, concat_axis=0, tiled=True)  5.43 us
    pallas_call x1, Pallas kernels, body(): pl.pallas_call(near_kernel, out_shape=sds((blocks, 2 * FOLD, lanes), f32)...  5.36 us
    pallas_call x1, Pallas kernels, body(): pl.pallas_call(window_kernel, out_shape=(near_shape, sds(piece_w, f32), s...  5.21 us
  transfers between devices with their start and end apart: 16, of which 6 were waited for; matrix products, arithmetic and copies ran while one was open for 0% of the time, Pallas kernels for 17%

profile of v2, /device:TPU:5, one launch (start us, length us, event | category | flops | bytes accessed | tf_op | source)
XLA Modules:
  0.0 102.3 jit_solution(7011150527428745144)
XLA Ops:
  0.7 2.5 %ask.1 = (bf16[8,144,128]{2,1,0:T(8,128)(2,1)}, bf16[2,128,128]{2,1,0:T(8,128)(2,1)}, bf16[2,128,128]{2,1,0:T(8,128)(2,1)}) custom-call(s32[2]{0:T(128)} %global_blocks.5, s32[3,16]{1,0:T(4,128)} %bitcast.1, bf16[2048,128]{1,0:T(8,128)(2,1)} %k_ref.9, bf16[2048,128]{1,0:T(8,128)(2,1)} %v_ref.7), custom_call_target="tpu_custom_call" | custom-call | tf_op jit(solution)/shard_map/ask/pallas_call | solution.py:473
  3.2 5.8 %all-to-all-start = ((bf16[8,144,128]{2,1,0:T(8,128)(2,1)}), bf16[8,144,128]{2,1,0:T(8,128)(2,1)S(1)}, u32[]{:S(2)}, u32[]{:S(2)}) async-start(bf16[8,144,128]{2,1,0:T(8,128)(2,1)} %get-tuple-element.32), calls=%async_computation | async-start | bytes 589824 | tf_op jit(solution)/shard_map/all_to_all | solution.py:489
  9.0 4.2 %collective-permute-start.1 = (bf16[2,128,128]{2,1,0:T(8,128)(2,1)}, bf16[2,128,128]{2,1,0:T(8,128)(2,1)S(1)}, u32[]{:S(2)}, u32[]{:S(2)}) collective-permute-start(bf16[2,128,128]{2,1,0:T(8,128)(2,1)} %get-tuple-element.34), channel_id=1, source_target_pairs={{4,8},{8,4},{12,16},{16,12},{20,24},{24,20},{5,9},{9,5},{13,17},{1... | collective-permute-start | bytes 196616 | tf_op jit(solution)/shard_map/ppermute | solution.py:494
  13.3 3.2 %collective-permute-done.1.high_ref = bf16[2,128,128]{2,1,0:T(8,128)(2,1)S(1)} collective-permute-done((bf16[2,128,128]{2,1,0:T(8,128)(2,1)}, bf16[2,128,128]{2,1,0:T(8,128)(2,1)S(1)}, u32[]{:S(2)}, u32[]{:S(2)}) %collective-permute-start.1) | collective-permute-done | bytes 65568 | tf_op jit(solution)/shard_map/ppermute | solution.py:494
  17.3 2.9 %serve.1 = (bf16[8,2,64,128]{3,2,1,0:T(8,128)(2,1)}, bf16[2,2,32,128]{3,2,1,0:T(8,128)(2,1)}, s32[8]{0:T(128)}) custom-call(s32[2]{0:T(128)} %global_blocks.5, bf16[8,144,128]{2,1,0:T(8,128)(2,1)} %copy-done.22, bf16[2048,128]{1,0:T(8,128)(2,1)} %k_ref.9, bf16[2048,128]{1,0:T(8,128)(2,1)} %v_ref.7), custom_call_target="tpu_custom_call" | custom-call | tf_op jit(solution)/shard_map/serve/pallas_call | solution.py:497
  20.1 6.0 %all-to-all-start.1 = ((bf16[8,2,64,128]{3,2,1,0:T(8,128)(2,1)}), bf16[8,2,64,128]{3,2,1,0:T(8,128)(2,1)S(1)}, u32[]{:S(2)}, u32[]{:S(2)}) async-start(bf16[8,2,64,128]{3,2,1,0:T(8,128)(2,1)} %get-tuple-element.36), calls=%async_computation.1 | async-start | bytes 524288 | tf_op jit(solution)/shard_map/all_to_all | solution.py:510
  26.1 1.8 %collective-permute-start.2 = (bf16[2,2,32,128]{3,2,1,0:T(8,128)(2,1)}, bf16[2,2,32,128]{3,2,1,0:T(8,128)(2,1)S(1)}, u32[]{:S(2)}, u32[]{:S(2)}) collective-permute-start(bf16[2,2,32,128]{3,2,1,0:T(8,128)(2,1)} %get-tuple-element.39.refs_0_), channel_id=1, source_target_pairs={{0,1},{1,0},{2,3},{3,2},{4,5},{5,4},{6,7},{7,6},{8,9},{9,8},{10,11... | collective-permute-start | bytes 98312 | tf_op jit(solution)/shard_map/ppermute | solution.py:512
  29.6 5.4 %near.1.st_ref = f32[16,16,256]{2,1,0:T(8,128)} custom-call(bf16[2048,256]{1,0:T(8,128)(2,1)} %q_ref.5, bf16[2048,256]{1,0:T(8,128)(2,1)} %g_ref.5, bf16[2048,128]{1,0:T(8,128)(2,1)} %k_ref.9, bf16[2048,128]{1,0:T(8,128)(2,1)} %v_ref.7, bf16[2,128,128]{2,1,0:T(8,128)(2,1)} %copy-done.10, bf16[2,128,128]{2,1,0:T(8,128)(2,1)} %copy-done.13), custom_call_target="tpu_custom_call" | custom-call | flops 805306368 | bytes 4194304 | tf_op jit(solution)/shard_map/near/pallas_call | solution.py:533
  36.2 1.5 %glob.1.glob_ref = bf16[2,2,128,128]{3,2,1,0:T(8,128)(2,1)} custom-call(bf16[2,2,32,128]{3,2,1,0:T(8,128)(2,1)} %get-tuple-element.39.refs_0_, bf16[2,2,32,128]{3,2,1,0:T(8,128)(2,1)} %copy-done.23, bf16[2,2,32,128]{3,2,1,0:T(8,128)(2,1)} %copy-done.24, bf16[2,2,32,128]{3,2,1,0:T(8,128)(2,1)} %copy-done.25), custom_call_target="tpu_custom_call" | custom-call | tf_op jit(solution)/shard_map/glob/pallas_call | solution.py:514
  42.8 12.7 %far.1 = (bf16[16,640,256]{2,1,0:T(8,128)(2,1)S(1)}, f32[16,8,256]{2,1,0:T(8,128)S(1)}, f32[12,2,64,128]{3,2,1,0:T(8,128)S(1)}, bf16[12,2,64,128]{3,2,1,0:T(8,128)(2,1)S(1)}) custom-call(s32[16,3]{1,0:T(8,128)S(1)} %copy.9.random_blocks, bf16[2048,256]{1,0:T(8,128)(2,1)S(1)} %copy-done.4, bf16[2048,256]{1,0:T(8,128)(2,1)S(1)} %copy-done.5, ...), custom_call_target="tpu_custom_call" | custom-call | flops 2684354560 | bytes 8388608 | tf_op jit(solution)/shard_map/far/pallas_call | solution.py:551
  55.5 2.3 %copy-done.2 = bf16[16,640,256]{2,1,0:T(8,128)(2,1)} copy-done((bf16[16,640,256]{2,1,0:T(8,128)(2,1)}, bf16[16,640,256]{2,1,0:T(8,128)(2,1)S(1)}, u32[]{:S(2)}) %copy-start.2) | copy-done | bytes 5242904
  58.0 1.5 %collective-permute-done.6.got_ref = bf16[12,2,64,128]{3,2,1,0:T(8,128)(2,1)S(1)} collective-permute-done((bf16[12,2,64,128]{3,2,1,0:T(8,128)(2,1)S(1)}, bf16[12,2,64,128]{3,2,1,0:T(8,128)(2,1)S(1)}, u32[]{:S(2)}, u32[]{:S(2)}) %collective-permute-start.6) | collective-permute-done | bytes 393248 | tf_op jit(solution)/shard_map/ppermute | solution.py:600
  59.6 1.3 %collective-permute-start.7 = (bf16[12,2,32,128]{3,2,1,0:T(8,128)(2,1)S(1)}, bf16[12,2,32,128]{3,2,1,0:T(8,128)(2,1)S(1)}, u32[]{:S(2)}, u32[]{:S(2)}) collective-permute-start(bf16[12,2,32,128]{3,2,1,0:T(8,128)(2,1)S(1)} %get-tuple-element.46), channel_id=1, source_target_pairs={{0,2},{1,3},{2,0},{3,1},{4,6},{5,7},{6,4},{7,5},{8,10},{9,11},{10,... | collective-permute-start | bytes 589832 | tf_op jit(solution)/shard_map/ppermute | solution.py:611
  60.9 5.2 %window.1 = (bf16[16,384,256]{2,1,0:T(8,128)(2,1)S(1)}, f32[16,2,64,128]{3,2,1,0:T(8,128)S(1)}, bf16[16,2,64,128]{3,2,1,0:T(8,128)(2,1)S(1)}) custom-call(bf16[2048,256]{1,0:T(8,128)(2,1)S(1)} %copy-done.4, bf16[2048,256]{1,0:T(8,128)(2,1)S(1)} %copy-done.5, bf16[2048,128]{1,0:T(8,128)(2,1)S(1)} %copy-done, bf16[2048,128]{1,0:T(8,128)(2,1)S(1)} %copy-done.1, ...), custom_call_target="tpu_custom_call" | custom-call | flops 805306368 | bytes 8388608 | tf_op jit(solution)/shard_map/window/pallas_call | solution.py:570
  66.1 1.7 %copy-done.6 = bf16[16,384,256]{2,1,0:T(8,128)(2,1)} copy-done((bf16[16,384,256]{2,1,0:T(8,128)(2,1)}, bf16[16,384,256]{2,1,0:T(8,128)(2,1)S(1)}, u32[]{:S(2)}) %copy-start.6) | copy-done | bytes 3145752
  70.5 5.4 %all-to-all-start.2 = ((bf16[8,8,32,128]{3,2,1,0:T(8,128)(2,1)}), bf16[8,8,32,128]{3,2,1,0:T(8,128)(2,1)S(1)}, u32[]{:S(2)}, u32[]{:S(2)}) async-start(bf16[8,8,32,128]{3,2,1,0:T(8,128)(2,1)} %terms.1), calls=%async_computation.2 | async-start | bytes 1048576 | tf_op jit(solution)/shard_map/all_to_all | solution.py:625
  77.0 1.7 %collective-permute-done.8.got_ref = bf16[16,2,64,128]{3,2,1,0:T(8,128)(2,1)S(1)} collective-permute-done((bf16[16,2,64,128]{3,2,1,0:T(8,128)(2,1)}, bf16[16,2,64,128]{3,2,1,0:T(8,128)(2,1)S(1)}, u32[]{:S(2)}, u32[]{:S(2)}) %collective-permute-start.8) | collective-permute-done | bytes 524320 | tf_op jit(solution)/shard_map/ppermute | solution.py:600
  78.7 1.2 %copy-done.9 = f32[16,2,64,128]{3,2,1,0:T(8,128)S(1)} copy-done((f32[16,2,64,128]{3,2,1,0:T(8,128)S(1)}, f32[16,2,64,128]{3,2,1,0:T(8,128)}, u32[]{:S(2)}) %copy-start.9) | copy-done | bytes 1048600
  80.4 2.5 %copy-done.3 = bf16[16,640,256]{2,1,0:T(8,128)(2,1)S(1)} copy-done((bf16[16,640,256]{2,1,0:T(8,128)(2,1)S(1)}, bf16[16,640,256]{2,1,0:T(8,128)(2,1)}, u32[]{:S(2)}) %copy-start.3) | copy-done | bytes 5242904
  82.9 1.9 %copy-done.7 = bf16[16,384,256]{2,1,0:T(8,128)(2,1)S(1)} copy-done((bf16[16,384,256]{2,1,0:T(8,128)(2,1)S(1)}, bf16[16,384,256]{2,1,0:T(8,128)(2,1)}, u32[]{:S(2)}) %copy-start.7) | copy-done | bytes 3145752
  84.8 5.7 %queries.1 = bf16[2048,256]{1,0:T(8,128)(2,1)} custom-call(s32[16,3]{1,0:T(8,128)S(1)} %copy.9.random_blocks, bf16[2048,128]{1,0:T(8,128)(2,1)S(1)} %copy-done, bf16[2,128,128]{2,1,0:T(8,128)(2,1)S(1)} %copy-done.12, bf16[2,128,128]{2,1,0:T(8,128)(2,1)S(1)} %copy-done.15, bf16[8,2,64,128]{3,2,1,0:T(8,128)(2,1)S(1)} %all-to-all-done.1.mine_ref, ...), custom_call_target="tpu_custom_call" | custom-call | flops 1073741824 | bytes 8388608 | tf_op jit(solution)/shard_map/queries/pallas_call | solution.py:582
  91.2 1.3 %collective-permute-start.11 = (bf16[16,2,32,128]{3,2,1,0:T(8,128)(2,1)S(1)}, bf16[16,2,32,128]{3,2,1,0:T(8,128)(2,1)S(1)}, u32[]{:S(2)}, u32[]{:S(2)}) collective-permute-start(bf16[16,2,32,128]{3,2,1,0:T(8,128)(2,1)S(1)} %settle.1.refs_0_), channel_id=1, source_target_pairs={{0,2},{1,3},{2,0},{3,1},{4,6},{5,7},{6,4},{7,5},{8,10},{9,11},{10,... | collective-permute-start | bytes 786440 | tf_op jit(solution)/shard_map/ppermute | solution.py:637
  93.5 5.0 %collective-permute-done.11.refs_2_ = bf16[16,2,32,128]{3,2,1,0:T(8,128)(2,1)S(1)} collective-permute-done((bf16[16,2,32,128]{3,2,1,0:T(8,128)(2,1)S(1)}, bf16[16,2,32,128]{3,2,1,0:T(8,128)(2,1)S(1)}, u32[]{:S(2)}, u32[]{:S(2)}) %collective-permute-start.11) | collective-permute-done | bytes 262176 | tf_op jit(solution)/shard_map/ppermute | solution.py:637
  98.5 1.5 %collective-permute-start.12 = (bf16[16,2,32,128]{3,2,1,0:T(8,128)(2,1)S(1)}, bf16[16,2,32,128]{3,2,1,0:T(8,128)(2,1)S(1)}, u32[]{:S(2)}, u32[]{:S(2)}) collective-permute-start(bf16[16,2,32,128]{3,2,1,0:T(8,128)(2,1)S(1)} %collective-permute-done.11.refs_2_), channel_id=1, source_target_pairs={{0,1},{1,0},{2,3},{3,2},{4,5},{5,4},{6,7},{7,6},{8,9},{9,8},{10,11... | collective-permute-start | bytes 786440 | tf_op jit(solution)/shard_map/ppermute | solution.py:640
  (75 shorter events, 17.1 us)
Async XLA Ops:
  0.6 37.3 %copy-start.26 = (s32[16,3]{0,1:T(4,128)S(1)}, s32[16,3]{0,1:T(4,128)}, u32[]{:S(2)}) copy-start(s32[16,3]{0,1:T(4,128)} %param.10) | copy-start | bytes 580
  0.6 38.6 %copy-start.4 = (bf16[2048,256]{1,0:T(8,128)(2,1)S(1)}, bf16[2048,256]{1,0:T(8,128)(2,1)}, u32[]{:S(2)}) copy-start(bf16[2048,256]{1,0:T(8,128)(2,1)} %q_ref.5) | copy-start | bytes 3145732
  0.7 38.6 %copy-start.5 = (bf16[2048,256]{1,0:T(8,128)(2,1)S(1)}, bf16[2048,256]{1,0:T(8,128)(2,1)}, u32[]{:S(2)}) copy-start(bf16[2048,256]{1,0:T(8,128)(2,1)} %g_ref.5) | copy-start | bytes 3145732
  3.2 13.3 %all-to-all-start = ((bf16[8,144,128]{2,1,0:T(8,128)(2,1)}), bf16[8,144,128]{2,1,0:T(8,128)(2,1)S(1)}, u32[]{:S(2)}, u32[]{:S(2)}) async-start(bf16[8,144,128]{2,1,0:T(8,128)(2,1)} %get-tuple-element.32), calls=%async_computation | async-start | bytes 589824 | tf_op jit(solution)/shard_map/all_to_all | solution.py:489
  9.0 4.3 %collective-permute-start = (bf16[2,128,128]{2,1,0:T(8,128)(2,1)}, bf16[2,128,128]{2,1,0:T(8,128)(2,1)S(1)}, u32[]{:S(2)}, u32[]{:S(2)}) collective-permute-start(bf16[2,128,128]{2,1,0:T(8,128)(2,1)} %get-tuple-element.33), channel_id=1, source_target_pairs={{0,4},{4,0},{8,12},{12,8},{16,20},{20,16},{24,28},{28,24},{1,5},{5... | collective-permute-start | bytes 196616 | tf_op jit(solution)/shard_map/ppermute | solution.py:493
  9.0 7.5 %collective-permute-start.1 = (bf16[2,128,128]{2,1,0:T(8,128)(2,1)}, bf16[2,128,128]{2,1,0:T(8,128)(2,1)S(1)}, u32[]{:S(2)}, u32[]{:S(2)}) collective-permute-start(bf16[2,128,128]{2,1,0:T(8,128)(2,1)} %get-tuple-element.34), channel_id=1, source_target_pairs={{4,8},{8,4},{12,16},{16,12},{20,24},{24,20},{5,9},{9,5},{13,17},{1... | collective-permute-start | bytes 196616 | tf_op jit(solution)/shard_map/ppermute | solution.py:494
  20.1 17.5 %all-to-all-start.1 = ((bf16[8,2,64,128]{3,2,1,0:T(8,128)(2,1)}), bf16[8,2,64,128]{3,2,1,0:T(8,128)(2,1)S(1)}, u32[]{:S(2)}, u32[]{:S(2)}) async-start(bf16[8,2,64,128]{3,2,1,0:T(8,128)(2,1)} %get-tuple-element.36), calls=%async_computation.1 | async-start | bytes 524288 | tf_op jit(solution)/shard_map/all_to_all | solution.py:510
  26.1 8.8 %collective-permute-start.2 = (bf16[2,2,32,128]{3,2,1,0:T(8,128)(2,1)}, bf16[2,2,32,128]{3,2,1,0:T(8,128)(2,1)S(1)}, u32[]{:S(2)}, u32[]{:S(2)}) collective-permute-start(bf16[2,2,32,128]{3,2,1,0:T(8,128)(2,1)} %get-tuple-element.39.refs_0_), channel_id=1, source_target_pairs={{0,1},{1,0},{2,3},{3,2},{4,5},{5,4},{6,7},{7,6},{8,9},{9,8},{10,11... | collective-permute-start | bytes 98312 | tf_op jit(solution)/shard_map/ppermute | solution.py:512
  28.0 7.0 %collective-permute-start.3 = (bf16[2,2,32,128]{3,2,1,0:T(8,128)(2,1)}, bf16[2,2,32,128]{3,2,1,0:T(8,128)(2,1)S(1)}, u32[]{:S(2)}, u32[]{:S(2)}) collective-permute-start(bf16[2,2,32,128]{3,2,1,0:T(8,128)(2,1)} %get-tuple-element.39.refs_0_), channel_id=1, source_target_pairs={{0,2},{1,3},{2,0},{3,1},{4,6},{5,7},{6,4},{7,5},{8,10},{9,11},{10,... | collective-permute-start | bytes 98312 | tf_op jit(solution)/shard_map/ppermute | solution.py:512
  29.2 5.8 %collective-permute-start.4 = (bf16[2,2,32,128]{3,2,1,0:T(8,128)(2,1)}, bf16[2,2,32,128]{3,2,1,0:T(8,128)(2,1)S(1)}, u32[]{:S(2)}, u32[]{:S(2)}) collective-permute-start(bf16[2,2,32,128]{3,2,1,0:T(8,128)(2,1)} %get-tuple-element.39.refs_0_), channel_id=1, source_target_pairs={{0,3},{1,2},{2,1},{3,0},{4,7},{5,6},{6,5},{7,4},{8,11},{9,10},{10,... | collective-permute-start | bytes 98312 | tf_op jit(solution)/shard_map/ppermute | solution.py:512
  37.7 1.5 %collective-permute-start.5 = (bf16[8,2,64,128]{3,2,1,0:T(8,128)(2,1)S(1)}, bf16[8,2,64,128]{3,2,1,0:T(8,128)(2,1)S(1)}, u32[]{:S(2)}, u32[]{:S(2)}) collective-permute-start(bf16[8,2,64,128]{3,2,1,0:T(8,128)(2,1)S(1)} %all-to-all-done.1.mine_ref), channel_id=1, source_target_pairs={{0,1},{1,0},{2,3},{3,2},{4,5},{5,4},{6,7},{7,6},{8,9},{9,8},{10,11... | collective-permute-start | bytes 786440 | tf_op jit(solution)/shard_map/ppermute | solution.py:547
  38.0 22.9 %copy-start = (bf16[2048,128]{1,0:T(8,128)(2,1)S(1)}, bf16[2048,128]{1,0:T(8,128)(2,1)}, u32[]{:S(2)}) copy-start(bf16[2048,128]{1,0:T(8,128)(2,1)} %k_ref.9) | copy-start | bytes 1572868
  38.0 22.9 %copy-start.1 = (bf16[2048,128]{1,0:T(8,128)(2,1)S(1)}, bf16[2048,128]{1,0:T(8,128)(2,1)}, u32[]{:S(2)}) copy-start(bf16[2048,128]{1,0:T(8,128)(2,1)} %v_ref.7) | copy-start | bytes 1572868
  42.8 18.2 %copy-start.12 = (bf16[2,128,128]{2,1,0:T(8,128)(2,1)S(1)}, bf16[2,128,128]{2,1,0:T(8,128)(2,1)}, u32[]{:S(2)}) copy-start(bf16[2,128,128]{2,1,0:T(8,128)(2,1)} %copy-done.10) | copy-start | bytes 196612
  42.8 18.2 %copy-start.15 = (bf16[2,128,128]{2,1,0:T(8,128)(2,1)S(1)}, bf16[2,128,128]{2,1,0:T(8,128)(2,1)}, u32[]{:S(2)}) copy-start(bf16[2,128,128]{2,1,0:T(8,128)(2,1)} %copy-done.13) | copy-start | bytes 196612
  57.8 22.6 %copy-start.17 = (bf16[2,2,128,128]{3,2,1,0:T(8,128)(2,1)S(1)}, bf16[2,2,128,128]{3,2,1,0:T(8,128)(2,1)}, u32[]{:S(2)}) copy-start(bf16[2,2,128,128]{3,2,1,0:T(8,128)(2,1)} %glob.1.glob_ref) | copy-start | bytes 393220
  57.8 1.7 %collective-permute-start.6 = (bf16[12,2,64,128]{3,2,1,0:T(8,128)(2,1)S(1)}, bf16[12,2,64,128]{3,2,1,0:T(8,128)(2,1)S(1)}, u32[]{:S(2)}, u32[]{:S(2)}) collective-permute-start(bf16[12,2,64,128]{3,2,1,0:T(8,128)(2,1)S(1)} %get-tuple-element.44), channel_id=1, source_target_pairs={{0,1},{1,0},{2,3},{3,2},{4,5},{5,4},{6,7},{7,6},{8,9},{9,8},{10,11... | collective-permute-start | bytes 1179656 | tf_op jit(solution)/shard_map/ppermute | solution.py:600
  59.6 10.0 %collective-permute-start.7 = (bf16[12,2,32,128]{3,2,1,0:T(8,128)(2,1)S(1)}, bf16[12,2,32,128]{3,2,1,0:T(8,128)(2,1)S(1)}, u32[]{:S(2)}, u32[]{:S(2)}) collective-permute-start(bf16[12,2,32,128]{3,2,1,0:T(8,128)(2,1)S(1)} %get-tuple-element.46), channel_id=1, source_target_pairs={{0,2},{1,3},{2,0},{3,1},{4,6},{5,7},{6,4},{7,5},{8,10},{9,11},{10,... | collective-permute-start | bytes 589832 | tf_op jit(solution)/shard_map/ppermute | solution.py:611
  70.5 20.0 %all-to-all-start.2 = ((bf16[8,8,32,128]{3,2,1,0:T(8,128)(2,1)}), bf16[8,8,32,128]{3,2,1,0:T(8,128)(2,1)S(1)}, u32[]{:S(2)}, u32[]{:S(2)}) async-start(bf16[8,8,32,128]{3,2,1,0:T(8,128)(2,1)} %terms.1), calls=%async_computation.2 | async-start | bytes 1048576 | tf_op jit(solution)/shard_map/all_to_all | solution.py:625
  75.9 2.8 %collective-permute-start.8 = (bf16[16,2,64,128]{3,2,1,0:T(8,128)(2,1)}, bf16[16,2,64,128]{3,2,1,0:T(8,128)(2,1)S(1)}, u32[]{:S(2)}, u32[]{:S(2)}) collective-permute-start(bf16[16,2,64,128]{3,2,1,0:T(8,128)(2,1)} %copy-done.21), channel_id=1, source_target_pairs={{0,1},{1,0},{2,3},{3,2},{4,5},{5,4},{6,7},{7,6},{8,9},{9,8},{10,11... | collective-permute-start | bytes 1572872 | tf_op jit(solution)/shard_map/ppermute | solution.py:600
  80.1 10.4 %collective-permute-start.9 = (bf16[16,2,32,128]{3,2,1,0:T(8,128)(2,1)S(1)}, bf16[16,2,32,128]{3,2,1,0:T(8,128)(2,1)S(1)}, u32[]{:S(2)}, u32[]{:S(2)}) collective-permute-start(bf16[16,2,32,128]{3,2,1,0:T(8,128)(2,1)S(1)} %get-tuple-element.58), channel_id=1, source_target_pairs={{0,2},{1,3},{2,0},{3,1},{4,6},{5,7},{6,4},{7,5},{8,10},{9,11},{10,... | collective-permute-start | bytes 786440 | tf_op jit(solution)/shard_map/ppermute | solution.py:611
  91.2 7.3 %collective-permute-start.11 = (bf16[16,2,32,128]{3,2,1,0:T(8,128)(2,1)S(1)}, bf16[16,2,32,128]{3,2,1,0:T(8,128)(2,1)S(1)}, u32[]{:S(2)}, u32[]{:S(2)}) collective-permute-start(bf16[16,2,32,128]{3,2,1,0:T(8,128)(2,1)S(1)} %settle.1.refs_0_), channel_id=1, source_target_pairs={{0,2},{1,3},{2,0},{3,1},{4,6},{5,7},{6,4},{7,5},{8,10},{9,11},{10,... | collective-permute-start | bytes 786440 | tf_op jit(solution)/shard_map/ppermute | solution.py:637
  92.5 7.5 %collective-permute-start.10 = (bf16[16,2,32,128]{3,2,1,0:T(8,128)(2,1)S(1)}, bf16[16,2,32,128]{3,2,1,0:T(8,128)(2,1)S(1)}, u32[]{:S(2)}, u32[]{:S(2)}) collective-permute-start(bf16[16,2,32,128]{3,2,1,0:T(8,128)(2,1)S(1)} %settle.1.refs_0_), channel_id=1, source_target_pairs={{0,1},{1,0},{2,3},{3,2},{4,5},{5,4},{6,7},{7,6},{8,9},{9,8},{10,11... | collective-permute-start | bytes 786440 | tf_op jit(solution)/shard_map/ppermute | solution.py:640
  98.5 2.7 %collective-permute-start.12 = (bf16[16,2,32,128]{3,2,1,0:T(8,128)(2,1)S(1)}, bf16[16,2,32,128]{3,2,1,0:T(8,128)(2,1)S(1)}, u32[]{:S(2)}, u32[]{:S(2)}) collective-permute-start(bf16[16,2,32,128]{3,2,1,0:T(8,128)(2,1)S(1)} %collective-permute-done.11.refs_2_), channel_id=1, source_target_pairs={{0,1},{1,0},{2,3},{3,2},{4,5},{5,4},{6,7},{7,6},{8,9},{9,8},{10,11... | collective-permute-start | bytes 786440 | tf_op jit(solution)/shard_map/ppermute | solution.py:640
  (19 other events, 58.3 us)

commit v3 on v2

v3 whole, which is shorter than its diff:
```python
import functools
import math

import jax
import jax.numpy as jnp
from jax import lax
from jax.experimental import pallas as pl
from jax.experimental.pallas import tpu as pltpu
from jax.sharding import PartitionSpec as P

DH = 128
BLOCK = 128
HALF = BLOCK // 2
R = 3
G = 2
WINDOW = 3
FAR = R + G
LISTED = WINDOW + FAR
MIB = 1024 * 1024
MASKED = -1e30
FACTOR = float(DH) ** -0.5
SCALE = FACTOR * math.log2(math.e)
FOLD = 8
MARKS = 16

NT = (((1,), (1,)), ((), ()))
NN = (((1,), (0,)), ((), ()))
TN = (((0,), (0,)), ((), ()))


def mm(a, b, dims):
    return lax.dot_general(a, b, dims, preferred_element_type=jnp.float32)


def stack_heads(ref, u):
    rows = ref[u * BLOCK : (u + 1) * BLOCK, :]
    return jnp.concatenate(
        [rows[:, h * DH : (h + 1) * DH] for h in range(rows.shape[1] // DH)], axis=0
    )


def fold(x):
    return jnp.sum(x.reshape(x.shape[0] // FOLD, FOLD, x.shape[1]), axis=0)


def panel(k, v, q, g):
    s = mm(k, q, NT)
    dp = mm(v, g, NT)
    top = jnp.max(s, axis=0, keepdims=True) * SCALE
    e = jnp.exp2(s * SCALE - top)
    return top, e, dp, fold(e), fold(e * dp)


def places():
    head_index = lax.axis_index("head")
    return lax.rem(head_index, 2), lax.div(head_index, 2)


def glob_slices(peers):
    rows = 2 * G * HALF
    size = max(MARKS, rows // peers)
    return rows // size, size


def ask_kernel(
    global_blocks, random_blocks, random_ref, k_ref, v_ref, out_ref, low_ref, high_ref, owners, rows, sems
):
    tokens = k_ref.shape[0]
    blocks = tokens // BLOCK
    peers = out_ref.shape[0]
    core, _ = places()
    slices, size = glob_slices(peers)
    edges, copies = [], []

    def begin(group, src, dst):
        group.append(pltpu.make_async_copy(src, dst, sems.at[len(edges) + len(copies)]))
        group[-1].start()

    for j in range(G):
        start = lax.rem(global_blocks[j], blocks) * BLOCK + core * HALF
        start = pl.multiple_of(start, HALF)
        for which, ref in ((0, k_ref), (1, v_ref)):
            at = (2 * j + which) * HALF
            begin(copies, ref.at[pl.ds(start, HALF), :], rows.at[pl.ds(at, HALF), :])
    odd = lax.rem(lax.axis_index("seq"), 2)
    for which, ref in ((0, k_ref), (1, v_ref)):
        for edge_ref, at in ((low_ref, (1 - odd) * (tokens - BLOCK)), (high_ref, odd * (tokens - BLOCK))):
            start = pl.multiple_of(at, BLOCK)
            begin(edges, ref.at[pl.ds(start, BLOCK), :], edge_ref.at[which])
    wanted = random_ref[...]

    def mark(j, carry):
        within = wanted - j * blocks
        mine = jnp.logical_and(within >= 0, within < blocks)
        top = jnp.max(jnp.where(mine, within, -1).astype(jnp.float32))
        out_ref[j, :MARKS, :] = jnp.full((MARKS, DH), top, jnp.float32).astype(jnp.bfloat16)
        return carry

    lax.fori_loop(0, peers, mark, 0, unroll=min(peers, 8))
    for b in range(blocks):
        for r in range(R):
            owners[b * R + r] = lax.div(random_blocks[r, b], blocks)
    for copy in copies:
        copy.wait()
    out_ref[:slices, MARKS:, :] = rows[...].reshape(slices, size, DH)
    if slices < peers:
        out_ref[slices:, MARKS:, :] = jnp.zeros((peers - slices, size, DH), jnp.bfloat16)
    for copy in edges:
        copy.wait()


def serve_kernel(global_blocks, asked_ref, k_ref, v_ref, out_ref, requested_ref, sems):
    blocks = k_ref.shape[0] // BLOCK
    core, _ = places()
    peers = out_ref.shape[0]
    many = min(peers, 8)
    slices, size = glob_slices(peers)

    def copy(j, start, which, ref):
        return pltpu.make_async_copy(
            ref.at[pl.ds(start, HALF), :],
            out_ref.at[j, pl.ds(which * HALF, HALF), :],
            sems.at[j, which],
        )

    def begin(j, carry):
        wanted = jnp.max(asked_ref[j, :MARKS, :].astype(jnp.float32)).astype(jnp.int32)
        requested_ref[j] = wanted
        start = pl.multiple_of(jnp.clip(wanted, 0, blocks - 1) * BLOCK + core * HALF, HALF)
        copy(j, start, 0, k_ref).start()
        copy(j, start, 1, v_ref).start()
        return carry

    lax.fori_loop(0, peers, begin, 0, unroll=many)
    index = jnp.minimum(lax.axis_index("seq"), slices - 1)
    owner = lax.div(global_blocks[lax.div(index * size, 2 * HALF)], blocks)
    out_ref[:, 2 * HALF :, :] = jnp.broadcast_to(
        asked_ref[owner, MARKS:, :][None], (peers, size, DH)
    )

    def end(j, carry):
        copy(j, 0, 0, k_ref).wait()
        copy(j, 0, 1, v_ref).wait()
        return carry

    lax.fori_loop(0, peers, end, 0, unroll=many)


def split_kernel(count, keep_ref, got_ref, out_ref, *send_refs):
    share = out_ref.shape[2]
    _, column = places()
    own = pl.ds(pl.multiple_of(column * share, share), share)
    total = keep_ref[:, :, own, :].astype(jnp.float32) + got_ref[:, :, own, :].astype(jnp.float32)
    out_ref[...] = total.astype(out_ref.dtype)
    for m in range(1, count):
        there = pl.ds(pl.multiple_of((column ^ m) * share, share), share)
        send_refs[m - 1][...] = (
            keep_ref[:, :, there, :].astype(jnp.float32) + got_ref[:, :, there, :].astype(jnp.float32)
        ).astype(jnp.bfloat16)


def terms_kernel(keep_ref, *refs):
    *got_refs, terms_ref, low_ref, high_ref = refs
    peers, _, share, _ = terms_ref.shape
    odd = lax.rem(lax.axis_index("seq"), 2) == 1

    def total(slot, n=1):
        x = keep_ref[slot : slot + n].astype(jnp.float32)
        for ref in got_refs:
            x = x + ref[slot : slot + n].astype(jnp.float32)
        return x.astype(jnp.bfloat16)

    terms_ref[:, :2] = total(0, peers)
    glob = total(peers, G).reshape(1, 2 * G, share, DH)
    terms_ref[:, 2:] = jnp.broadcast_to(glob, (peers, 2 * G, share, DH))
    previous = total(peers + G)[0]
    following = total(peers + G + 1)[0]
    low_ref[...] = jnp.where(odd, previous, following)
    high_ref[...] = jnp.where(odd, following, previous)


def settle_kernel(requested, global_blocks, back_ref, low_ref, high_ref, *refs):
    *got_refs, out_ref, acc = refs
    blocks = out_ref.shape[0]
    peers, _, share, _ = back_ref.shape
    seq_index = lax.axis_index("seq")
    acc[...] = sum(ref[...].astype(jnp.float32) for ref in got_refs)
    at_low, at_high = edge_places(blocks)
    acc[jnp.clip(at_low - 1, 0, blocks - 1)] += low_ref[...].astype(jnp.float32)
    acc[jnp.clip(at_high - 1, 0, blocks - 1)] += high_ref[...].astype(jnp.float32)

    def one(j, carry):
        wanted = requested[j]

        @pl.when(wanted >= 0)
        def _():
            acc[wanted] += back_ref[j, :2].astype(jnp.float32)

        return carry

    lax.fori_loop(0, peers, one, 0)
    for j in range(G):

        @pl.when(lax.div(global_blocks[j], blocks) == seq_index)
        def _():
            rows = back_ref[:, 2 + 2 * j : 4 + 2 * j].astype(jnp.float32)
            acc[lax.rem(global_blocks[j], blocks)] += jnp.sum(rows, axis=0)

    out_ref[...] = acc[...].astype(jnp.bfloat16)


def join_kernel(count, *refs):
    *got_refs, dk_ref, dv_ref, dk, dv = refs
    blocks, _, share, _ = got_refs[0].shape
    core, column = places()
    for m in range(count):
        for c in range(2):
            at = (core ^ c) * HALF + (column ^ m) * share
            rows = pl.ds(pl.multiple_of(at, share), share)
            ref = got_refs[2 * m + c]
            dk[:, rows, :] = ref[:, 0]
            dv[:, rows, :] = ref[:, 1]
    dk_ref[...] = dk[...].reshape(dk_ref.shape)
    dv_ref[...] = dv[...].reshape(dv_ref.shape)


def edge_places(blocks):
    odd = lax.rem(lax.axis_index("seq"), 2)
    return (1 - odd) * (blocks + 1), odd * (blocks + 1)


def fill_window(k_ref, v_ref, low_ref, high_ref, k_all, v_all):
    rows = k_ref.shape[0]
    low, high = (pl.ds(pl.multiple_of(i * BLOCK, BLOCK), BLOCK) for i in edge_places(rows // BLOCK))
    for to, own, which in ((k_all, k_ref, 0), (v_all, v_ref, 1)):
        to[low, :] = low_ref[which]
        to[high, :] = high_ref[which]
        to[BLOCK : BLOCK + rows] = own[...]


def near_kernel(q_ref, g_ref, k_ref, v_ref, low_ref, high_ref, st_ref, k_all, v_all):
    step = pl.program_id(0)
    blocks = k_ref.shape[0] // BLOCK
    seq_index = lax.axis_index("seq")
    per = st_ref.shape[0]

    @pl.when(step == 0)
    def _():
        fill_window(k_ref, v_ref, low_ref, high_ref, k_all, v_all)

    for u in range(per):
        b = step * per + u
        q = stack_heads(q_ref, u)
        g = stack_heads(g_ref, u)
        no_left = jnp.logical_and(seq_index == 0, b == 0)
        no_right = jnp.logical_and(seq_index == lax.axis_size("seq") - 1, b == blocks - 1)
        biases = (jnp.where(no_left, MASKED, 0.0), None, jnp.where(no_right, MASKED, 0.0))
        for w in range(WINDOW):
            rows = pl.ds(pl.multiple_of((b + w) * BLOCK, BLOCK), BLOCK)
            top, _, _, l, d = panel(k_all[rows, :], v_all[rows, :], q, g)
            if biases[w] is not None:
                top = top + biases[w]
            st_ref[u, w : w + 1] = top
            st_ref[u, WINDOW + w : WINDOW + w + 1] = jnp.sum(l, axis=0, keepdims=True)
            st_ref[u, 2 * WINDOW + w : 2 * WINDOW + w + 1] = jnp.sum(d, axis=0, keepdims=True)


def far_kernel(
    owners, q_ref, g_ref, mine_ref, other_ref, st_ref, low_ref, high_ref,
    ds_ref, fd_ref, *refs,
):
    *share_refs, q_all, g_all, k_all, v_all, acc, e_all, dp_all, ds_all, in_sems, out_sems = refs
    blocks = q_ref.shape[0] // BLOCK
    peers = mine_ref.shape[0]
    core, column = places()
    own, opp = pl.ds(core * HALF, HALF), pl.ds((1 - core) * HALF, HALF)
    slices, size = glob_slices(peers)

    def at(b):
        return pl.ds(pl.multiple_of(b * BLOCK, BLOCK), BLOCK)

    def fetch(b, which):
        src, dst = ((q_ref, q_all), (g_ref, g_all))[which]
        return pltpu.make_async_copy(src.at[at(b), :], dst.at[at(b), :], in_sems.at[b, which])

    def put(b):
        return pltpu.make_async_copy(ds_all.at[b], ds_ref.at[b], out_sems.at[b])

    for b in range(blocks):
        fetch(b, 0).start()
        fetch(b, 1).start()
    for to, which in ((k_all, 0), (v_all, 1)):
        rows = slice(which * HALF, (which + 1) * HALF)
        to[:peers, own, :] = mine_ref[:, rows, :]
        to[:peers, opp, :] = other_ref[:, rows, :]
    for i in range(slices):
        unit, offset = divmod(i * size, HALF)
        to = (k_all, v_all)[unit % 2]
        slot = peers + unit // 2
        to[slot, pl.ds(pl.multiple_of(core * HALF + offset, MARKS), size), :] = mine_ref[i, 2 * HALF :, :]
        to[slot, pl.ds(pl.multiple_of((1 - core) * HALF + offset, MARKS), size), :] = other_ref[i, 2 * HALF :, :]
    acc[...] = jnp.zeros_like(acc)

    def heads(ref, b):
        rows = ref[at(b), :]
        return jnp.concatenate(
            [rows[:, h * DH : (h + 1) * DH] for h in range(rows.shape[1] // DH)], axis=0
        )

    def slots_of(b):
        return [owners[b * R + r] for r in range(R)] + [peers + j for j in range(G)]

    def work(new, new_slot, old, old_slot, stats):
        if new is not None:
            fetch(new, 0).wait()
            fetch(new, 1).wait()
            q1, g1, slots1 = heads(q_all, new), heads(g_all, new), slots_of(new)
        if old is not None:
            q2, g2, slots2 = heads(q_all, old), heads(g_all, old), slots_of(old)
        tops, ls, dd = [], [], []
        for i in range(FAR):
            rows = slice(i * BLOCK, (i + 1) * BLOCK)
            if new is not None:
                s = mm(k_all[slots1[i]], q1, NT)
                dp = mm(v_all[slots1[i]], g1, NT)
            if old is not None:
                p = e_all[old_slot, rows] * stats[i]
                ds = (p * (dp_all[old_slot, rows] - stats[FAR])).astype(jnp.bfloat16)
                ds_all[old, rows] = ds
                acc[slots2[i], 0] += mm(ds, q2, NN)
                acc[slots2[i], 1] += mm(p.astype(jnp.bfloat16), g2, NN)
            if new is not None:
                top = jnp.max(s, axis=0, keepdims=True) * SCALE
                e = jnp.exp2(s * SCALE - top)
                e_all[new_slot, rows] = e
                dp_all[new_slot, rows] = dp
                tops.append(top)
                ls.append(fold(e))
                dd.append(fold(e * dp))
        if old is not None:
            put(old).start()
        if new is None:
            return None
        near = [[st_ref[new, i * WINDOW + w : i * WINDOW + w + 1] for w in range(WINDOW)] for i in range(3)]
        top = functools.reduce(jnp.maximum, near[0] + tops)
        near_weight = [jnp.exp2(t - top) for t in near[0]]
        weight = [jnp.exp2(t - top) for t in tops]
        l = jnp.sum(sum(w * x for w, x in zip(weight, ls)), axis=0, keepdims=True)
        d = jnp.sum(sum(w * x for w, x in zip(weight, dd)), axis=0, keepdims=True)
        l = l + sum(w * x for w, x in zip(near_weight, near[1]))
        d = d + sum(w * x for w, x in zip(near_weight, near[2]))
        inv = 1.0 / l
        delta = d * inv
        for w in range(WINDOW):
            fd_ref[new, w : w + 1] = near[0][w]
            fd_ref[new, WINDOW + w : WINDOW + w + 1] = near_weight[w] * inv
        fd_ref[new, 2 * WINDOW : 2 * WINDOW + 1] = delta
        return tuple(w * inv for w in weight) + (delta,)

    def pair(t, stats):
        stats = work(2 * t + 1, 1, 2 * t, 0, stats)
        return work(2 * t + 2, 0, 2 * t + 1, 1, stats)

    stats = work(0, 0, None, None, None)
    stats = lax.fori_loop(0, blocks // 2 - 1, pair, stats)
    stats = work(blocks - 1, 1, blocks - 2, 0, stats)
    work(None, None, blocks - 1, 1, stats)

    for slot, w, b, swap in ((peers + G, 0, 0, 1), (peers + G + 1, WINDOW - 1, blocks - 1, 0)):
        odd = lax.rem(lax.axis_index("seq"), 2) == swap
        q, g = heads(q_all, b), heads(g_all, b)
        s = mm(jnp.where(odd, low_ref[0], high_ref[0]), q, NT)
        dp = mm(jnp.where(odd, low_ref[1], high_ref[1]), g, NT)
        p = jnp.exp2(s * SCALE - jnp.max(s, axis=0, keepdims=True) * SCALE)
        p = p * fd_ref[b, WINDOW + w : WINDOW + w + 1]
        ds = (p * (dp - fd_ref[b, 2 * WINDOW : 2 * WINDOW + 1])).astype(jnp.bfloat16)
        acc[slot, 0] = mm(ds, q, NN)
        acc[slot, 1] = mm(p.astype(jnp.bfloat16), g, NN)

    share = share_refs[0].shape[2]
    for m, ref in enumerate(share_refs):
        start = (core ^ (m & 1)) * HALF + (column ^ (m >> 1)) * share
        rows = pl.ds(pl.multiple_of(start, share), share)
        for which, f in ((0, FACTOR), (1, 1.0)):
            ref[:, which] = (acc[:, which, rows, :] * f).astype(ref.dtype)
    for b in range(blocks):
        put(b).wait()


def close_kernel(
    q_ref, g_ref, k_ref, v_ref, low_ref, high_ref, fd_ref, ds_ref, keep_ref, send_ref, k_all, v_all, acc
):
    step = pl.program_id(0)
    per = fd_ref.shape[0]
    core, _ = places()
    own, opp = pl.ds(core * HALF, HALF), pl.ds((1 - core) * HALF, HALF)

    @pl.when(step == 0)
    def _():
        fill_window(k_ref, v_ref, low_ref, high_ref, k_all, v_all)
        acc[...] = jnp.zeros_like(acc)

    for u in range(per):
        b = step * per + u
        q = stack_heads(q_ref, u)
        g = stack_heads(g_ref, u)
        delta = fd_ref[u, 2 * WINDOW : 2 * WINDOW + 1]
        ds, pb = [], []
        for w in range(WINDOW):
            rows = pl.ds(pl.multiple_of((b + w) * BLOCK, BLOCK), BLOCK)
            s = mm(k_all[rows, :], q, NT)
            dp = mm(v_all[rows, :], g, NT)
            top = fd_ref[u, w : w + 1]
            top = jnp.where(top < MASKED / 2, 0.0, top)
            p = jnp.exp2(s * SCALE - top) * fd_ref[u, WINDOW + w : WINDOW + w + 1]
            ds.append((p * (dp - delta)).astype(jnp.bfloat16))
            pb.append(p.astype(jnp.bfloat16))
        ds = jnp.concatenate(ds, axis=0)
        pb = jnp.concatenate(pb, axis=0)
        ds_ref[u] = ds
        shape = (WINDOW, BLOCK, DH)
        acc[pl.ds(b, WINDOW), 0] += mm(ds, q, NN).reshape(shape)
        acc[pl.ds(b, WINDOW), 1] += mm(pb, g, NN).reshape(shape)

    @pl.when(step == pl.num_programs(0) - 1)
    def _():
        for which, f in ((0, FACTOR), (1, 1.0)):
            keep_ref[:, which] = (acc[1:-1, which, own, :] * f).astype(keep_ref.dtype)
            send_ref[:, which] = (acc[1:-1, which, opp, :] * f).astype(jnp.bfloat16)


def queries_kernel(
    owners, k_ref, low_ref, high_ref, mine_ref, other_ref, dsw_ref, dsf_ref, dq_ref, k_all, kt_all
):
    blocks = k_ref.shape[0] // BLOCK
    peers = mine_ref.shape[0]
    per = dsw_ref.shape[0]
    core, _ = places()
    step = pl.program_id(0)
    first_random = blocks + 2
    first_global = first_random + peers
    slices, size = glob_slices(peers)

    @pl.when(step == 0)
    def _():
        at_low, at_high = edge_places(blocks)
        k_all[at_low] = low_ref[0]
        k_all[at_high] = high_ref[0]
        k_all[1 : blocks + 1] = k_ref[...].reshape(blocks, BLOCK, DH)
        for ref, c in ((mine_ref, core), (other_ref, 1 - core)):
            k_all[first_random:first_global, pl.ds(c * HALF, HALF), :] = ref[:, :HALF, :]
            for i in range(slices):
                unit, offset = divmod(i * size, HALF)
                if unit % 2 == 0:
                    rows = pl.ds(pl.multiple_of(c * HALF + offset, MARKS), size)
                    k_all[first_global + unit // 2, rows, :] = ref[i, 2 * HALF :, :]

        def turn(j, carry):
            kt_all[j] = k_all[j].T
            return carry

        lax.fori_loop(0, first_global + G, turn, 0, unroll=4)

    for u in range(per):
        b = step * per + u
        panels = [b + w for w in range(WINDOW)]
        panels += [first_random + owners[b * R + r] for r in range(R)]
        panels += [first_global + j for j in range(G)]
        turned = [kt_all[i] for i in panels]
        dqt = mm(jnp.concatenate(turned[:WINDOW], axis=1), dsw_ref[u], NN)
        dqt = (dqt + mm(jnp.concatenate(turned[WINDOW:], axis=1), dsf_ref[u], NN)) * FACTOR
        for h in range(dq_ref.shape[1] // DH):
            dq_ref[u * BLOCK : (u + 1) * BLOCK, h * DH : (h + 1) * DH] = (
                dqt[:, h * BLOCK : (h + 1) * BLOCK].T.astype(jnp.bfloat16)
            )


def whole(a):
    return pl.BlockSpec(a.shape, lambda i, *_: (0,) * len(a.shape))


def per_block(per, *rest):
    return pl.BlockSpec((per,) + rest, lambda i, *_: (i,) + (0,) * len(rest))


def partners(size, stride):
    return [(i, i ^ stride) for i in range(size)]


def body(query_vectors, key_vectors, value_vectors, output_grad, random_blocks, global_blocks):
    seq_count = lax.axis_size("seq")
    head_count = lax.axis_size("head")
    rows_dev, columns = query_vectors.shape
    blocks = rows_dev // BLOCK
    per = math.gcd(blocks, 4)
    steps = blocks // per
    lanes = columns // DH * BLOCK
    bf16 = jnp.bfloat16
    f32 = jnp.float32
    sds = jax.ShapeDtypeStruct
    core_pairs = partners(head_count, 1)
    limit = (16 + seq_count // 2) * MIB
    params = pltpu.CompilerParams(dimension_semantics=("arbitrary",), vmem_limit_bytes=limit)
    unit = 2 * blocks * lanes * BLOCK * DH

    vmem = pl.BlockSpec(memory_space=pltpu.VMEM)
    smem = pl.BlockSpec(memory_space=pltpu.SMEM)
    hbm = pl.BlockSpec(memory_space=pltpu.HBM)
    small = pltpu.CompilerParams(vmem_limit_bytes=limit)
    large = pltpu.CompilerParams(vmem_limit_bytes=60 * MIB)
    share = BLOCK // head_count
    columns_count = head_count // 2

    edge = (2, BLOCK, DH)
    _, size = glob_slices(seq_count)
    asking, to_low, to_high, owners = pl.pallas_call(
        ask_kernel,
        out_shape=(
            sds((seq_count, MARKS + size, DH), bf16),
            sds(edge, bf16),
            sds(edge, bf16),
            sds((blocks * R,), jnp.int32),
        ),
        in_specs=[smem, smem, vmem, hbm, hbm],
        out_specs=(vmem, vmem, vmem, smem),
        scratch_shapes=[
            pltpu.VMEM((2 * G * HALF, DH), bf16),
            pltpu.SemaphoreType.DMA((2 * G + 4,)),
        ],
        compiler_params=large,
        name="ask",
    )(global_blocks, random_blocks.T, random_blocks.T, key_vectors, value_vectors)
    asked = lax.all_to_all(asking, "seq", split_axis=0, concat_axis=0, tiled=True)

    low_pairs = [(i, i ^ 1) for i in range(seq_count)]
    high_pairs = [(i, i + 1 if i % 2 else i - 1) for i in range(1, seq_count - 1)]
    low = lax.ppermute(to_low, "seq", low_pairs)
    high = lax.ppermute(to_high, "seq", high_pairs)
    asked, low, high = lax.optimization_barrier((asked, low, high))

    served, requested = pl.pallas_call(
        serve_kernel,
        out_shape=(sds((seq_count, 2 * HALF + size, DH), bf16), sds((seq_count,), jnp.int32)),
        in_specs=[smem, vmem, hbm, hbm],
        out_specs=(vmem, smem),
        scratch_shapes=[pltpu.SemaphoreType.DMA((seq_count, 2))],
        compiler_params=large,
        name="serve",
    )(global_blocks, asked, key_vectors, value_vectors)
    mine = lax.all_to_all(served, "seq", split_axis=0, concat_axis=0, tiled=True)

    rows_spec = pl.BlockSpec((per * BLOCK, columns), lambda i, *_: (i, 0))
    st_spec = per_block(per, 2 * FOLD, lanes)
    fd_spec = per_block(per, FOLD, lanes)
    nearby = (key_vectors, value_vectors, low, high)
    window_scratch = [pltpu.VMEM(((blocks + 2) * BLOCK, DH), bf16)] * 2
    st = pl.pallas_call(
        near_kernel,
        out_shape=sds((blocks, 2 * FOLD, lanes), f32),
        grid=(steps,),
        in_specs=[rows_spec, rows_spec] + [whole(a) for a in nearby],
        out_specs=st_spec,
        scratch_shapes=window_scratch,
        compiler_params=large,
        cost_estimate=pl.CostEstimate(
            flops=2 * WINDOW * unit, bytes_accessed=4 * MIB, transcendentals=blocks * lanes * WINDOW * BLOCK
        ),
        name="near",
    )(query_vectors, output_grad, *nearby)
    mine, st = lax.optimization_barrier((mine, st))
    other = lax.ppermute(mine, "head", core_pairs)

    slots = seq_count + G + 2
    piece = (slots, 2, share, DH)
    dsf, fd, *pieces = pl.pallas_call(
        far_kernel,
        out_shape=(
            sds((blocks, FAR * BLOCK, lanes), bf16),
            sds((blocks, FOLD, lanes), f32),
        )
        + (sds(piece, bf16),) * head_count,
        in_specs=[smem, hbm, hbm] + [vmem] * 5,
        out_specs=(hbm, vmem) + (vmem,) * head_count,
        scratch_shapes=[pltpu.VMEM(query_vectors.shape, bf16)] * 2
        + [pltpu.VMEM((seq_count + G, BLOCK, DH), bf16)] * 2
        + [pltpu.VMEM((slots, 2, BLOCK, DH), f32)]
        + [pltpu.VMEM((2, FAR * BLOCK, lanes), f32)] * 2
        + [
            pltpu.VMEM((blocks, FAR * BLOCK, lanes), bf16),
            pltpu.SemaphoreType.DMA((blocks, 2)),
            pltpu.SemaphoreType.DMA((blocks,)),
        ],
        compiler_params=large,
        cost_estimate=pl.CostEstimate(
            flops=5 * FAR * unit, bytes_accessed=8 * MIB, transcendentals=blocks * lanes * FAR * BLOCK
        ),
        name="far",
    )(owners, query_vectors, output_grad, mine, other, st, low, high)

    piece_w = (blocks, 2, HALF, DH)
    near_spec = per_block(per, WINDOW * BLOCK, lanes)
    far_spec = per_block(per, FAR * BLOCK, lanes)
    dsw, keep_w, send_w = pl.pallas_call(
        close_kernel,
        out_shape=(sds((blocks, WINDOW * BLOCK, lanes), bf16), sds(piece_w, bf16), sds(piece_w, bf16)),
        grid=(steps,),
        in_specs=[rows_spec, rows_spec] + [whole(a) for a in nearby] + [fd_spec],
        out_specs=(near_spec, whole(sds(piece_w, bf16)), whole(sds(piece_w, bf16))),
        scratch_shapes=window_scratch + [pltpu.VMEM((blocks + 2, 2, BLOCK, DH), f32)],
        compiler_params=large,
        cost_estimate=pl.CostEstimate(flops=4 * WINDOW * unit, bytes_accessed=8 * MIB, transcendentals=0),
        name="close",
    )(query_vectors, output_grad, *nearby, fd)

    others = [m << 1 for m in range(1, columns_count)]

    def reduced(kept, sent, name, dtype):
        got = lax.ppermute(sent, "head", core_pairs)
        part = (kept.shape[0], 2, share, DH)
        home, *away = pl.pallas_call(
            functools.partial(split_kernel, columns_count),
            out_shape=(sds(part, dtype),) + (sds(part, bf16),) * len(others),
            in_specs=[vmem, vmem],
            out_specs=(vmem,) * (1 + len(others)),
            compiler_params=small,
            name=name,
        )(kept, got)
        return [home] + [
            lax.ppermute(a, "head", partners(head_count, m)) for a, m in zip(away, others)
        ]

    parts = pieces[:1] + [
        lax.ppermute(pieces[m], "head", partners(head_count, m)) for m in range(1, head_count)
    ]
    parts[-1], send_w = lax.optimization_barrier((parts[-1], send_w))
    terms, to_low, to_high = pl.pallas_call(
        terms_kernel,
        out_shape=(
            sds((seq_count, 2 + 2 * G, share, DH), bf16),
            sds((2, share, DH), bf16),
            sds((2, share, DH), bf16),
        ),
        in_specs=[vmem] * len(parts),
        out_specs=(vmem,) * 3,
        compiler_params=small,
        name="terms",
    )(*parts)
    parts_w = reduced(keep_w, send_w, "split_close", bf16)
    dsw, to_low = lax.optimization_barrier((dsw, to_low))
    query_grad = pl.pallas_call(
        queries_kernel,
        out_shape=sds(query_vectors.shape, bf16),
        grid_spec=pltpu.PrefetchScalarGridSpec(
            num_scalar_prefetch=1,
            grid=(steps,),
            in_specs=[whole(a) for a in (key_vectors, low, high, mine, other)] + [near_spec, far_spec],
            out_specs=rows_spec,
            scratch_shapes=[pltpu.VMEM((blocks + 2 + seq_count + G, BLOCK, DH), bf16)] * 2,
        ),
        compiler_params=large,
        cost_estimate=pl.CostEstimate(flops=LISTED * unit, bytes_accessed=8 * MIB, transcendentals=0),
        name="queries",
    )(owners, key_vectors, low, high, mine, other, dsw, dsf)
    back = lax.all_to_all(terms, "seq", split_axis=0, concat_axis=0, tiled=True)
    from_low = lax.ppermute(to_low, "seq", low_pairs)
    from_high = lax.ppermute(to_high, "seq", high_pairs)
    back, query_grad = lax.optimization_barrier((back, query_grad))
    held = pl.pallas_call(
        settle_kernel,
        out_shape=sds((blocks, 2, share, DH), bf16),
        in_specs=[smem, smem] + [vmem] * (3 + len(parts_w)),
        out_specs=vmem,
        scratch_shapes=[pltpu.VMEM((blocks, 2, share, DH), f32)],
        compiler_params=small,
        name="settle",
    )(requested, global_blocks, back, from_low, from_high, *parts_w)

    rows = [held] + [lax.ppermute(held, "head", partners(head_count, m)) for m in others]
    pieces = []
    for a in rows:
        pieces += [a, lax.ppermute(a, "head", core_pairs)]
    key_grad, value_grad = pl.pallas_call(
        functools.partial(join_kernel, columns_count),
        out_shape=(sds(key_vectors.shape, bf16),) * 2,
        in_specs=[vmem] * len(pieces),
        out_specs=(vmem, vmem),
        scratch_shapes=[pltpu.VMEM((blocks, BLOCK, DH), bf16)] * 2,
        compiler_params=small,
        name="join",
    )(*pieces)
    return query_grad, key_grad, value_grad


def solution(mesh):
    return jax.shard_map(
        body,
        mesh=mesh,
        in_specs=(
            P("seq", "head"),
            P("seq", None),
            P("seq", None),
            P("seq", "head"),
            P("seq", None),
            P(),
        ),
        out_specs=(P("seq", "head"), P("seq", None), P("seq", None)),
        check_vma=False,
    )
```

time: 104 us -> 94 us (0.904)
  local copies, waits for them, and re-layouts: 17 us -> 2.44 us
  starting transfers between devices: 31.8 us -> 37.7 us
  waiting for transfers between devices: 13.9 us -> 9.6 us
  Pallas kernels: 38.8 us -> 42.5 us
    unnamed x55 -> x18, local copies, waits for them, and re-layouts: 17 us -> 2.44 us
    ppermute x1, starting transfers between devices: 0.23 us -> 4.81 us  [body(): other = lax.ppermute(mine, 'head', core_pairs)]
    ppermute x2 -> x1, waiting for transfers between devices: 3.24 us -> 0.01 us  [reduced(): got = lax.ppermute(sent, 'head', core_pairs)]
    ppermute x3 -> x5, starting transfers between devices: 3.45 us -> 6.2 us  [the longest x1 4.16 us: body(): from_high = lax.ppermute(to_high, 'seq', high_pairs)]
    ppermute x2, starting transfers between devices: 2.47 us -> 4.87 us  [body(): pieces += [a, lax.ppermute(a, 'head', core_pairs)]]
    pallas_call x1, Pallas kernels: 5.68 us -> 7.65 us  [body(): pl.pallas_call(queries_kernel, out_shape=sds(query_vectors.shape, bf16),...]
    pallas_call x6 -> x5, Pallas kernels: 25.7 us -> 27.5 us  [the longest x1 13.4 us: body(): pl.pallas_call(far_kernel, out_shape=(sds((blocks, FAR * BLOCK, lanes), b...]
    ppermute x1, waiting for transfers between devices: 5.05 us -> 3.59 us  [body(): lax.ppermute(held, 'head', partners(head_count, m))]
  transfers between devices with their start and end apart: 16 -> 16, of which waited for: 6 -> 6; matrix products, arithmetic and copies ran while one was open for 0% -> 0% of each run, Pallas kernels for 17% -> 24%
where the time goes in v3:
time: 94 us; the launch traced here: 93 us
  Pallas kernels  42.5 us (45%)
  starting transfers between devices  37.7 us (40%)
  waiting for transfers between devices  9.6 us (10%)
  local copies, waits for them, and re-layouts  2.44 us (3%)
    pallas_call x1, Pallas kernels, body(): pl.pallas_call(far_kernel, out_shape=(sds((blocks, FAR * BLOCK, lanes), b...  13.4 us
    pallas_call x1, Pallas kernels, body(): pl.pallas_call(close_kernel, out_shape=(sds((blocks, WINDOW * BLOCK, lane...  8.03 us
    pallas_call x1, Pallas kernels, body(): pl.pallas_call(queries_kernel, out_shape=sds(query_vectors.shape, bf16),...  7.65 us
    all_to_all x1, starting transfers between devices, body(): lax.all_to_all(asking, 'seq', split_axis=0, concat_axis=0, tiled=True)  5.79 us
    all_to_all x1, starting transfers between devices, body(): lax.all_to_all(served, 'seq', split_axis=0, concat_axis=0, tiled=True)  5.42 us
    pallas_call x1, Pallas kernels, body(): pl.pallas_call(near_kernel, out_shape=sds((blocks, 2 * FOLD, lanes), f32)...  5.37 us
    ppermute x2, starting transfers between devices, body(): pieces += [a, lax.ppermute(a, 'head', core_pairs)]  4.87 us
    ppermute x1, starting transfers between devices, body(): other = lax.ppermute(mine, 'head', core_pairs)  4.81 us
  transfers between devices with their start and end apart: 16, of which 6 were waited for; matrix products, arithmetic and copies ran while one was open for 0% of the time, Pallas kernels for 24%

profile of v3, /device:TPU:5, one launch (start us, length us, event | category | flops | bytes accessed | tf_op | source)
XLA Modules:
  0.0 93.0 jit_solution(12089336628310878556)
XLA Ops:
  0.6 2.4 %ask.1 = (bf16[8,48,128]{2,1,0:T(8,128)(2,1)}, bf16[2,128,128]{2,1,0:T(8,128)(2,1)}, bf16[2,128,128]{2,1,0:T(8,128)(2,1)}, s32[48]{0:T(128)}) custom-call(s32[2]{0:T(128)} %global_blocks.5, s32[3,16]{1,0:T(4,128)} %bitcast.1, s32[3,16]{1,0:T(4,128)} %bitcast.2, bf16[2048,128]{1,0:T(8,128)(2,1)} %k_ref.9, bf16[2048,128]{1,0:T(8,128)(2,1)} %v_ref.7), custom_call_target="tpu_custom_call" | custom-call | tf_op jit(solution)/shard_map/ask/pallas_call | solution.py:516
  3.0 5.8 %all-to-all-start = ((bf16[8,48,128]{2,1,0:T(8,128)(2,1)}), bf16[8,48,128]{2,1,0:T(8,128)(2,1)S(1)}, u32[]{:S(2)}, u32[]{:S(2)}) async-start(bf16[8,48,128]{2,1,0:T(8,128)(2,1)} %get-tuple-element.37), calls=%async_computation | async-start | bytes 196608 | tf_op jit(solution)/shard_map/all_to_all | solution.py:533
  8.8 4.2 %collective-permute-start.1 = (bf16[2,128,128]{2,1,0:T(8,128)(2,1)}, bf16[2,128,128]{2,1,0:T(8,128)(2,1)S(1)}, u32[]{:S(2)}, u32[]{:S(2)}) collective-permute-start(bf16[2,128,128]{2,1,0:T(8,128)(2,1)} %get-tuple-element.39), channel_id=1, source_target_pairs={{4,8},{8,4},{12,16},{16,12},{20,24},{24,20},{5,9},{9,5},{13,17},{1... | collective-permute-start | bytes 196616 | tf_op jit(solution)/shard_map/ppermute | solution.py:538
  13.1 2.1 %collective-permute-done.1.high_ref = bf16[2,128,128]{2,1,0:T(8,128)(2,1)S(1)} collective-permute-done((bf16[2,128,128]{2,1,0:T(8,128)(2,1)}, bf16[2,128,128]{2,1,0:T(8,128)(2,1)S(1)}, u32[]{:S(2)}, u32[]{:S(2)}) %collective-permute-start.1) | collective-permute-done | bytes 65568 | tf_op jit(solution)/shard_map/ppermute | solution.py:538
  15.9 2.8 %serve.1 = (bf16[8,160,128]{2,1,0:T(8,128)(2,1)}, s32[8]{0:T(128)}) custom-call(s32[2]{0:T(128)} %global_blocks.5, bf16[8,48,128]{2,1,0:T(8,128)(2,1)} %copy-done.5, bf16[2048,128]{1,0:T(8,128)(2,1)} %k_ref.9, bf16[2048,128]{1,0:T(8,128)(2,1)} %v_ref.7), custom_call_target="tpu_custom_call" | custom-call | tf_op jit(solution)/shard_map/serve/pallas_call | solution.py:541
  18.7 5.4 %all-to-all-start.1 = ((bf16[8,160,128]{2,1,0:T(8,128)(2,1)}), bf16[8,160,128]{2,1,0:T(8,128)(2,1)S(1)}, u32[]{:S(2)}, u32[]{:S(2)}) async-start(bf16[8,160,128]{2,1,0:T(8,128)(2,1)} %get-tuple-element.41), calls=%async_computation.1 | async-start | bytes 655360 | tf_op jit(solution)/shard_map/all_to_all | solution.py:550
  24.1 5.4 %near.1.st_ref = f32[16,16,256]{2,1,0:T(8,128)} custom-call(bf16[2048,256]{1,0:T(8,128)(2,1)} %q_ref.5, bf16[2048,256]{1,0:T(8,128)(2,1)} %g_ref.5, bf16[2048,128]{1,0:T(8,128)(2,1)} %k_ref.9, bf16[2048,128]{1,0:T(8,128)(2,1)} %v_ref.7, bf16[2,128,128]{2,1,0:T(8,128)(2,1)} %copy-done.7, bf16[2,128,128]{2,1,0:T(8,128)(2,1)} %copy-done.8), custom_call_target="tpu_custom_call" | custom-call | flops 805306368 | bytes 4194304 | tf_op jit(solution)/shard_map/near/pallas_call | solution.py:557
  30.3 4.8 %collective-permute-start.2 = (bf16[8,160,128]{2,1,0:T(8,128)(2,1)S(1)}, bf16[8,160,128]{2,1,0:T(8,128)(2,1)S(1)}, u32[]{:S(2)}, u32[]{:S(2)}) collective-permute-start(bf16[8,160,128]{2,1,0:T(8,128)(2,1)S(1)} %all-to-all-done.1.mine_ref), channel_id=1, source_target_pairs={{0,1},{1,0},{2,3},{3,2},{4,5},{5,4},{6,7},{7,6},{8,9},{9,8},{10,11... | collective-permute-start | bytes 983048 | tf_op jit(solution)/shard_map/ppermute | solution.py:571
  35.1 1.3 %collective-permute-done.2.other_ref = bf16[8,160,128]{2,1,0:T(8,128)(2,1)S(1)} collective-permute-done((bf16[8,160,128]{2,1,0:T(8,128)(2,1)S(1)}, bf16[8,160,128]{2,1,0:T(8,128)(2,1)S(1)}, u32[]{:S(2)}, u32[]{:S(2)}) %collective-permute-start.2) | collective-permute-done | bytes 327712 | tf_op jit(solution)/shard_map/ppermute | solution.py:571
  37.1 13.4 %far.1 = (bf16[16,640,256]{2,1,0:T(8,128)(2,1)}, f32[16,8,256]{2,1,0:T(8,128)}, bf16[12,2,32,128]{3,2,1,0:T(8,128)(2,1)}, bf16[12,2,32,128]{3,2,1,0:T(8,128)(2,1...) custom-call(s32[48]{0:T(128)} %get-tuple-element.36.owners, bf16[2048,256]{1,0:T(8,128)(2,1)} %q_ref.5, ...), custom_call_target="tpu_custom_call" | custom-call | flops 3355443200 | bytes 8388608 | tf_op jit(solution)/shard_map/far/pallas_call | solution.py:575
  50.5 1.5 %collective-permute-start.5 = (bf16[12,2,32,128]{3,2,1,0:T(8,128)(2,1)}, bf16[12,2,32,128]{3,2,1,0:T(8,128)(2,1)S(1)}, u32[]{:S(2)}, u32[]{:S(2)}) collective-permute-start(bf16[12,2,32,128]{3,2,1,0:T(8,128)(2,1)} %get-tuple-element.49), channel_id=1, source_target_pairs={{0,3},{1,2},{2,1},{3,0},{4,7},{5,6},{6,5},{7,4},{8,11},{9,10},{10,... | collective-permute-start | bytes 589832 | tf_op jit(solution)/shard_map/ppermute | solution.py:633
  52.4 8.0 %close.1 = (bf16[16,384,256]{2,1,0:T(8,128)(2,1)}, bf16[16,2,64,128]{3,2,1,0:T(8,128)(2,1)}, bf16[16,2,64,128]{3,2,1,0:T(8,128)(2,1)}) custom-call(bf16[2048,256]{1,0:T(8,128)(2,1)} %q_ref.5, bf16[2048,256]{1,0:T(8,128)(2,1)} %g_ref.5, bf16[2048,128]{1,0:T(8,128)(2,1)} %k_ref.9, bf16[2048,128]{1,0:T(8,128)(2,1)} %v_ref.7, bf16[2,128,128]{2,1,0:T(8,128)(2,1)} %copy-done.7, ...), custom_call_target="tpu_custom_call" | custom-call | flops 1610612736 | bytes 8388608 | tf_op jit(solution)/shard_map/close/pallas_call | solution.py:603
  61.8 0.9 terms.1
  62.7 4.0 %all-to-all-start.2 = ((bf16[8,6,32,128]{3,2,1,0:T(8,128)(2,1)}), bf16[8,6,32,128]{3,2,1,0:T(8,128)(2,1)S(1)}, u32[]{:S(2)}, u32[]{:S(2)}) async-start(bf16[8,6,32,128]{3,2,1,0:T(8,128)(2,1)} %get-tuple-element.53), calls=%async_computation.2 | async-start | bytes 786432 | tf_op jit(solution)/shard_map/all_to_all | solution.py:664
  66.7 1.0 %copy-done = bf16[16,2,64,128]{3,2,1,0:T(8,128)(2,1)S(1)} copy-done((bf16[16,2,64,128]{3,2,1,0:T(8,128)(2,1)S(1)}, bf16[16,2,64,128]{3,2,1,0:T(8,128)(2,1)}, u32[]{:S(2)}) %copy-start) | copy-done | bytes 524312
  67.9 1.3 %collective-permute-start.9 = (bf16[16,2,32,128]{3,2,1,0:T(8,128)(2,1)S(1)}, bf16[16,2,32,128]{3,2,1,0:T(8,128)(2,1)S(1)}, u32[]{:S(2)}, u32[]{:S(2)}) collective-permute-start(bf16[16,2,32,128]{3,2,1,0:T(8,128)(2,1)S(1)} %get-tuple-element.66), channel_id=1, source_target_pairs={{0,2},{1,3},{2,0},{3,1},{4,6},{5,7},{6,4},{7,5},{8,10},{9,11},{10,... | collective-permute-start | bytes 786440 | tf_op jit(solution)/shard_map/ppermute | solution.py:629
  69.2 4.2 %collective-permute-start.7 = (bf16[2,32,128]{2,1,0:T(8,128)(2,1)S(1)}, bf16[2,32,128]{2,1,0:T(8,128)(2,1)S(1)}, u32[]{:S(2)}, u32[]{:S(2)}) collective-permute-start(bf16[2,32,128]{2,1,0:T(8,128)(2,1)S(1)} %get-tuple-element.62), channel_id=1, source_target_pairs={{4,8},{8,4},{12,16},{16,12},{20,24},{24,20},{5,9},{9,5},{13,17},{1... | collective-permute-start | bytes 49160 | tf_op jit(solution)/shard_map/ppermute | solution.py:666
  73.4 7.7 %queries.1 = bf16[2048,256]{1,0:T(8,128)(2,1)} custom-call(s32[48]{0:T(128)} %get-tuple-element.36.owners, bf16[2048,128]{1,0:T(8,128)(2,1)} %k_ref.9, bf16[2,128,128]{2,1,0:T(8,128)(2,1)} %copy-done.7, bf16[2,128,128]{2,1,0:T(8,128)(2,1)} %copy-done.8, bf16[8,160,128]{2,1,0:T(8,128)(2,1)} %copy-done.4, bf16[8,160,128]{2,1,0:T(8,128)(2,1)} %copy-done.6, ...), custom_call_target="tpu_custom_call" | custom-call | flops 1073741824 | bytes 8388608 | tf_op jit(solution)/shard_map/queries/pallas_call | solution.py:650
  81.1 0.8 settle.1.refs_0_
  82.3 2.1 %collective-permute-start.10 = (bf16[16,2,32,128]{3,2,1,0:T(8,128)(2,1)S(1)}, bf16[16,2,32,128]{3,2,1,0:T(8,128)(2,1)S(1)}, u32[]{:S(2)}, u32[]{:S(2)}) collective-permute-start(bf16[16,2,32,128]{3,2,1,0:T(8,128)(2,1)S(1)} %settle.1.refs_0_), channel_id=1, source_target_pairs={{0,1},{1,0},{2,3},{3,2},{4,5},{5,4},{6,7},{7,6},{8,9},{9,8},{10,11... | collective-permute-start | bytes 786440 | tf_op jit(solution)/shard_map/ppermute | solution.py:681
  84.4 3.6 %collective-permute-done.11.refs_2_ = bf16[16,2,32,128]{3,2,1,0:T(8,128)(2,1)S(1)} collective-permute-done((bf16[16,2,32,128]{3,2,1,0:T(8,128)(2,1)S(1)}, bf16[16,2,32,128]{3,2,1,0:T(8,128)(2,1)S(1)}, u32[]{:S(2)}, u32[]{:S(2)}) %collective-permute-start.11) | collective-permute-done | bytes 262176 | tf_op jit(solution)/shard_map/ppermute | solution.py:678
  88.0 2.8 %collective-permute-start.12 = (bf16[16,2,32,128]{3,2,1,0:T(8,128)(2,1)S(1)}, bf16[16,2,32,128]{3,2,1,0:T(8,128)(2,1)S(1)}, u32[]{:S(2)}, u32[]{:S(2)}) collective-permute-start(bf16[16,2,32,128]{3,2,1,0:T(8,128)(2,1)S(1)} %collective-permute-done.11.refs_2_), channel_id=1, source_target_pairs={{0,1},{1,0},{2,3},{3,2},{4,5},{5,4},{6,7},{7,6},{8,9},{9,8},{10,11... | collective-permute-start | bytes 786440 | tf_op jit(solution)/shard_map/ppermute | solution.py:681
  90.8 1.2 %collective-permute-done.12.refs_3_ = bf16[16,2,32,128]{3,2,1,0:T(8,128)(2,1)S(1)} collective-permute-done((bf16[16,2,32,128]{3,2,1,0:T(8,128)(2,1)S(1)}, bf16[16,2,32,128]{3,2,1,0:T(8,128)(2,1)S(1)}, u32[]{:S(2)}, u32[]{:S(2)}) %collective-permute-start.12) | collective-permute-done | bytes 262176 | tf_op jit(solution)/shard_map/ppermute | solution.py:681
  91.9 1.1 %join.1 = (bf16[2048,128]{1,0:T(8,128)(2,1)}, bf16[2048,128]{1,0:T(8,128)(2,1)}) custom-call(bf16[16,2,32,128]{3,2,1,0:T(8,128)(2,1)S(1)} %settle.1.refs_0_, bf16[16,2,32,128]{3,2,1,0:T(8,128)(2,1)S(1)} %collective-permute-done.10.refs_1_, bf16[16,2,32,128]{3,2,1,0:T(8,128)(2,1)S(1)} %collective-permute-done.11.refs_2_, ...), custom_call_target="tpu_custom_call" | custom-call | tf_op jit(solution)/shard_map/join/pallas_call | solution.py:682
  (36 shorter events, 4.6 us)
Async XLA Ops:
  3.0 12.2 %all-to-all-start = ((bf16[8,48,128]{2,1,0:T(8,128)(2,1)}), bf16[8,48,128]{2,1,0:T(8,128)(2,1)S(1)}, u32[]{:S(2)}, u32[]{:S(2)}) async-start(bf16[8,48,128]{2,1,0:T(8,128)(2,1)} %get-tuple-element.37), calls=%async_computation | async-start | bytes 196608 | tf_op jit(solution)/shard_map/all_to_all | solution.py:533
  8.8 4.3 %collective-permute-start = (bf16[2,128,128]{2,1,0:T(8,128)(2,1)}, bf16[2,128,128]{2,1,0:T(8,128)(2,1)S(1)}, u32[]{:S(2)}, u32[]{:S(2)}) collective-permute-start(bf16[2,128,128]{2,1,0:T(8,128)(2,1)} %get-tuple-element.38), channel_id=1, source_target_pairs={{0,4},{4,0},{8,12},{12,8},{16,20},{20,16},{24,28},{28,24},{1,5},{5... | collective-permute-start | bytes 196616 | tf_op jit(solution)/shard_map/ppermute | solution.py:537
  8.8 6.4 %collective-permute-start.1 = (bf16[2,128,128]{2,1,0:T(8,128)(2,1)}, bf16[2,128,128]{2,1,0:T(8,128)(2,1)S(1)}, u32[]{:S(2)}, u32[]{:S(2)}) collective-permute-start(bf16[2,128,128]{2,1,0:T(8,128)(2,1)} %get-tuple-element.39), channel_id=1, source_target_pairs={{4,8},{8,4},{12,16},{16,12},{20,24},{24,20},{5,9},{9,5},{13,17},{1... | collective-permute-start | bytes 196616 | tf_op jit(solution)/shard_map/ppermute | solution.py:538
  13.1 11.0 %copy-start.7 = (bf16[2,128,128]{2,1,0:T(8,128)(2,1)}, bf16[2,128,128]{2,1,0:T(8,128)(2,1)S(1)}, u32[]{:S(2)}) copy-start(bf16[2,128,128]{2,1,0:T(8,128)(2,1)S(1)} %collective-permute-done.low_ref) | copy-start | bytes 196612
  15.2 8.9 %copy-start.8 = (bf16[2,128,128]{2,1,0:T(8,128)(2,1)}, bf16[2,128,128]{2,1,0:T(8,128)(2,1)S(1)}, u32[]{:S(2)}) copy-start(bf16[2,128,128]{2,1,0:T(8,128)(2,1)S(1)} %collective-permute-done.1.high_ref) | copy-start | bytes 196612
  18.7 11.6 %all-to-all-start.1 = ((bf16[8,160,128]{2,1,0:T(8,128)(2,1)}), bf16[8,160,128]{2,1,0:T(8,128)(2,1)S(1)}, u32[]{:S(2)}, u32[]{:S(2)}) async-start(bf16[8,160,128]{2,1,0:T(8,128)(2,1)} %get-tuple-element.41), calls=%async_computation.1 | async-start | bytes 655360 | tf_op jit(solution)/shard_map/all_to_all | solution.py:550
  30.3 6.1 %copy-start.4 = (bf16[8,160,128]{2,1,0:T(8,128)(2,1)}, bf16[8,160,128]{2,1,0:T(8,128)(2,1)S(1)}, u32[]{:S(2)}) copy-start(bf16[8,160,128]{2,1,0:T(8,128)(2,1)S(1)} %all-to-all-done.1.mine_ref) | copy-start | bytes 983044
  30.3 6.1 %collective-permute-start.2 = (bf16[8,160,128]{2,1,0:T(8,128)(2,1)S(1)}, bf16[8,160,128]{2,1,0:T(8,128)(2,1)S(1)}, u32[]{:S(2)}, u32[]{:S(2)}) collective-permute-start(bf16[8,160,128]{2,1,0:T(8,128)(2,1)S(1)} %all-to-all-done.1.mine_ref), channel_id=1, source_target_pairs={{0,1},{1,0},{2,3},{3,2},{4,5},{5,4},{6,7},{7,6},{8,9},{9,8},{10,11... | collective-permute-start | bytes 983048 | tf_op jit(solution)/shard_map/ppermute | solution.py:571
  36.4 0.7 copy-start.6
  50.5 11.4 %copy-start.1 = (bf16[12,2,32,128]{3,2,1,0:T(8,128)(2,1)S(1)}, bf16[12,2,32,128]{3,2,1,0:T(8,128)(2,1)}, u32[]{:S(2)}) copy-start(bf16[12,2,32,128]{3,2,1,0:T(8,128)(2,1)} %get-tuple-element.46.keep_ref) | copy-start | bytes 589828
  50.5 10.0 %collective-permute-start.5 = (bf16[12,2,32,128]{3,2,1,0:T(8,128)(2,1)}, bf16[12,2,32,128]{3,2,1,0:T(8,128)(2,1)S(1)}, u32[]{:S(2)}, u32[]{:S(2)}) collective-permute-start(bf16[12,2,32,128]{3,2,1,0:T(8,128)(2,1)} %get-tuple-element.49), channel_id=1, source_target_pairs={{0,3},{1,2},{2,1},{3,0},{4,7},{5,6},{6,5},{7,4},{8,11},{9,10},{10,... | collective-permute-start | bytes 589832 | tf_op jit(solution)/shard_map/ppermute | solution.py:633
  52.0 9.2 %collective-permute-start.3 = (bf16[12,2,32,128]{3,2,1,0:T(8,128)(2,1)}, bf16[12,2,32,128]{3,2,1,0:T(8,128)(2,1)S(1)}, u32[]{:S(2)}, u32[]{:S(2)}) collective-permute-start(bf16[12,2,32,128]{3,2,1,0:T(8,128)(2,1)} %get-tuple-element.47), channel_id=1, source_target_pairs={{0,1},{1,0},{2,3},{3,2},{4,5},{5,4},{6,7},{7,6},{8,9},{9,8},{10,11... | collective-permute-start | bytes 589832 | tf_op jit(solution)/shard_map/ppermute | solution.py:633
  52.1 9.7 %collective-permute-start.4 = (bf16[12,2,32,128]{3,2,1,0:T(8,128)(2,1)}, bf16[12,2,32,128]{3,2,1,0:T(8,128)(2,1)S(1)}, u32[]{:S(2)}, u32[]{:S(2)}) collective-permute-start(bf16[12,2,32,128]{3,2,1,0:T(8,128)(2,1)} %get-tuple-element.48), channel_id=1, source_target_pairs={{0,2},{1,3},{2,0},{3,1},{4,6},{5,7},{6,4},{7,5},{8,10},{9,11},{10,... | collective-permute-start | bytes 589832 | tf_op jit(solution)/shard_map/ppermute | solution.py:633
  60.4 6.2 %collective-permute-start.8 = (bf16[16,2,64,128]{3,2,1,0:T(8,128)(2,1)}, bf16[16,2,64,128]{3,2,1,0:T(8,128)(2,1)S(1)}, u32[]{:S(2)}, u32[]{:S(2)}) collective-permute-start(bf16[16,2,64,128]{3,2,1,0:T(8,128)(2,1)} %get-tuple-element.64), channel_id=1, source_target_pairs={{0,1},{1,0},{2,3},{3,2},{4,5},{5,4},{6,7},{7,6},{8,9},{9,8},{10,11... | collective-permute-start | bytes 1572872 | tf_op jit(solution)/shard_map/ppermute | solution.py:618
  62.7 18.4 %all-to-all-start.2 = ((bf16[8,6,32,128]{3,2,1,0:T(8,128)(2,1)}), bf16[8,6,32,128]{3,2,1,0:T(8,128)(2,1)S(1)}, u32[]{:S(2)}, u32[]{:S(2)}) async-start(bf16[8,6,32,128]{3,2,1,0:T(8,128)(2,1)} %get-tuple-element.53), calls=%async_computation.2 | async-start | bytes 786432 | tf_op jit(solution)/shard_map/all_to_all | solution.py:664
  66.7 1.0 %copy-start = (bf16[16,2,64,128]{3,2,1,0:T(8,128)(2,1)S(1)}, bf16[16,2,64,128]{3,2,1,0:T(8,128)(2,1)}, u32[]{:S(2)}) copy-start(bf16[16,2,64,128]{3,2,1,0:T(8,128)(2,1)} %get-tuple-element.63.keep_ref) | copy-start | bytes 1572868
  67.9 13.2 %collective-permute-start.9 = (bf16[16,2,32,128]{3,2,1,0:T(8,128)(2,1)S(1)}, bf16[16,2,32,128]{3,2,1,0:T(8,128)(2,1)S(1)}, u32[]{:S(2)}, u32[]{:S(2)}) collective-permute-start(bf16[16,2,32,128]{3,2,1,0:T(8,128)(2,1)S(1)} %get-tuple-element.66), channel_id=1, source_target_pairs={{0,2},{1,3},{2,0},{3,1},{4,6},{5,7},{6,4},{7,5},{8,10},{9,11},{10,... | collective-permute-start | bytes 786440 | tf_op jit(solution)/shard_map/ppermute | solution.py:629
  69.1 12.0 %collective-permute-start.6 = (bf16[2,32,128]{2,1,0:T(8,128)(2,1)S(1)}, bf16[2,32,128]{2,1,0:T(8,128)(2,1)S(1)}, u32[]{:S(2)}, u32[]{:S(2)}) collective-permute-start(bf16[2,32,128]{2,1,0:T(8,128)(2,1)S(1)} %get-tuple-element.61), channel_id=1, source_target_pairs={{0,4},{4,0},{8,12},{12,8},{16,20},{20,16},{24,28},{28,24},{1,5},{5... | collective-permute-start | bytes 49160 | tf_op jit(solution)/shard_map/ppermute | solution.py:665
  69.2 11.9 %collective-permute-start.7 = (bf16[2,32,128]{2,1,0:T(8,128)(2,1)S(1)}, bf16[2,32,128]{2,1,0:T(8,128)(2,1)S(1)}, u32[]{:S(2)}, u32[]{:S(2)}) collective-permute-start(bf16[2,32,128]{2,1,0:T(8,128)(2,1)S(1)} %get-tuple-element.62), channel_id=1, source_target_pairs={{4,8},{8,4},{12,16},{16,12},{20,24},{24,20},{5,9},{9,5},{13,17},{1... | collective-permute-start | bytes 49160 | tf_op jit(solution)/shard_map/ppermute | solution.py:666
  73.4 7.7 %copy-start.2 = (s32[2]{0:T(128)S(1)}, s32[2]{0:T(128)}, u32[]{:S(2)}) copy-start(s32[2]{0:T(128)} %global_blocks.5) | copy-start | bytes 28
  73.4 7.7 %copy-start.3 = (s32[8]{0:T(128)S(1)}, s32[8]{0:T(128)}, u32[]{:S(2)}) copy-start(s32[8]{0:T(128)} %get-tuple-element.59.requested) | copy-start | bytes 100
  82.0 6.0 %collective-permute-start.11 = (bf16[16,2,32,128]{3,2,1,0:T(8,128)(2,1)S(1)}, bf16[16,2,32,128]{3,2,1,0:T(8,128)(2,1)S(1)}, u32[]{:S(2)}, u32[]{:S(2)}) collective-permute-start(bf16[16,2,32,128]{3,2,1,0:T(8,128)(2,1)S(1)} %settle.1.refs_0_), channel_id=1, source_target_pairs={{0,2},{1,3},{2,0},{3,1},{4,6},{5,7},{6,4},{7,5},{8,10},{9,11},{10,... | collective-permute-start | bytes 786440 | tf_op jit(solution)/shard_map/ppermute | solution.py:678
  82.3 8.5 %collective-permute-start.10 = (bf16[16,2,32,128]{3,2,1,0:T(8,128)(2,1)S(1)}, bf16[16,2,32,128]{3,2,1,0:T(8,128)(2,1)S(1)}, u32[]{:S(2)}, u32[]{:S(2)}) collective-permute-start(bf16[16,2,32,128]{3,2,1,0:T(8,128)(2,1)S(1)} %settle.1.refs_0_), channel_id=1, source_target_pairs={{0,1},{1,0},{2,3},{3,2},{4,5},{5,4},{6,7},{7,6},{8,9},{9,8},{10,11... | collective-permute-start | bytes 786440 | tf_op jit(solution)/shard_map/ppermute | solution.py:681
  88.0 3.9 %collective-permute-start.12 = (bf16[16,2,32,128]{3,2,1,0:T(8,128)(2,1)S(1)}, bf16[16,2,32,128]{3,2,1,0:T(8,128)(2,1)S(1)}, u32[]{:S(2)}, u32[]{:S(2)}) collective-permute-start(bf16[16,2,32,128]{3,2,1,0:T(8,128)(2,1)S(1)} %collective-permute-done.11.refs_2_), channel_id=1, source_target_pairs={{0,1},{1,0},{2,3},{3,2},{4,5},{5,4},{6,7},{7,6},{8,9},{9,8},{10,11... | collective-permute-start | bytes 786440 | tf_op jit(solution)/shard_map/ppermute | solution.py:681
  (1 other events, 0.7 us)

commit v4 on v3

--- a/solution.py
+++ b/solution.py
@@ -318,17 +318,22 @@
         if old is not None:
             q2, g2, slots2 = heads(q_all, old), heads(g_all, old), slots_of(old)
         tops, ls, dd = [], [], []
+
+        def dots(i):
+            return mm(k_all[slots1[i]], q1, NT), mm(v_all[slots1[i]], g1, NT)
+
+        if new is not None:
+            ready = dots(0)
         for i in range(FAR):
             rows = slice(i * BLOCK, (i + 1) * BLOCK)
             if new is not None:
-                s = mm(k_all[slots1[i]], q1, NT)
-                dp = mm(v_all[slots1[i]], g1, NT)
+                s, dp = ready
+                if i + 1 < FAR:
+                    ready = dots(i + 1)
             if old is not None:
                 p = e_all[old_slot, rows] * stats[i]
                 ds = (p * (dp_all[old_slot, rows] - stats[FAR])).astype(jnp.bfloat16)
                 ds_all[old, rows] = ds
-                acc[slots2[i], 0] += mm(ds, q2, NN)
-                acc[slots2[i], 1] += mm(p.astype(jnp.bfloat16), g2, NN)
             if new is not None:
                 top = jnp.max(s, axis=0, keepdims=True) * SCALE
                 e = jnp.exp2(s * SCALE - top)
@@ -337,6 +342,9 @@
                 tops.append(top)
                 ls.append(fold(e))
                 dd.append(fold(e * dp))
+            if old is not None:
+                acc[slots2[i], 0] += mm(ds, q2, NN)
+                acc[slots2[i], 1] += mm(p.astype(jnp.bfloat16), g2, NN)
         if old is not None:
             put(old).start()
         if new is None:
@@ -357,13 +365,17 @@
         fd_ref[new, 2 * WINDOW : 2 * WINDOW + 1] = delta
         return tuple(w * inv for w in weight) + (delta,)
 
-    def pair(t, stats):
-        stats = work(2 * t + 1, 1, 2 * t, 0, stats)
-        return work(2 * t + 2, 0, 2 * t + 1, 1, stats)
+    turn = math.gcd(blocks, 4)
+
+    def several(t, stats, last=False):
+        for j in range(turn - last):
+            b = t * turn + j
+            stats = work(b + 1, (j + 1) % 2, b, j % 2, stats)
+        return stats
 
     stats = work(0, 0, None, None, None)
-    stats = lax.fori_loop(0, blocks // 2 - 1, pair, stats)
-    stats = work(blocks - 1, 1, blocks - 2, 0, stats)
+    stats = lax.fori_loop(0, blocks // turn - 1, several, stats)
+    stats = several(blocks // turn - 1, stats, True)
     work(None, None, blocks - 1, 1, stats)
 
     for slot, w, b, swap in ((peers + G, 0, 0, 1), (peers + G + 1, WINDOW - 1, blocks - 1, 0)):
@@ -430,8 +442,9 @@
 
 
 def queries_kernel(
-    owners, k_ref, low_ref, high_ref, mine_ref, other_ref, dsw_ref, dsf_ref, dq_ref, k_all, kt_all
+    first, owners, k_ref, low_ref, high_ref, mine_ref, other_ref, dsw_ref, dsf_ref, *refs
 ):
+    *_, dq_ref, k_all, kt_all = refs
     blocks = k_ref.shape[0] // BLOCK
     peers = mine_ref.shape[0]
     per = dsw_ref.shape[0]
@@ -462,7 +475,7 @@
         lax.fori_loop(0, first_global + G, turn, 0, unroll=4)
 
     for u in range(per):
-        b = step * per + u
+        b = first + step * per + u
         panels = [b + w for w in range(WINDOW)]
         panels += [first_random + owners[b * R + r] for r in range(R)]
         panels += [first_global + j for j in range(G)]
@@ -647,20 +660,31 @@
     )(*parts)
     parts_w = reduced(keep_w, send_w, "split_close", bf16)
     dsw, to_low = lax.optimization_barrier((dsw, to_low))
-    query_grad = pl.pallas_call(
-        queries_kernel,
-        out_shape=sds(query_vectors.shape, bf16),
-        grid_spec=pltpu.PrefetchScalarGridSpec(
-            num_scalar_prefetch=1,
-            grid=(steps,),
-            in_specs=[whole(a) for a in (key_vectors, low, high, mine, other)] + [near_spec, far_spec],
-            out_specs=rows_spec,
-            scratch_shapes=[pltpu.VMEM((blocks + 2 + seq_count + G, BLOCK, DH), bf16)] * 2,
-        ),
-        compiler_params=large,
-        cost_estimate=pl.CostEstimate(flops=LISTED * unit, bytes_accessed=8 * MIB, transcendentals=0),
-        name="queries",
-    )(owners, key_vectors, low, high, mine, other, dsw, dsf)
+
+    def queries(half, dsw, done):
+        shift = half * (steps // 2)
+        part = lambda *rest: pl.BlockSpec((per,) + rest, lambda i, *_: (i + shift,) + (0,) * len(rest))
+        return pl.pallas_call(
+            functools.partial(queries_kernel, shift * per),
+            out_shape=sds(query_vectors.shape, bf16),
+            grid_spec=pltpu.PrefetchScalarGridSpec(
+                num_scalar_prefetch=1,
+                grid=(steps // 2,),
+                in_specs=[whole(a) for a in (key_vectors, low, high, mine, other)]
+                + [part(WINDOW * BLOCK, lanes), part(FAR * BLOCK, lanes)]
+                + [hbm] * len(done),
+                out_specs=pl.BlockSpec((per * BLOCK, columns), lambda i, *_: (i + shift, 0)),
+                scratch_shapes=[pltpu.VMEM((blocks + 2 + seq_count + G, BLOCK, DH), bf16)] * 2,
+            ),
+            input_output_aliases={8: 0} if done else {},
+            compiler_params=large,
+            cost_estimate=pl.CostEstimate(
+                flops=LISTED * unit // 2, bytes_accessed=4 * MIB, transcendentals=0
+            ),
+            name="queries",
+        )(owners, key_vectors, low, high, mine, other, dsw, dsf, *done)
+
+    query_grad = queries(0, dsw, ())
     back = lax.all_to_all(terms, "seq", split_axis=0, concat_axis=0, tiled=True)
     from_low = lax.ppermute(to_low, "seq", low_pairs)
     from_high = lax.ppermute(to_high, "seq", high_pairs)
@@ -675,7 +699,10 @@
         name="settle",
     )(requested, global_blocks, back, from_low, from_high, *parts_w)
 
+    dsw, query_grad, held = lax.optimization_barrier((dsw, query_grad, held))
+    query_grad = queries(1, dsw, (query_grad,))
     rows = [held] + [lax.ppermute(held, "head", partners(head_count, m)) for m in others]
+    rows[-1], query_grad = lax.optimization_barrier((rows[-1], query_grad))
     pieces = []
     for a in rows:
         pieces += [a, lax.ppermute(a, "head", core_pairs)]

time: 94 us -> 91.2 us (0.970)
  waiting for transfers between devices: 9.6 us -> 6.02 us
  Pallas kernels: 42.5 us -> 45 us
  starting transfers between devices: 37.7 us -> 36 us
    ppermute x1, waiting for transfers between devices: 3.59 us -> 0.01 us  [body(): lax.ppermute(held, 'head', partners(head_count, m))]
    pallas_call x1 -> x2, Pallas kernels: 7.65 us -> 10.4 us  [queries(): pl.pallas_call(functools.partial(queries_kernel, shift * per), out_shape=...]
    ppermute x2, starting transfers between devices: 4.87 us -> 3.29 us  [body(): pieces += [a, lax.ppermute(a, 'head', core_pairs)]]
  transfers between devices with their start and end apart: 16 -> 16, of which waited for: 6 -> 5; matrix products, arithmetic and copies ran while one was open for 0% -> 0% of each run, Pallas kernels for 24% -> 27%
where the time goes in v4:
time: 91.2 us; the launch traced here: 90.3 us
  Pallas kernels  45 us (49%)
  starting transfers between devices  36 us (39%)
  waiting for transfers between devices  6.02 us (7%)
  local copies, waits for them, and re-layouts  2.44 us (3%)
    pallas_call x1, Pallas kernels, body(): pl.pallas_call(far_kernel, out_shape=(sds((blocks, FAR * BLOCK, lanes), b...  13.1 us
    pallas_call x2, Pallas kernels, queries(): pl.pallas_call(functools.partial(queries_kernel, shift * per), out_shape=...  10.4 us
    pallas_call x1, Pallas kernels, body(): pl.pallas_call(close_kernel, out_shape=(sds((blocks, WINDOW * BLOCK, lane...  8.03 us
    all_to_all x1, starting transfers between devices, body(): lax.all_to_all(asking, 'seq', split_axis=0, concat_axis=0, tiled=True)  5.79 us
    pallas_call x1, Pallas kernels, body(): pl.pallas_call(near_kernel, out_shape=sds((blocks, 2 * FOLD, lanes), f32)...  5.37 us
    all_to_all x1, starting transfers between devices, body(): lax.all_to_all(served, 'seq', split_axis=0, concat_axis=0, tiled=True)  5.37 us
    ppermute x1, starting transfers between devices, body(): other = lax.ppermute(mine, 'head', core_pairs)  4.81 us
    ppermute x1, starting transfers between devices, body(): high = lax.ppermute(to_high, 'seq', high_pairs)  4.23 us
  transfers between devices with their start and end apart: 16, of which 5 were waited for; matrix products, arithmetic and copies ran while one was open for 0% of the time, Pallas kernels for 27%

profile of v4, /device:TPU:5, one launch (start us, length us, event | category | flops | bytes accessed | tf_op | source)
XLA Modules:
  0.0 90.3 jit_solution(6059427850770604249)
XLA Ops:
  0.6 2.4 %ask.1 = (bf16[8,48,128]{2,1,0:T(8,128)(2,1)}, bf16[2,128,128]{2,1,0:T(8,128)(2,1)}, bf16[2,128,128]{2,1,0:T(8,128)(2,1)}, s32[48]{0:T(128)}) custom-call(s32[2]{0:T(128)} %global_blocks.5, s32[3,16]{1,0:T(4,128)} %bitcast.1, s32[3,16]{1,0:T(4,128)} %bitcast.2, bf16[2048,128]{1,0:T(8,128)(2,1)} %k_ref.11, bf16[2048,128]{1,0:T(8,128)(2,1)} %v_ref.7), custom_call_target="tpu_custom_call" | custom-call | tf_op jit(solution)/shard_map/ask/pallas_call | solution.py:529
  3.0 5.8 %all-to-all-start = ((bf16[8,48,128]{2,1,0:T(8,128)(2,1)}), bf16[8,48,128]{2,1,0:T(8,128)(2,1)S(1)}, u32[]{:S(2)}, u32[]{:S(2)}) async-start(bf16[8,48,128]{2,1,0:T(8,128)(2,1)} %get-tuple-element.41), calls=%async_computation | async-start | bytes 196608 | tf_op jit(solution)/shard_map/all_to_all | solution.py:546
  8.8 4.2 %collective-permute-start.1 = (bf16[2,128,128]{2,1,0:T(8,128)(2,1)}, bf16[2,128,128]{2,1,0:T(8,128)(2,1)S(1)}, u32[]{:S(2)}, u32[]{:S(2)}) collective-permute-start(bf16[2,128,128]{2,1,0:T(8,128)(2,1)} %get-tuple-element.43), channel_id=1, source_target_pairs={{4,8},{8,4},{12,16},{16,12},{20,24},{24,20},{5,9},{9,5},{13,17},{1... | collective-permute-start | bytes 196616 | tf_op jit(solution)/shard_map/ppermute | solution.py:551
  13.1 2.1 %collective-permute-done.1.high_ref = bf16[2,128,128]{2,1,0:T(8,128)(2,1)S(1)} collective-permute-done((bf16[2,128,128]{2,1,0:T(8,128)(2,1)}, bf16[2,128,128]{2,1,0:T(8,128)(2,1)S(1)}, u32[]{:S(2)}, u32[]{:S(2)}) %collective-permute-start.1) | collective-permute-done | bytes 65568 | tf_op jit(solution)/shard_map/ppermute | solution.py:551
  15.9 2.9 %serve.1 = (bf16[8,160,128]{2,1,0:T(8,128)(2,1)}, s32[8]{0:T(128)}) custom-call(s32[2]{0:T(128)} %global_blocks.5, bf16[8,48,128]{2,1,0:T(8,128)(2,1)} %copy-done.8, bf16[2048,128]{1,0:T(8,128)(2,1)} %k_ref.11, bf16[2048,128]{1,0:T(8,128)(2,1)} %v_ref.7), custom_call_target="tpu_custom_call" | custom-call | tf_op jit(solution)/shard_map/serve/pallas_call | solution.py:554
  18.8 5.4 %all-to-all-start.1 = ((bf16[8,160,128]{2,1,0:T(8,128)(2,1)}), bf16[8,160,128]{2,1,0:T(8,128)(2,1)S(1)}, u32[]{:S(2)}, u32[]{:S(2)}) async-start(bf16[8,160,128]{2,1,0:T(8,128)(2,1)} %get-tuple-element.48), calls=%async_computation.1 | async-start | bytes 655360 | tf_op jit(solution)/shard_map/all_to_all | solution.py:563
  24.1 5.4 %near.1.st_ref = f32[16,16,256]{2,1,0:T(8,128)} custom-call(bf16[2048,256]{1,0:T(8,128)(2,1)} %q_ref.5, bf16[2048,256]{1,0:T(8,128)(2,1)} %g_ref.5, bf16[2048,128]{1,0:T(8,128)(2,1)} %k_ref.11, bf16[2048,128]{1,0:T(8,128)(2,1)} %v_ref.7, bf16[2,128,128]{2,1,0:T(8,128)(2,1)} %copy-done.6, bf16[2,128,128]{2,1,0:T(8,128)(2,1)} %copy-done.7), custom_call_target="tpu_custom_call" | custom-call | flops 805306368 | bytes 4194304 | tf_op jit(solution)/shard_map/near/pallas_call | solution.py:570
  30.3 4.8 %collective-permute-start.2 = (bf16[8,160,128]{2,1,0:T(8,128)(2,1)S(1)}, bf16[8,160,128]{2,1,0:T(8,128)(2,1)S(1)}, u32[]{:S(2)}, u32[]{:S(2)}) collective-permute-start(bf16[8,160,128]{2,1,0:T(8,128)(2,1)S(1)} %all-to-all-done.1.mine_ref), channel_id=1, source_target_pairs={{0,1},{1,0},{2,3},{3,2},{4,5},{5,4},{6,7},{7,6},{8,9},{9,8},{10,11... | collective-permute-start | bytes 983048 | tf_op jit(solution)/shard_map/ppermute | solution.py:584
  35.1 1.3 %collective-permute-done.2.other_ref = bf16[8,160,128]{2,1,0:T(8,128)(2,1)S(1)} collective-permute-done((bf16[8,160,128]{2,1,0:T(8,128)(2,1)S(1)}, bf16[8,160,128]{2,1,0:T(8,128)(2,1)S(1)}, u32[]{:S(2)}, u32[]{:S(2)}) %collective-permute-start.2) | collective-permute-done | bytes 327712 | tf_op jit(solution)/shard_map/ppermute | solution.py:584
  37.1 13.1 %far.1 = (bf16[16,640,256]{2,1,0:T(8,128)(2,1)}, f32[16,8,256]{2,1,0:T(8,128)}, bf16[12,2,32,128]{3,2,1,0:T(8,128)(2,1)}, bf16[12,2,32,128]{3,2,1,0:T(8,128)(2,1...) custom-call(s32[48]{0:T(128)} %get-tuple-element.46.owners, bf16[2048,256]{1,0:T(8,128)(2,1)} %q_ref.5, ...), custom_call_target="tpu_custom_call" | custom-call | flops 3355443200 | bytes 8388608 | tf_op jit(solution)/shard_map/far/pallas_call | solution.py:588
  50.2 1.5 %collective-permute-start.5 = (bf16[12,2,32,128]{3,2,1,0:T(8,128)(2,1)}, bf16[12,2,32,128]{3,2,1,0:T(8,128)(2,1)S(1)}, u32[]{:S(2)}, u32[]{:S(2)}) collective-permute-start(bf16[12,2,32,128]{3,2,1,0:T(8,128)(2,1)} %get-tuple-element.56), channel_id=1, source_target_pairs={{0,3},{1,2},{2,1},{3,0},{4,7},{5,6},{6,5},{7,4},{8,11},{9,10},{10,... | collective-permute-start | bytes 589832 | tf_op jit(solution)/shard_map/ppermute | solution.py:646
  52.1 8.0 %close.1 = (bf16[16,384,256]{2,1,0:T(8,128)(2,1)}, bf16[16,2,64,128]{3,2,1,0:T(8,128)(2,1)}, bf16[16,2,64,128]{3,2,1,0:T(8,128)(2,1)}) custom-call(bf16[2048,256]{1,0:T(8,128)(2,1)} %q_ref.5, bf16[2048,256]{1,0:T(8,128)(2,1)} %g_ref.5, bf16[2048,128]{1,0:T(8,128)(2,1)} %k_ref.11, bf16[2048,128]{1,0:T(8,128)(2,1)} %v_ref.7, bf16[2,128,128]{2,1,0:T(8,128)(2,1)} %copy-done.6, ...), custom_call_target="tpu_custom_call" | custom-call | flops 1610612736 | bytes 8388608 | tf_op jit(solution)/shard_map/close/pallas_call | solution.py:616
  61.6 0.9 terms.1
  62.4 4.0 %all-to-all-start.2 = ((bf16[8,6,32,128]{3,2,1,0:T(8,128)(2,1)}), bf16[8,6,32,128]{3,2,1,0:T(8,128)(2,1)S(1)}, u32[]{:S(2)}, u32[]{:S(2)}) async-start(bf16[8,6,32,128]{3,2,1,0:T(8,128)(2,1)} %get-tuple-element.61), calls=%async_computation.2 | async-start | bytes 786432 | tf_op jit(solution)/shard_map/all_to_all | solution.py:688
  66.4 1.0 %copy-done = bf16[16,2,64,128]{3,2,1,0:T(8,128)(2,1)S(1)} copy-done((bf16[16,2,64,128]{3,2,1,0:T(8,128)(2,1)S(1)}, bf16[16,2,64,128]{3,2,1,0:T(8,128)(2,1)}, u32[]{:S(2)}) %copy-start) | copy-done | bytes 524312
  67.6 1.3 %collective-permute-start.9 = (bf16[16,2,32,128]{3,2,1,0:T(8,128)(2,1)S(1)}, bf16[16,2,32,128]{3,2,1,0:T(8,128)(2,1)S(1)}, u32[]{:S(2)}, u32[]{:S(2)}) collective-permute-start(bf16[16,2,32,128]{3,2,1,0:T(8,128)(2,1)S(1)} %get-tuple-element.71), channel_id=1, source_target_pairs={{0,2},{1,3},{2,0},{3,1},{4,6},{5,7},{6,4},{7,5},{8,10},{9,11},{10,... | collective-permute-start | bytes 786440 | tf_op jit(solution)/shard_map/ppermute | solution.py:642
  69.0 4.2 %collective-permute-start.7 = (bf16[2,32,128]{2,1,0:T(8,128)(2,1)S(1)}, bf16[2,32,128]{2,1,0:T(8,128)(2,1)S(1)}, u32[]{:S(2)}, u32[]{:S(2)}) collective-permute-start(bf16[2,32,128]{2,1,0:T(8,128)(2,1)S(1)} %get-tuple-element.67), channel_id=1, source_target_pairs={{4,8},{8,4},{12,16},{16,12},{20,24},{24,20},{5,9},{9,5},{13,17},{1... | collective-permute-start | bytes 49160 | tf_op jit(solution)/shard_map/ppermute | solution.py:690
  73.2 5.2 %queries.2.refs_0_ = bf16[2048,256]{1,0:T(8,128)(2,1)} custom-call(s32[48]{0:T(128)} %get-tuple-element.46.owners, bf16[2048,128]{1,0:T(8,128)(2,1)} %k_ref.11, bf16[2,128,128]{2,1,0:T(8,128)(2,1)} %copy-done.6, bf16[2,128,128]{2,1,0:T(8,128)(2,1)} %copy-done.7, bf16[8,160,128]{2,1,0:T(8,128)(2,1)} %copy-done.4, bf16[8,160,128]{2,1,0:T(8,128)(2,1)} %copy-done.5, ...), custom_call_target="tpu_custom_call" | custom-call | flops 536870912 | bytes 4194304 | tf_op jit(solution)/shard_map/queries/pallas_call | solution.py:667
  78.4 0.8 settle.1.refs_0_
  79.5 2.1 %collective-permute-start.11 = (bf16[16,2,32,128]{3,2,1,0:T(8,128)(2,1)S(1)}, bf16[16,2,32,128]{3,2,1,0:T(8,128)(2,1)S(1)}, u32[]{:S(2)}, u32[]{:S(2)}) collective-permute-start(bf16[16,2,32,128]{3,2,1,0:T(8,128)(2,1)S(1)} %settle.1.refs_0_), channel_id=1, source_target_pairs={{0,1},{1,0},{2,3},{3,2},{4,5},{5,4},{6,7},{7,6},{8,9},{9,8},{10,11... | collective-permute-start | bytes 786440 | tf_op jit(solution)/shard_map/ppermute | solution.py:708
  81.7 5.2 %queries.3 = bf16[2048,256]{1,0:T(8,128)(2,1)} custom-call(s32[48]{0:T(128)} %get-tuple-element.46.owners, bf16[2048,128]{1,0:T(8,128)(2,1)} %k_ref.11, bf16[2,128,128]{2,1,0:T(8,128)(2,1)} %copy-done.6, bf16[2,128,128]{2,1,0:T(8,128)(2,1)} %copy-done.7, bf16[8,160,128]{2,1,0:T(8,128)(2,1)} %copy-done.4, ...), custom_call_target="tpu_custom_call", output_to_operand_aliasing={{}: (8, {})} | custom-call | flops 536870912 | bytes 4194304 | tf_op jit(solution)/shard_map/queries/pallas_call | solution.py:667
  86.8 1.2 %collective-permute-start.12 = (bf16[16,2,32,128]{3,2,1,0:T(8,128)(2,1)S(1)}, bf16[16,2,32,128]{3,2,1,0:T(8,128)(2,1)S(1)}, u32[]{:S(2)}, u32[]{:S(2)}) collective-permute-start(bf16[16,2,32,128]{3,2,1,0:T(8,128)(2,1)S(1)} %collective-permute-done.10.refs_2_), channel_id=1, source_target_pairs={{0,1},{1,0},{2,3},{3,2},{4,5},{5,4},{6,7},{7,6},{8,9},{9,8},{10,11... | collective-permute-start | bytes 786440 | tf_op jit(solution)/shard_map/ppermute | solution.py:708
  88.0 1.2 %collective-permute-done.12.refs_3_ = bf16[16,2,32,128]{3,2,1,0:T(8,128)(2,1)S(1)} collective-permute-done((bf16[16,2,32,128]{3,2,1,0:T(8,128)(2,1)S(1)}, bf16[16,2,32,128]{3,2,1,0:T(8,128)(2,1)S(1)}, u32[]{:S(2)}, u32[]{:S(2)}) %collective-permute-start.12) | collective-permute-done | bytes 262176 | tf_op jit(solution)/shard_map/ppermute | solution.py:708
  89.2 1.1 %join.1 = (bf16[2048,128]{1,0:T(8,128)(2,1)}, bf16[2048,128]{1,0:T(8,128)(2,1)}) custom-call(bf16[16,2,32,128]{3,2,1,0:T(8,128)(2,1)S(1)} %settle.1.refs_0_, bf16[16,2,32,128]{3,2,1,0:T(8,128)(2,1)S(1)} %collective-permute-done.11.refs_1_, bf16[16,2,32,128]{3,2,1,0:T(8,128)(2,1)S(1)} %collective-permute-done.10.refs_2_, ...), custom_call_target="tpu_custom_call" | custom-call | tf_op jit(solution)/shard_map/join/pallas_call | solution.py:709
  (37 shorter events, 4.6 us)
Async XLA Ops:
  3.0 12.2 %all-to-all-start = ((bf16[8,48,128]{2,1,0:T(8,128)(2,1)}), bf16[8,48,128]{2,1,0:T(8,128)(2,1)S(1)}, u32[]{:S(2)}, u32[]{:S(2)}) async-start(bf16[8,48,128]{2,1,0:T(8,128)(2,1)} %get-tuple-element.41), calls=%async_computation | async-start | bytes 196608 | tf_op jit(solution)/shard_map/all_to_all | solution.py:546
  8.8 4.3 %collective-permute-start = (bf16[2,128,128]{2,1,0:T(8,128)(2,1)}, bf16[2,128,128]{2,1,0:T(8,128)(2,1)S(1)}, u32[]{:S(2)}, u32[]{:S(2)}) collective-permute-start(bf16[2,128,128]{2,1,0:T(8,128)(2,1)} %get-tuple-element.42), channel_id=1, source_target_pairs={{0,4},{4,0},{8,12},{12,8},{16,20},{20,16},{24,28},{28,24},{1,5},{5... | collective-permute-start | bytes 196616 | tf_op jit(solution)/shard_map/ppermute | solution.py:550
  8.8 6.4 %collective-permute-start.1 = (bf16[2,128,128]{2,1,0:T(8,128)(2,1)}, bf16[2,128,128]{2,1,0:T(8,128)(2,1)S(1)}, u32[]{:S(2)}, u32[]{:S(2)}) collective-permute-start(bf16[2,128,128]{2,1,0:T(8,128)(2,1)} %get-tuple-element.43), channel_id=1, source_target_pairs={{4,8},{8,4},{12,16},{16,12},{20,24},{24,20},{5,9},{9,5},{13,17},{1... | collective-permute-start | bytes 196616 | tf_op jit(solution)/shard_map/ppermute | solution.py:551
  13.1 11.0 %copy-start.6 = (bf16[2,128,128]{2,1,0:T(8,128)(2,1)}, bf16[2,128,128]{2,1,0:T(8,128)(2,1)S(1)}, u32[]{:S(2)}) copy-start(bf16[2,128,128]{2,1,0:T(8,128)(2,1)S(1)} %collective-permute-done.low_ref) | copy-start | bytes 196612
  15.2 8.9 %copy-start.7 = (bf16[2,128,128]{2,1,0:T(8,128)(2,1)}, bf16[2,128,128]{2,1,0:T(8,128)(2,1)S(1)}, u32[]{:S(2)}) copy-start(bf16[2,128,128]{2,1,0:T(8,128)(2,1)S(1)} %collective-permute-done.1.high_ref) | copy-start | bytes 196612
  18.8 11.5 %all-to-all-start.1 = ((bf16[8,160,128]{2,1,0:T(8,128)(2,1)}), bf16[8,160,128]{2,1,0:T(8,128)(2,1)S(1)}, u32[]{:S(2)}, u32[]{:S(2)}) async-start(bf16[8,160,128]{2,1,0:T(8,128)(2,1)} %get-tuple-element.48), calls=%async_computation.1 | async-start | bytes 655360 | tf_op jit(solution)/shard_map/all_to_all | solution.py:563
  30.3 6.1 %copy-start.4 = (bf16[8,160,128]{2,1,0:T(8,128)(2,1)}, bf16[8,160,128]{2,1,0:T(8,128)(2,1)S(1)}, u32[]{:S(2)}) copy-start(bf16[8,160,128]{2,1,0:T(8,128)(2,1)S(1)} %all-to-all-done.1.mine_ref) | copy-start | bytes 983044
  30.3 6.1 %collective-permute-start.2 = (bf16[8,160,128]{2,1,0:T(8,128)(2,1)S(1)}, bf16[8,160,128]{2,1,0:T(8,128)(2,1)S(1)}, u32[]{:S(2)}, u32[]{:S(2)}) collective-permute-start(bf16[8,160,128]{2,1,0:T(8,128)(2,1)S(1)} %all-to-all-done.1.mine_ref), channel_id=1, source_target_pairs={{0,1},{1,0},{2,3},{3,2},{4,5},{5,4},{6,7},{7,6},{8,9},{9,8},{10,11... | collective-permute-start | bytes 983048 | tf_op jit(solution)/shard_map/ppermute | solution.py:584
  36.4 0.7 copy-start.5
  50.2 11.4 %copy-start.1 = (bf16[12,2,32,128]{3,2,1,0:T(8,128)(2,1)S(1)}, bf16[12,2,32,128]{3,2,1,0:T(8,128)(2,1)}, u32[]{:S(2)}) copy-start(bf16[12,2,32,128]{3,2,1,0:T(8,128)(2,1)} %get-tuple-element.53.keep_ref) | copy-start | bytes 589828
  50.2 10.0 %collective-permute-start.5 = (bf16[12,2,32,128]{3,2,1,0:T(8,128)(2,1)}, bf16[12,2,32,128]{3,2,1,0:T(8,128)(2,1)S(1)}, u32[]{:S(2)}, u32[]{:S(2)}) collective-permute-start(bf16[12,2,32,128]{3,2,1,0:T(8,128)(2,1)} %get-tuple-element.56), channel_id=1, source_target_pairs={{0,3},{1,2},{2,1},{3,0},{4,7},{5,6},{6,5},{7,4},{8,11},{9,10},{10,... | collective-permute-start | bytes 589832 | tf_op jit(solution)/shard_map/ppermute | solution.py:646
  51.7 9.2 %collective-permute-start.3 = (bf16[12,2,32,128]{3,2,1,0:T(8,128)(2,1)}, bf16[12,2,32,128]{3,2,1,0:T(8,128)(2,1)S(1)}, u32[]{:S(2)}, u32[]{:S(2)}) collective-permute-start(bf16[12,2,32,128]{3,2,1,0:T(8,128)(2,1)} %get-tuple-element.54), channel_id=1, source_target_pairs={{0,1},{1,0},{2,3},{3,2},{4,5},{5,4},{6,7},{7,6},{8,9},{9,8},{10,11... | collective-permute-start | bytes 589832 | tf_op jit(solution)/shard_map/ppermute | solution.py:646
  51.9 9.7 %collective-permute-start.4 = (bf16[12,2,32,128]{3,2,1,0:T(8,128)(2,1)}, bf16[12,2,32,128]{3,2,1,0:T(8,128)(2,1)S(1)}, u32[]{:S(2)}, u32[]{:S(2)}) collective-permute-start(bf16[12,2,32,128]{3,2,1,0:T(8,128)(2,1)} %get-tuple-element.55), channel_id=1, source_target_pairs={{0,2},{1,3},{2,0},{3,1},{4,6},{5,7},{6,4},{7,5},{8,10},{9,11},{10,... | collective-permute-start | bytes 589832 | tf_op jit(solution)/shard_map/ppermute | solution.py:646
  60.2 6.3 %collective-permute-start.8 = (bf16[16,2,64,128]{3,2,1,0:T(8,128)(2,1)}, bf16[16,2,64,128]{3,2,1,0:T(8,128)(2,1)S(1)}, u32[]{:S(2)}, u32[]{:S(2)}) collective-permute-start(bf16[16,2,64,128]{3,2,1,0:T(8,128)(2,1)} %get-tuple-element.69), channel_id=1, source_target_pairs={{0,1},{1,0},{2,3},{3,2},{4,5},{5,4},{6,7},{7,6},{8,9},{9,8},{10,11... | collective-permute-start | bytes 1572872 | tf_op jit(solution)/shard_map/ppermute | solution.py:631
  62.4 15.9 %all-to-all-start.2 = ((bf16[8,6,32,128]{3,2,1,0:T(8,128)(2,1)}), bf16[8,6,32,128]{3,2,1,0:T(8,128)(2,1)S(1)}, u32[]{:S(2)}, u32[]{:S(2)}) async-start(bf16[8,6,32,128]{3,2,1,0:T(8,128)(2,1)} %get-tuple-element.61), calls=%async_computation.2 | async-start | bytes 786432 | tf_op jit(solution)/shard_map/all_to_all | solution.py:688
  66.4 1.0 %copy-start = (bf16[16,2,64,128]{3,2,1,0:T(8,128)(2,1)S(1)}, bf16[16,2,64,128]{3,2,1,0:T(8,128)(2,1)}, u32[]{:S(2)}) copy-start(bf16[16,2,64,128]{3,2,1,0:T(8,128)(2,1)} %get-tuple-element.68.keep_ref) | copy-start | bytes 1572868
  67.6 10.8 %collective-permute-start.9 = (bf16[16,2,32,128]{3,2,1,0:T(8,128)(2,1)S(1)}, bf16[16,2,32,128]{3,2,1,0:T(8,128)(2,1)S(1)}, u32[]{:S(2)}, u32[]{:S(2)}) collective-permute-start(bf16[16,2,32,128]{3,2,1,0:T(8,128)(2,1)S(1)} %get-tuple-element.71), channel_id=1, source_target_pairs={{0,2},{1,3},{2,0},{3,1},{4,6},{5,7},{6,4},{7,5},{8,10},{9,11},{10,... | collective-permute-start | bytes 786440 | tf_op jit(solution)/shard_map/ppermute | solution.py:642
  68.9 9.5 %collective-permute-start.6 = (bf16[2,32,128]{2,1,0:T(8,128)(2,1)S(1)}, bf16[2,32,128]{2,1,0:T(8,128)(2,1)S(1)}, u32[]{:S(2)}, u32[]{:S(2)}) collective-permute-start(bf16[2,32,128]{2,1,0:T(8,128)(2,1)S(1)} %get-tuple-element.66), channel_id=1, source_target_pairs={{0,4},{4,0},{8,12},{12,8},{16,20},{20,16},{24,28},{28,24},{1,5},{5... | collective-permute-start | bytes 49160 | tf_op jit(solution)/shard_map/ppermute | solution.py:689
  69.0 9.4 %collective-permute-start.7 = (bf16[2,32,128]{2,1,0:T(8,128)(2,1)S(1)}, bf16[2,32,128]{2,1,0:T(8,128)(2,1)S(1)}, u32[]{:S(2)}, u32[]{:S(2)}) collective-permute-start(bf16[2,32,128]{2,1,0:T(8,128)(2,1)S(1)} %get-tuple-element.67), channel_id=1, source_target_pairs={{4,8},{8,4},{12,16},{16,12},{20,24},{24,20},{5,9},{9,5},{13,17},{1... | collective-permute-start | bytes 49160 | tf_op jit(solution)/shard_map/ppermute | solution.py:690
  73.2 5.2 %copy-start.2 = (s32[2]{0:T(128)S(1)}, s32[2]{0:T(128)}, u32[]{:S(2)}) copy-start(s32[2]{0:T(128)} %global_blocks.5) | copy-start | bytes 28
  73.2 5.2 %copy-start.3 = (s32[8]{0:T(128)S(1)}, s32[8]{0:T(128)}, u32[]{:S(2)}) copy-start(s32[8]{0:T(128)} %get-tuple-element.64.requested) | copy-start | bytes 100
  79.2 7.6 %collective-permute-start.10 = (bf16[16,2,32,128]{3,2,1,0:T(8,128)(2,1)S(1)}, bf16[16,2,32,128]{3,2,1,0:T(8,128)(2,1)S(1)}, u32[]{:S(2)}, u32[]{:S(2)}) collective-permute-start(bf16[16,2,32,128]{3,2,1,0:T(8,128)(2,1)S(1)} %settle.1.refs_0_), channel_id=1, source_target_pairs={{0,2},{1,3},{2,0},{3,1},{4,6},{5,7},{6,4},{7,5},{8,10},{9,11},{10,... | collective-permute-start | bytes 786440 | tf_op jit(solution)/shard_map/ppermute | solution.py:704
  79.5 8.5 %collective-permute-start.11 = (bf16[16,2,32,128]{3,2,1,0:T(8,128)(2,1)S(1)}, bf16[16,2,32,128]{3,2,1,0:T(8,128)(2,1)S(1)}, u32[]{:S(2)}, u32[]{:S(2)}) collective-permute-start(bf16[16,2,32,128]{3,2,1,0:T(8,128)(2,1)S(1)} %settle.1.refs_0_), channel_id=1, source_target_pairs={{0,1},{1,0},{2,3},{3,2},{4,5},{5,4},{6,7},{7,6},{8,9},{9,8},{10,11... | collective-permute-start | bytes 786440 | tf_op jit(solution)/shard_map/ppermute | solution.py:708
  86.8 2.3 %collective-permute-start.12 = (bf16[16,2,32,128]{3,2,1,0:T(8,128)(2,1)S(1)}, bf16[16,2,32,128]{3,2,1,0:T(8,128)(2,1)S(1)}, u32[]{:S(2)}, u32[]{:S(2)}) collective-permute-start(bf16[16,2,32,128]{3,2,1,0:T(8,128)(2,1)S(1)} %collective-permute-done.10.refs_2_), channel_id=1, source_target_pairs={{0,1},{1,0},{2,3},{3,2},{4,5},{5,4},{6,7},{7,6},{8,9},{9,8},{10,11... | collective-permute-start | bytes 786440 | tf_op jit(solution)/shard_map/ppermute | solution.py:708
  (1 other events, 0.7 us)

commit v5 on v4

--- a/solution.py
+++ b/solution.py
@@ -21,6 +21,7 @@
 FACTOR = float(DH) ** -0.5
 SCALE = FACTOR * math.log2(math.e)
 FOLD = 8
+SPARE = 9
 MARKS = 16
 
 NT = (((1,), (1,)), ((), ()))
@@ -269,7 +270,7 @@
     owners, q_ref, g_ref, mine_ref, other_ref, st_ref, low_ref, high_ref,
     ds_ref, fd_ref, *refs,
 ):
-    *share_refs, q_all, g_all, k_all, v_all, acc, e_all, dp_all, ds_all, in_sems, out_sems = refs
+    *share_refs, k_all, v_all, acc, e_all, dp_all, ds_all, out_sems = refs
     blocks = q_ref.shape[0] // BLOCK
     peers = mine_ref.shape[0]
     core, column = places()
@@ -279,16 +280,9 @@
     def at(b):
         return pl.ds(pl.multiple_of(b * BLOCK, BLOCK), BLOCK)
 
-    def fetch(b, which):
-        src, dst = ((q_ref, q_all), (g_ref, g_all))[which]
-        return pltpu.make_async_copy(src.at[at(b), :], dst.at[at(b), :], in_sems.at[b, which])
-
     def put(b):
         return pltpu.make_async_copy(ds_all.at[b], ds_ref.at[b], out_sems.at[b])
 
-    for b in range(blocks):
-        fetch(b, 0).start()
-        fetch(b, 1).start()
     for to, which in ((k_all, 0), (v_all, 1)):
         rows = slice(which * HALF, (which + 1) * HALF)
         to[:peers, own, :] = mine_ref[:, rows, :]
@@ -312,11 +306,9 @@
 
     def work(new, new_slot, old, old_slot, stats):
         if new is not None:
-            fetch(new, 0).wait()
-            fetch(new, 1).wait()
-            q1, g1, slots1 = heads(q_all, new), heads(g_all, new), slots_of(new)
+            q1, g1, slots1 = heads(q_ref, new), heads(g_ref, new), slots_of(new)
         if old is not None:
-            q2, g2, slots2 = heads(q_all, old), heads(g_all, old), slots_of(old)
+            q2, g2, slots2 = heads(q_ref, old), heads(g_ref, old), slots_of(old)
         tops, ls, dd = [], [], []
 
         def dots(i):
@@ -380,7 +372,7 @@
 
     for slot, w, b, swap in ((peers + G, 0, 0, 1), (peers + G + 1, WINDOW - 1, blocks - 1, 0)):
         odd = lax.rem(lax.axis_index("seq"), 2) == swap
-        q, g = heads(q_all, b), heads(g_all, b)
+        q, g = heads(q_ref, b), heads(g_ref, b)
         s = mm(jnp.where(odd, low_ref[0], high_ref[0]), q, NT)
         dp = mm(jnp.where(odd, low_ref[1], high_ref[1]), g, NT)
         p = jnp.exp2(s * SCALE - jnp.max(s, axis=0, keepdims=True) * SCALE)
@@ -574,13 +566,17 @@
         in_specs=[rows_spec, rows_spec] + [whole(a) for a in nearby],
         out_specs=st_spec,
         scratch_shapes=window_scratch,
-        compiler_params=large,
+        compiler_params=params,
         cost_estimate=pl.CostEstimate(
             flops=2 * WINDOW * unit, bytes_accessed=4 * MIB, transcendentals=blocks * lanes * WINDOW * BLOCK
         ),
         name="near",
     )(query_vectors, output_grad, *nearby)
     mine, st = lax.optimization_barrier((mine, st))
+    queries_in, grads_in, mine = lax.optimization_barrier((query_vectors, output_grad, mine))
+    here = lax.axis_index("seq") < seq_count
+    queries_in = jnp.where(here, queries_in, 0).astype(bf16)
+    grads_in = jnp.where(here, grads_in, 0).astype(bf16)
     other = lax.ppermute(mine, "head", core_pairs)
 
     slots = seq_count + G + 2
@@ -588,27 +584,25 @@
     dsf, fd, *pieces = pl.pallas_call(
         far_kernel,
         out_shape=(
-            sds((blocks, FAR * BLOCK, lanes), bf16),
+            sds((blocks * SPARE, FAR * BLOCK, lanes), bf16),
             sds((blocks, FOLD, lanes), f32),
         )
         + (sds(piece, bf16),) * head_count,
-        in_specs=[smem, hbm, hbm] + [vmem] * 5,
+        in_specs=[smem] + [vmem] * 7,
         out_specs=(hbm, vmem) + (vmem,) * head_count,
-        scratch_shapes=[pltpu.VMEM(query_vectors.shape, bf16)] * 2
-        + [pltpu.VMEM((seq_count + G, BLOCK, DH), bf16)] * 2
+        scratch_shapes=[pltpu.VMEM((seq_count + G, BLOCK, DH), bf16)] * 2
         + [pltpu.VMEM((slots, 2, BLOCK, DH), f32)]
         + [pltpu.VMEM((2, FAR * BLOCK, lanes), f32)] * 2
         + [
             pltpu.VMEM((blocks, FAR * BLOCK, lanes), bf16),
-            pltpu.SemaphoreType.DMA((blocks, 2)),
             pltpu.SemaphoreType.DMA((blocks,)),
         ],
-        compiler_params=large,
+        compiler_params=small,
         cost_estimate=pl.CostEstimate(
             flops=5 * FAR * unit, bytes_accessed=8 * MIB, transcendentals=blocks * lanes * FAR * BLOCK
         ),
         name="far",
-    )(owners, query_vectors, output_grad, mine, other, st, low, high)
+    )(owners, queries_in, grads_in, mine, other, st, low, high)
 
     piece_w = (blocks, 2, HALF, DH)
     near_spec = per_block(per, WINDOW * BLOCK, lanes)

time: 91.2 us -> 90.3 us (level)
  local copies, waits for them, and re-layouts: 2.44 us -> 7.56 us
  Pallas kernels: 45 us -> 40.1 us
  waiting for transfers between devices: 6.02 us -> 3.56 us
  other arithmetic: 0 us -> 1.68 us
    unnamed x18 -> x28, local copies, waits for them, and re-layouts: 2.44 us -> 7.56 us
    pallas_call x1, Pallas kernels: 13.1 us -> 10.3 us  [body(): pl.pallas_call(far_kernel, out_shape=(sds((blocks * SPARE, FAR * BLOCK, l...]
    pallas_call x1, Pallas kernels: 5.37 us -> 3.08 us  [body(): pl.pallas_call(near_kernel, out_shape=sds((blocks, 2 * FOLD, lanes), f32)...]
    select_n x0 -> x1, other arithmetic: none -> 1.68 us  [body(): grads_in = jnp.where(here, grads_in, 0).astype(bf16)]
    ppermute x1, starting transfers between devices: 4.81 us -> 3.33 us  [body(): other = lax.ppermute(mine, 'head', core_pairs)]
    ppermute x1, waiting for transfers between devices: 1.26 us -> 0.01 us  [body(): other = lax.ppermute(mine, 'head', core_pairs)]
    all_to_all x1, starting transfers between devices: 4 us -> 5.2 us  [body(): back = lax.all_to_all(terms, 'seq', split_axis=0, concat_axis=0, tiled=True)]
  transfers between devices with their start and end apart: 16 -> 16, of which waited for: 5 -> 3; matrix products, arithmetic and copies ran while one was open for 0% -> 2% of each run, Pallas kernels for 27% -> 25%
where the time goes in v5:
time: 90.3 us; the launch traced here: 89.2 us
  Pallas kernels  40.1 us (44%)
  starting transfers between devices  35.5 us (39%)
  local copies, waits for them, and re-layouts  7.56 us (8%)
  waiting for transfers between devices  3.56 us (4%)
  other arithmetic  1.68 us (2%)
    pallas_call x2, Pallas kernels, queries(): pl.pallas_call(functools.partial(queries_kernel, shift * per), out_shape=...  10.4 us
    pallas_call x1, Pallas kernels, body(): pl.pallas_call(far_kernel, out_shape=(sds((blocks * SPARE, FAR * BLOCK, l...  10.3 us
    pallas_call x1, Pallas kernels, body(): pl.pallas_call(close_kernel, out_shape=(sds((blocks, WINDOW * BLOCK, lane...  8.09 us
    unnamed x28, local copies, waits for them, and re-layouts  7.56 us
    all_to_all x1, starting transfers between devices, body(): lax.all_to_all(asking, 'seq', split_axis=0, concat_axis=0, tiled=True)  5.79 us
    all_to_all x1, starting transfers between devices, body(): lax.all_to_all(served, 'seq', split_axis=0, concat_axis=0, tiled=True)  5.42 us
    all_to_all x1, starting transfers between devices, body(): back = lax.all_to_all(terms, 'seq', split_axis=0, concat_axis=0, tiled=True)  5.2 us
    ppermute x1, starting transfers between devices, body(): from_high = lax.ppermute(to_high, 'seq', high_pairs)  4.25 us
  transfers between devices with their start and end apart: 16, of which 3 were waited for; matrix products, arithmetic and copies ran while one was open for 2% of the time, Pallas kernels for 25%

profile of v5, /device:TPU:5, one launch (start us, length us, event | category | flops | bytes accessed | tf_op | source)
XLA Modules:
  0.0 89.2 jit_solution(355945204017566425)
XLA Ops:
  0.6 2.5 %ask.1 = (bf16[8,48,128]{2,1,0:T(8,128)(2,1)}, bf16[2,128,128]{2,1,0:T(8,128)(2,1)}, bf16[2,128,128]{2,1,0:T(8,128)(2,1)}, s32[48]{0:T(128)}) custom-call(s32[2]{0:T(128)} %global_blocks.5, s32[3,16]{1,0:T(4,128)} %bitcast.1, s32[3,16]{1,0:T(4,128)} %bitcast.2, bf16[2048,128]{1,0:T(8,128)(2,1)} %k_ref.11, bf16[2048,128]{1,0:T(8,128)(2,1)} %v_ref.7), custom_call_target="tpu_custom_call" | custom-call | tf_op jit(solution)/shard_map/ask/pallas_call | solution.py:521
  3.1 5.8 %all-to-all-start = ((bf16[8,48,128]{2,1,0:T(8,128)(2,1)}), bf16[8,48,128]{2,1,0:T(8,128)(2,1)S(1)}, u32[]{:S(2)}, u32[]{:S(2)}) async-start(bf16[8,48,128]{2,1,0:T(8,128)(2,1)} %get-tuple-element.44), calls=%async_computation | async-start | bytes 196608 | tf_op jit(solution)/shard_map/all_to_all | solution.py:538
  8.9 4.2 %collective-permute-start.1 = (bf16[2,128,128]{2,1,0:T(8,128)(2,1)}, bf16[2,128,128]{2,1,0:T(8,128)(2,1)S(1)}, u32[]{:S(2)}, u32[]{:S(2)}) collective-permute-start(bf16[2,128,128]{2,1,0:T(8,128)(2,1)} %get-tuple-element.46), channel_id=1, source_target_pairs={{4,8},{8,4},{12,16},{16,12},{20,24},{24,20},{5,9},{9,5},{13,17},{1... | collective-permute-start | bytes 196616 | tf_op jit(solution)/shard_map/ppermute | solution.py:543
  13.2 2.1 %collective-permute-done.1.high_ref = bf16[2,128,128]{2,1,0:T(8,128)(2,1)S(1)} collective-permute-done((bf16[2,128,128]{2,1,0:T(8,128)(2,1)}, bf16[2,128,128]{2,1,0:T(8,128)(2,1)S(1)}, u32[]{:S(2)}, u32[]{:S(2)}) %collective-permute-start.1) | collective-permute-done | bytes 65568 | tf_op jit(solution)/shard_map/ppermute | solution.py:543
  16.0 2.8 %serve.1 = (bf16[8,160,128]{2,1,0:T(8,128)(2,1)}, s32[8]{0:T(128)}) custom-call(s32[2]{0:T(128)} %global_blocks.5, bf16[8,48,128]{2,1,0:T(8,128)(2,1)} %copy-done.13, bf16[2048,128]{1,0:T(8,128)(2,1)} %k_ref.11, bf16[2048,128]{1,0:T(8,128)(2,1)} %v_ref.7), custom_call_target="tpu_custom_call" | custom-call | tf_op jit(solution)/shard_map/serve/pallas_call | solution.py:546
  18.8 5.4 %all-to-all-start.1 = ((bf16[8,160,128]{2,1,0:T(8,128)(2,1)}), bf16[8,160,128]{2,1,0:T(8,128)(2,1)S(1)}, u32[]{:S(2)}, u32[]{:S(2)}) async-start(bf16[8,160,128]{2,1,0:T(8,128)(2,1)} %get-tuple-element.51), calls=%async_computation.1 | async-start | bytes 655360 | tf_op jit(solution)/shard_map/all_to_all | solution.py:555
  24.3 1.0 %copy-done = bf16[2048,128]{1,0:T(8,128)(2,1)S(1)} copy-done((bf16[2048,128]{1,0:T(8,128)(2,1)S(1)}, bf16[2048,128]{1,0:T(8,128)(2,1)}, u32[]{:S(2)}) %copy-start) | copy-done | bytes 524312
  25.3 1.0 %copy-done.1 = bf16[2048,128]{1,0:T(8,128)(2,1)S(1)} copy-done((bf16[2048,128]{1,0:T(8,128)(2,1)S(1)}, bf16[2048,128]{1,0:T(8,128)(2,1)}, u32[]{:S(2)}) %copy-start.1) | copy-done | bytes 524312
  26.3 1.2 %copy-done.2 = bf16[2048,256]{1,0:T(8,128)(2,1)S(1)} copy-done((bf16[2048,256]{1,0:T(8,128)(2,1)S(1)}, bf16[2048,256]{1,0:T(8,128)(2,1)}, u32[]{:S(2)}) %copy-start.2) | copy-done | bytes 1048600
  27.6 1.2 %copy-done.3 = bf16[2048,256]{1,0:T(8,128)(2,1)S(1)} copy-done((bf16[2048,256]{1,0:T(8,128)(2,1)S(1)}, bf16[2048,256]{1,0:T(8,128)(2,1)}, u32[]{:S(2)}) %copy-start.3) | copy-done | bytes 1048600
  28.8 3.1 %near.1.st_ref = f32[16,16,256]{2,1,0:T(8,128)S(1)} custom-call(bf16[2048,256]{1,0:T(8,128)(2,1)S(1)} %copy-done.2, bf16[2048,256]{1,0:T(8,128)(2,1)S(1)} %copy-done.3, bf16[2048,128]{1,0:T(8,128)(2,1)S(1)} %copy-done, bf16[2048,128]{1,0:T(8,128)(2,1)S(1)} %copy-done.1, bf16[2,128,128]{2,1,0:T(8,128)(2,1)S(1)} %collective-permute-done.low_ref, ...), custom_call_target="tpu_custom_call" | custom-call | flops 805306368 | bytes 4194304 | tf_op jit(solution)/shard_map/near/pallas_call | solution.py:562
  31.9 3.3 %collective-permute-start.2 = (bf16[8,160,128]{2,1,0:T(8,128)(2,1)S(1)}, bf16[8,160,128]{2,1,0:T(8,128)(2,1)S(1)}, u32[]{:S(2)}, u32[]{:S(2)}) collective-permute-start(bf16[8,160,128]{2,1,0:T(8,128)(2,1)S(1)} %all-to-all-done.1.mine_ref), channel_id=1, source_target_pairs={{0,1},{1,0},{2,3},{3,2},{4,5},{5,4},{6,7},{7,6},{8,9},{9,8},{10,11... | collective-permute-start | bytes 983048 | tf_op jit(solution)/shard_map/ppermute | solution.py:580
  35.2 1.7 %broadcast_select_fusion = (bf16[2048,256]{1,0:T(8,128)(2,1)S(1)}, bf16[2048,256]{1,0:T(8,128)(2,1)S(1)}) fusion(bf16[2048,256]{1,0:T(8,128)(2,1)} %g_ref.3, pred[]{:T(512)S(6)} %lt.3, bf16[2048,256]{1,0:T(8,128)(2,1)} %q_ref.3), kind=kLoop, calls=%fused_computation | loop fusion | flops 1048576 | bytes 4194305 | tf_op jit(solution)/shard_map/jit(_where)/select_n | solution.py:579
  37.6 10.3 %far.1 = (bf16[144,640,256]{2,1,0:T(8,128)(2,1)}, f32[16,8,256]{2,1,0:T(8,128)S(1)}, bf16[12,2,32,128]{3,2,1,0:T(8,128)(2,1)S(1)}, bf16[12,2,32,128]{3,2,1,0:T(8...) custom-call(s32[48]{0:T(128)S(1)} %copy-done.10, ...), custom_call_target="tpu_custom_call" | custom-call | flops 3355443200 | bytes 8388608 | tf_op jit(solution)/shard_map/far/pallas_call | solution.py:584
  48.6 1.2 %collective-permute-start.5 = (bf16[12,2,32,128]{3,2,1,0:T(8,128)(2,1)S(1)}, bf16[12,2,32,128]{3,2,1,0:T(8,128)(2,1)S(1)}, u32[]{:S(2)}, u32[]{:S(2)}) collective-permute-start(bf16[12,2,32,128]{3,2,1,0:T(8,128)(2,1)S(1)} %get-tuple-element.62), channel_id=1, source_target_pairs={{0,3},{1,2},{2,1},{3,0},{4,7},{5,6},{6,5},{7,4},{8,11},{9,10},{10,... | collective-permute-start | bytes 589832 | tf_op jit(solution)/shard_map/ppermute | solution.py:640
  50.5 8.1 %close.1 = (bf16[16,384,256]{2,1,0:T(8,128)(2,1)}, bf16[16,2,64,128]{3,2,1,0:T(8,128)(2,1)}, bf16[16,2,64,128]{3,2,1,0:T(8,128)(2,1)}) custom-call(bf16[2048,256]{1,0:T(8,128)(2,1)} %q_ref.3, bf16[2048,256]{1,0:T(8,128)(2,1)} %g_ref.3, bf16[2048,128]{1,0:T(8,128)(2,1)} %k_ref.11, bf16[2048,128]{1,0:T(8,128)(2,1)} %v_ref.7, bf16[2,128,128]{2,1,0:T(8,128)(2,1)} %copy-done.6, ...), custom_call_target="tpu_custom_call" | custom-call | flops 1610612736 | bytes 8388608 | tf_op jit(solution)/shard_map/close/pallas_call | solution.py:610
  60.1 5.2 %all-to-all-start.2 = ((bf16[8,6,32,128]{3,2,1,0:T(8,128)(2,1)}), bf16[8,6,32,128]{3,2,1,0:T(8,128)(2,1)S(1)}, u32[]{:S(2)}, u32[]{:S(2)}) async-start(bf16[8,6,32,128]{3,2,1,0:T(8,128)(2,1)} %get-tuple-element.67), calls=%async_computation.2 | async-start | bytes 786432 | tf_op jit(solution)/shard_map/all_to_all | solution.py:682
  66.5 1.3 %collective-permute-start.9 = (bf16[16,2,32,128]{3,2,1,0:T(8,128)(2,1)S(1)}, bf16[16,2,32,128]{3,2,1,0:T(8,128)(2,1)S(1)}, u32[]{:S(2)}, u32[]{:S(2)}) collective-permute-start(bf16[16,2,32,128]{3,2,1,0:T(8,128)(2,1)S(1)} %get-tuple-element.77), channel_id=1, source_target_pairs={{0,2},{1,3},{2,0},{3,1},{4,6},{5,7},{6,4},{7,5},{8,10},{9,11},{10,... | collective-permute-start | bytes 786440 | tf_op jit(solution)/shard_map/ppermute | solution.py:636
  67.8 4.3 %collective-permute-start.7 = (bf16[2,32,128]{2,1,0:T(8,128)(2,1)S(1)}, bf16[2,32,128]{2,1,0:T(8,128)(2,1)S(1)}, u32[]{:S(2)}, u32[]{:S(2)}) collective-permute-start(bf16[2,32,128]{2,1,0:T(8,128)(2,1)S(1)} %get-tuple-element.73), channel_id=1, source_target_pairs={{4,8},{8,4},{12,16},{16,12},{20,24},{24,20},{5,9},{9,5},{13,17},{1... | collective-permute-start | bytes 49160 | tf_op jit(solution)/shard_map/ppermute | solution.py:684
  72.1 5.2 %queries.2.refs_0_ = bf16[2048,256]{1,0:T(8,128)(2,1)} custom-call(s32[48]{0:T(128)} %get-tuple-element.49.owners, bf16[2048,128]{1,0:T(8,128)(2,1)} %k_ref.11, bf16[2,128,128]{2,1,0:T(8,128)(2,1)} %copy-done.6, bf16[2,128,128]{2,1,0:T(8,128)(2,1)} %copy-done.7, bf16[8,160,128]{2,1,0:T(8,128)(2,1)} %copy-done.4, bf16[8,160,128]{2,1,0:T(8,128)(2,1)} %copy-done.5, ...), custom_call_target="tpu_custom_call" | custom-call | flops 536870912 | bytes 4194304 | tf_op jit(solution)/shard_map/queries/pallas_call | solution.py:661
  78.5 2.7 %collective-permute-start.11 = (bf16[16,2,32,128]{3,2,1,0:T(8,128)(2,1)S(1)}, bf16[16,2,32,128]{3,2,1,0:T(8,128)(2,1)S(1)}, u32[]{:S(2)}, u32[]{:S(2)}) collective-permute-start(bf16[16,2,32,128]{3,2,1,0:T(8,128)(2,1)S(1)} %settle.1.refs_0_), channel_id=1, source_target_pairs={{0,1},{1,0},{2,3},{3,2},{4,5},{5,4},{6,7},{7,6},{8,9},{9,8},{10,11... | collective-permute-start | bytes 786440 | tf_op jit(solution)/shard_map/ppermute | solution.py:702
  81.1 5.2 %queries.3 = bf16[2048,256]{1,0:T(8,128)(2,1)} custom-call(s32[48]{0:T(128)} %get-tuple-element.49.owners, bf16[2048,128]{1,0:T(8,128)(2,1)} %k_ref.11, bf16[2,128,128]{2,1,0:T(8,128)(2,1)} %copy-done.6, bf16[2,128,128]{2,1,0:T(8,128)(2,1)} %copy-done.7, bf16[8,160,128]{2,1,0:T(8,128)(2,1)} %copy-done.4, ...), custom_call_target="tpu_custom_call", output_to_operand_aliasing={{}: (8, {})} | custom-call | flops 536870912 | bytes 4194304 | tf_op jit(solution)/shard_map/queries/pallas_call | solution.py:661
  87.0 1.2 %collective-permute-done.12.refs_3_ = bf16[16,2,32,128]{3,2,1,0:T(8,128)(2,1)S(1)} collective-permute-done((bf16[16,2,32,128]{3,2,1,0:T(8,128)(2,1)S(1)}, bf16[16,2,32,128]{3,2,1,0:T(8,128)(2,1)S(1)}, u32[]{:S(2)}, u32[]{:S(2)}) %collective-permute-start.12) | collective-permute-done | bytes 262176 | tf_op jit(solution)/shard_map/ppermute | solution.py:702
  88.1 1.1 %join.1 = (bf16[2048,128]{1,0:T(8,128)(2,1)}, bf16[2048,128]{1,0:T(8,128)(2,1)}) custom-call(bf16[16,2,32,128]{3,2,1,0:T(8,128)(2,1)S(1)} %settle.1.refs_0_, bf16[16,2,32,128]{3,2,1,0:T(8,128)(2,1)S(1)} %collective-permute-done.11.refs_1_, bf16[16,2,32,128]{3,2,1,0:T(8,128)(2,1)S(1)} %collective-permute-done.10.refs_2_, ...), custom_call_target="tpu_custom_call" | custom-call | tf_op jit(solution)/shard_map/join/pallas_call | solution.py:703
  (48 shorter events, 7.2 us)
Async XLA Ops:
  0.6 76.7 %copy-start.9 = (s32[2]{0:T(128)S(1)}, s32[2]{0:T(128)}, u32[]{:S(2)}) copy-start(s32[2]{0:T(128)} %global_blocks.5) | copy-start | bytes 28
  3.1 12.2 %all-to-all-start = ((bf16[8,48,128]{2,1,0:T(8,128)(2,1)}), bf16[8,48,128]{2,1,0:T(8,128)(2,1)S(1)}, u32[]{:S(2)}, u32[]{:S(2)}) async-start(bf16[8,48,128]{2,1,0:T(8,128)(2,1)} %get-tuple-element.44), calls=%async_computation | async-start | bytes 196608 | tf_op jit(solution)/shard_map/all_to_all | solution.py:538
  8.9 4.3 %collective-permute-start = (bf16[2,128,128]{2,1,0:T(8,128)(2,1)}, bf16[2,128,128]{2,1,0:T(8,128)(2,1)S(1)}, u32[]{:S(2)}, u32[]{:S(2)}) collective-permute-start(bf16[2,128,128]{2,1,0:T(8,128)(2,1)} %get-tuple-element.45), channel_id=1, source_target_pairs={{0,4},{4,0},{8,12},{12,8},{16,20},{20,16},{24,28},{28,24},{1,5},{5... | collective-permute-start | bytes 196616 | tf_op jit(solution)/shard_map/ppermute | solution.py:542
  8.9 6.4 %collective-permute-start.1 = (bf16[2,128,128]{2,1,0:T(8,128)(2,1)}, bf16[2,128,128]{2,1,0:T(8,128)(2,1)S(1)}, u32[]{:S(2)}, u32[]{:S(2)}) collective-permute-start(bf16[2,128,128]{2,1,0:T(8,128)(2,1)} %get-tuple-element.46), channel_id=1, source_target_pairs={{4,8},{8,4},{12,16},{16,12},{20,24},{24,20},{5,9},{9,5},{13,17},{1... | collective-permute-start | bytes 196616 | tf_op jit(solution)/shard_map/ppermute | solution.py:543
  13.2 37.2 %copy-start.6 = (bf16[2,128,128]{2,1,0:T(8,128)(2,1)}, bf16[2,128,128]{2,1,0:T(8,128)(2,1)S(1)}, u32[]{:S(2)}) copy-start(bf16[2,128,128]{2,1,0:T(8,128)(2,1)S(1)} %collective-permute-done.low_ref) | copy-start | bytes 196612
  15.3 35.1 %copy-start.7 = (bf16[2,128,128]{2,1,0:T(8,128)(2,1)}, bf16[2,128,128]{2,1,0:T(8,128)(2,1)S(1)}, u32[]{:S(2)}) copy-start(bf16[2,128,128]{2,1,0:T(8,128)(2,1)S(1)} %collective-permute-done.1.high_ref) | copy-start | bytes 196612
  18.8 58.5 %copy-start.11 = (s32[8]{0:T(128)S(1)}, s32[8]{0:T(128)}, u32[]{:S(2)}) copy-start(s32[8]{0:T(128)} %get-tuple-element.70.requested) | copy-start | bytes 100
  18.8 13.0 %all-to-all-start.1 = ((bf16[8,160,128]{2,1,0:T(8,128)(2,1)}), bf16[8,160,128]{2,1,0:T(8,128)(2,1)S(1)}, u32[]{:S(2)}, u32[]{:S(2)}) async-start(bf16[8,160,128]{2,1,0:T(8,128)(2,1)} %get-tuple-element.51), calls=%async_computation.1 | async-start | bytes 655360 | tf_op jit(solution)/shard_map/all_to_all | solution.py:555
  26.3 1.2 %copy-start.2 = (bf16[2048,256]{1,0:T(8,128)(2,1)S(1)}, bf16[2048,256]{1,0:T(8,128)(2,1)}, u32[]{:S(2)}) copy-start(bf16[2048,256]{1,0:T(8,128)(2,1)} %q_ref.3) | copy-start | bytes 3145732
  27.6 1.2 %copy-start.3 = (bf16[2048,256]{1,0:T(8,128)(2,1)S(1)}, bf16[2048,256]{1,0:T(8,128)(2,1)}, u32[]{:S(2)}) copy-start(bf16[2048,256]{1,0:T(8,128)(2,1)} %g_ref.3) | copy-start | bytes 3145732
  31.9 40.2 %copy-start.4 = (bf16[8,160,128]{2,1,0:T(8,128)(2,1)}, bf16[8,160,128]{2,1,0:T(8,128)(2,1)S(1)}, u32[]{:S(2)}) copy-start(bf16[8,160,128]{2,1,0:T(8,128)(2,1)S(1)} %all-to-all-done.1.mine_ref) | copy-start | bytes 983044
  31.9 5.0 %collective-permute-start.2 = (bf16[8,160,128]{2,1,0:T(8,128)(2,1)S(1)}, bf16[8,160,128]{2,1,0:T(8,128)(2,1)S(1)}, u32[]{:S(2)}, u32[]{:S(2)}) collective-permute-start(bf16[8,160,128]{2,1,0:T(8,128)(2,1)S(1)} %all-to-all-done.1.mine_ref), channel_id=1, source_target_pairs={{0,1},{1,0},{2,3},{3,2},{4,5},{5,4},{6,7},{7,6},{8,9},{9,8},{10,11... | collective-permute-start | bytes 983048 | tf_op jit(solution)/shard_map/ppermute | solution.py:580
  36.9 35.1 %copy-start.5 = (bf16[8,160,128]{2,1,0:T(8,128)(2,1)}, bf16[8,160,128]{2,1,0:T(8,128)(2,1)S(1)}, u32[]{:S(2)}) copy-start(bf16[8,160,128]{2,1,0:T(8,128)(2,1)S(1)} %collective-permute-done.2.other_ref) | copy-start | bytes 983044
  48.6 10.0 %collective-permute-start.5 = (bf16[12,2,32,128]{3,2,1,0:T(8,128)(2,1)S(1)}, bf16[12,2,32,128]{3,2,1,0:T(8,128)(2,1)S(1)}, u32[]{:S(2)}, u32[]{:S(2)}) collective-permute-start(bf16[12,2,32,128]{3,2,1,0:T(8,128)(2,1)S(1)} %get-tuple-element.62), channel_id=1, source_target_pairs={{0,3},{1,2},{2,1},{3,0},{4,7},{5,6},{6,5},{7,4},{8,11},{9,10},{10,... | collective-permute-start | bytes 589832 | tf_op jit(solution)/shard_map/ppermute | solution.py:640
  49.8 9.2 %collective-permute-start.3 = (bf16[12,2,32,128]{3,2,1,0:T(8,128)(2,1)S(1)}, bf16[12,2,32,128]{3,2,1,0:T(8,128)(2,1)S(1)}, u32[]{:S(2)}, u32[]{:S(2)}) collective-permute-start(bf16[12,2,32,128]{3,2,1,0:T(8,128)(2,1)S(1)} %get-tuple-element.60), channel_id=1, source_target_pairs={{0,1},{1,0},{2,3},{3,2},{4,5},{5,4},{6,7},{7,6},{8,9},{9,8},{10,11... | collective-permute-start | bytes 589832 | tf_op jit(solution)/shard_map/ppermute | solution.py:640
  50.2 9.1 %collective-permute-start.4 = (bf16[12,2,32,128]{3,2,1,0:T(8,128)(2,1)S(1)}, bf16[12,2,32,128]{3,2,1,0:T(8,128)(2,1)S(1)}, u32[]{:S(2)}, u32[]{:S(2)}) collective-permute-start(bf16[12,2,32,128]{3,2,1,0:T(8,128)(2,1)S(1)} %get-tuple-element.61), channel_id=1, source_target_pairs={{0,2},{1,3},{2,0},{3,1},{4,6},{5,7},{6,4},{7,5},{8,10},{9,11},{10,... | collective-permute-start | bytes 589832 | tf_op jit(solution)/shard_map/ppermute | solution.py:640
  58.5 6.8 %collective-permute-start.8 = (bf16[16,2,64,128]{3,2,1,0:T(8,128)(2,1)}, bf16[16,2,64,128]{3,2,1,0:T(8,128)(2,1)S(1)}, u32[]{:S(2)}, u32[]{:S(2)}) collective-permute-start(bf16[16,2,64,128]{3,2,1,0:T(8,128)(2,1)} %get-tuple-element.75), channel_id=1, source_target_pairs={{0,1},{1,0},{2,3},{3,2},{4,5},{5,4},{6,7},{7,6},{8,9},{9,8},{10,11... | collective-permute-start | bytes 1572872 | tf_op jit(solution)/shard_map/ppermute | solution.py:625
  60.1 17.1 %all-to-all-start.2 = ((bf16[8,6,32,128]{3,2,1,0:T(8,128)(2,1)}), bf16[8,6,32,128]{3,2,1,0:T(8,128)(2,1)S(1)}, u32[]{:S(2)}, u32[]{:S(2)}) async-start(bf16[8,6,32,128]{3,2,1,0:T(8,128)(2,1)} %get-tuple-element.67), calls=%async_computation.2 | async-start | bytes 786432 | tf_op jit(solution)/shard_map/all_to_all | solution.py:682
  66.5 10.8 %collective-permute-start.9 = (bf16[16,2,32,128]{3,2,1,0:T(8,128)(2,1)S(1)}, bf16[16,2,32,128]{3,2,1,0:T(8,128)(2,1)S(1)}, u32[]{:S(2)}, u32[]{:S(2)}) collective-permute-start(bf16[16,2,32,128]{3,2,1,0:T(8,128)(2,1)S(1)} %get-tuple-element.77), channel_id=1, source_target_pairs={{0,2},{1,3},{2,0},{3,1},{4,6},{5,7},{6,4},{7,5},{8,10},{9,11},{10,... | collective-permute-start | bytes 786440 | tf_op jit(solution)/shard_map/ppermute | solution.py:636
  67.8 9.5 %collective-permute-start.6 = (bf16[2,32,128]{2,1,0:T(8,128)(2,1)S(1)}, bf16[2,32,128]{2,1,0:T(8,128)(2,1)S(1)}, u32[]{:S(2)}, u32[]{:S(2)}) collective-permute-start(bf16[2,32,128]{2,1,0:T(8,128)(2,1)S(1)} %get-tuple-element.72), channel_id=1, source_target_pairs={{0,4},{4,0},{8,12},{12,8},{16,20},{20,16},{24,28},{28,24},{1,5},{5... | collective-permute-start | bytes 49160 | tf_op jit(solution)/shard_map/ppermute | solution.py:683
  67.8 9.5 %collective-permute-start.7 = (bf16[2,32,128]{2,1,0:T(8,128)(2,1)S(1)}, bf16[2,32,128]{2,1,0:T(8,128)(2,1)S(1)}, u32[]{:S(2)}, u32[]{:S(2)}) collective-permute-start(bf16[2,32,128]{2,1,0:T(8,128)(2,1)S(1)} %get-tuple-element.73), channel_id=1, source_target_pairs={{4,8},{8,4},{12,16},{16,12},{20,24},{24,20},{5,9},{9,5},{13,17},{1... | collective-permute-start | bytes 49160 | tf_op jit(solution)/shard_map/ppermute | solution.py:684
  78.1 8.2 %collective-permute-start.10 = (bf16[16,2,32,128]{3,2,1,0:T(8,128)(2,1)S(1)}, bf16[16,2,32,128]{3,2,1,0:T(8,128)(2,1)S(1)}, u32[]{:S(2)}, u32[]{:S(2)}) collective-permute-start(bf16[16,2,32,128]{3,2,1,0:T(8,128)(2,1)S(1)} %settle.1.refs_0_), channel_id=1, source_target_pairs={{0,2},{1,3},{2,0},{3,1},{4,6},{5,7},{6,4},{7,5},{8,10},{9,11},{10,... | collective-permute-start | bytes 786440 | tf_op jit(solution)/shard_map/ppermute | solution.py:698
  78.5 8.5 %collective-permute-start.11 = (bf16[16,2,32,128]{3,2,1,0:T(8,128)(2,1)S(1)}, bf16[16,2,32,128]{3,2,1,0:T(8,128)(2,1)S(1)}, u32[]{:S(2)}, u32[]{:S(2)}) collective-permute-start(bf16[16,2,32,128]{3,2,1,0:T(8,128)(2,1)S(1)} %settle.1.refs_0_), channel_id=1, source_target_pairs={{0,1},{1,0},{2,3},{3,2},{4,5},{5,4},{6,7},{7,6},{8,9},{9,8},{10,11... | collective-permute-start | bytes 786440 | tf_op jit(solution)/shard_map/ppermute | solution.py:702
  86.3 1.8 %collective-permute-start.12 = (bf16[16,2,32,128]{3,2,1,0:T(8,128)(2,1)S(1)}, bf16[16,2,32,128]{3,2,1,0:T(8,128)(2,1)S(1)}, u32[]{:S(2)}, u32[]{:S(2)}) collective-permute-start(bf16[16,2,32,128]{3,2,1,0:T(8,128)(2,1)S(1)} %collective-permute-done.10.refs_2_), channel_id=1, source_target_pairs={{0,1},{1,0},{2,3},{3,2},{4,5},{5,4},{6,7},{7,6},{8,9},{9,8},{10,11... | collective-permute-start | bytes 786440 | tf_op jit(solution)/shard_map/ppermute | solution.py:702
  (6 other events, 5.1 us)

commit v6 on v5

--- a/solution.py
+++ b/solution.py
@@ -21,7 +21,7 @@
 FACTOR = float(DH) ** -0.5
 SCALE = FACTOR * math.log2(math.e)
 FOLD = 8
-SPARE = 9
+SPARE = 5
 MARKS = 16
 
 NT = (((1,), (1,)), ((), ()))
@@ -267,10 +267,10 @@
 
 
 def far_kernel(
-    owners, q_ref, g_ref, mine_ref, other_ref, st_ref, low_ref, high_ref,
-    ds_ref, fd_ref, *refs,
+    random_blocks, q_ref, g_ref, mine_ref, other_ref, st_ref, low_ref, high_ref,
+    ds_ref, sums_ref, *refs,
 ):
-    *share_refs, k_all, v_all, acc, e_all, dp_all, ds_all, out_sems = refs
+    *share_refs, k_all, v_all, acc, e_all, dp_all, ds_all, fd_ref, out_sems, sums_sem = refs
     blocks = q_ref.shape[0] // BLOCK
     peers = mine_ref.shape[0]
     core, column = places()
@@ -302,7 +302,7 @@
         )
 
     def slots_of(b):
-        return [owners[b * R + r] for r in range(R)] + [peers + j for j in range(G)]
+        return [lax.div(random_blocks[r, b], blocks) for r in range(R)] + [peers + j for j in range(G)]
 
     def work(new, new_slot, old, old_slot, stats):
         if new is not None:
@@ -368,6 +368,8 @@
     stats = work(0, 0, None, None, None)
     stats = lax.fori_loop(0, blocks // turn - 1, several, stats)
     stats = several(blocks // turn - 1, stats, True)
+    sums = pltpu.make_async_copy(fd_ref, sums_ref.at[pl.ds(0, blocks)], sums_sem)
+    sums.start()
     work(None, None, blocks - 1, 1, stats)
 
     for slot, w, b, swap in ((peers + G, 0, 0, 1), (peers + G + 1, WINDOW - 1, blocks - 1, 0)):
@@ -387,6 +389,7 @@
         rows = pl.ds(pl.multiple_of(start, share), share)
         for which, f in ((0, FACTOR), (1, 1.0)):
             ref[:, which] = (acc[:, which, rows, :] * f).astype(ref.dtype)
+    sums.wait()
     for b in range(blocks):
         put(b).wait()
 
@@ -585,24 +588,26 @@
         far_kernel,
         out_shape=(
             sds((blocks * SPARE, FAR * BLOCK, lanes), bf16),
-            sds((blocks, FOLD, lanes), f32),
+            sds((blocks * SPARE * 20, FOLD, lanes), f32),
         )
         + (sds(piece, bf16),) * head_count,
         in_specs=[smem] + [vmem] * 7,
-        out_specs=(hbm, vmem) + (vmem,) * head_count,
+        out_specs=(hbm, hbm) + (vmem,) * head_count,
         scratch_shapes=[pltpu.VMEM((seq_count + G, BLOCK, DH), bf16)] * 2
         + [pltpu.VMEM((slots, 2, BLOCK, DH), f32)]
         + [pltpu.VMEM((2, FAR * BLOCK, lanes), f32)] * 2
         + [
             pltpu.VMEM((blocks, FAR * BLOCK, lanes), bf16),
+            pltpu.VMEM((blocks, FOLD, lanes), f32),
             pltpu.SemaphoreType.DMA((blocks,)),
+            pltpu.SemaphoreType.DMA(()),
         ],
-        compiler_params=small,
+        compiler_params=pltpu.CompilerParams(vmem_limit_bytes=max(limit, 42 * MIB)),
         cost_estimate=pl.CostEstimate(
             flops=5 * FAR * unit, bytes_accessed=8 * MIB, transcendentals=blocks * lanes * FAR * BLOCK
         ),
         name="far",
-    )(owners, queries_in, grads_in, mine, other, st, low, high)
+    )(random_blocks.T, queries_in, grads_in, mine, other, st, low, high)
 
     piece_w = (blocks, 2, HALF, DH)
     near_spec = per_block(per, WINDOW * BLOCK, lanes)

time: 90.3 us -> 88.6 us (0.981)
  Pallas kernels: 40.1 us -> 39 us
    unnamed x28 -> x26, local copies, waits for them, and re-layouts: 7.56 us -> 6.95 us
  transfers between devices with their start and end apart: 16 -> 16, of which waited for: 3 -> 3; matrix products, arithmetic and copies ran while one was open for 2% -> 2% of each run, Pallas kernels for 25% -> 26%
where the time goes in v6:
time: 88.6 us; the launch traced here: 87.6 us
  Pallas kernels  39 us (44%)
  starting transfers between devices  35.6 us (40%)
  local copies, waits for them, and re-layouts  6.95 us (8%)
  waiting for transfers between devices  3.55 us (4%)
  other arithmetic  1.68 us (2%)
    pallas_call x2, Pallas kernels, queries(): pl.pallas_call(functools.partial(queries_kernel, shift * per), out_shape=...  10.4 us
    pallas_call x1, Pallas kernels, body(): pl.pallas_call(far_kernel, out_shape=(sds((blocks * SPARE, FAR * BLOCK, l...  9.52 us
    pallas_call x1, Pallas kernels, body(): pl.pallas_call(close_kernel, out_shape=(sds((blocks, WINDOW * BLOCK, lane...  8.05 us
    unnamed x26, local copies, waits for them, and re-layouts  6.95 us
    all_to_all x1, starting transfers between devices, body(): lax.all_to_all(asking, 'seq', split_axis=0, concat_axis=0, tiled=True)  5.79 us
    all_to_all x1, starting transfers between devices, body(): lax.all_to_all(served, 'seq', split_axis=0, concat_axis=0, tiled=True)  5.42 us
    all_to_all x1, starting transfers between devices, body(): back = lax.all_to_all(terms, 'seq', split_axis=0, concat_axis=0, tiled=True)  5.11 us
    ppermute x1, starting transfers between devices, body(): from_high = lax.ppermute(to_high, 'seq', high_pairs)  4.25 us
  transfers between devices with their start and end apart: 16, of which 3 were waited for; matrix products, arithmetic and copies ran while one was open for 2% of the time, Pallas kernels for 26%

profile of v6, /device:TPU:5, one launch (start us, length us, event | category | flops | bytes accessed | tf_op | source)
XLA Modules:
  0.0 87.6 jit_solution(9271499873073231001)
XLA Ops:
  0.6 2.4 %ask.1 = (bf16[8,48,128]{2,1,0:T(8,128)(2,1)}, bf16[2,128,128]{2,1,0:T(8,128)(2,1)}, bf16[2,128,128]{2,1,0:T(8,128)(2,1)}, s32[48]{0:T(128)}) custom-call(s32[2]{0:T(128)} %global_blocks.5, s32[3,16]{1,0:T(4,128)} %bitcast.1, s32[3,16]{1,0:T(4,128)} %bitcast.2, bf16[2048,128]{1,0:T(8,128)(2,1)} %k_ref.11, bf16[2048,128]{1,0:T(8,128)(2,1)} %v_ref.7), custom_call_target="tpu_custom_call" | custom-call | tf_op jit(solution)/shard_map/ask/pallas_call | solution.py:524
  3.0 5.8 %all-to-all-start = ((bf16[8,48,128]{2,1,0:T(8,128)(2,1)}), bf16[8,48,128]{2,1,0:T(8,128)(2,1)S(1)}, u32[]{:S(2)}, u32[]{:S(2)}) async-start(bf16[8,48,128]{2,1,0:T(8,128)(2,1)} %get-tuple-element.44), calls=%async_computation | async-start | bytes 196608 | tf_op jit(solution)/shard_map/all_to_all | solution.py:541
  8.8 4.2 %collective-permute-start.1 = (bf16[2,128,128]{2,1,0:T(8,128)(2,1)}, bf16[2,128,128]{2,1,0:T(8,128)(2,1)S(1)}, u32[]{:S(2)}, u32[]{:S(2)}) collective-permute-start(bf16[2,128,128]{2,1,0:T(8,128)(2,1)} %get-tuple-element.46), channel_id=1, source_target_pairs={{4,8},{8,4},{12,16},{16,12},{20,24},{24,20},{5,9},{9,5},{13,17},{1... | collective-permute-start | bytes 196616 | tf_op jit(solution)/shard_map/ppermute | solution.py:546
  13.1 2.1 %collective-permute-done.1.high_ref = bf16[2,128,128]{2,1,0:T(8,128)(2,1)S(1)} collective-permute-done((bf16[2,128,128]{2,1,0:T(8,128)(2,1)}, bf16[2,128,128]{2,1,0:T(8,128)(2,1)S(1)}, u32[]{:S(2)}, u32[]{:S(2)}) %collective-permute-start.1) | collective-permute-done | bytes 65568 | tf_op jit(solution)/shard_map/ppermute | solution.py:546
  15.9 2.8 %serve.1 = (bf16[8,160,128]{2,1,0:T(8,128)(2,1)}, s32[8]{0:T(128)}) custom-call(s32[2]{0:T(128)} %global_blocks.5, bf16[8,48,128]{2,1,0:T(8,128)(2,1)} %copy-done.12, bf16[2048,128]{1,0:T(8,128)(2,1)} %k_ref.11, bf16[2048,128]{1,0:T(8,128)(2,1)} %v_ref.7), custom_call_target="tpu_custom_call" | custom-call | tf_op jit(solution)/shard_map/serve/pallas_call | solution.py:549
  18.7 5.4 %all-to-all-start.1 = ((bf16[8,160,128]{2,1,0:T(8,128)(2,1)}), bf16[8,160,128]{2,1,0:T(8,128)(2,1)S(1)}, u32[]{:S(2)}, u32[]{:S(2)}) async-start(bf16[8,160,128]{2,1,0:T(8,128)(2,1)} %get-tuple-element.50), calls=%async_computation.1 | async-start | bytes 655360 | tf_op jit(solution)/shard_map/all_to_all | solution.py:558
  24.1 1.0 %copy-done = bf16[2048,128]{1,0:T(8,128)(2,1)S(1)} copy-done((bf16[2048,128]{1,0:T(8,128)(2,1)S(1)}, bf16[2048,128]{1,0:T(8,128)(2,1)}, u32[]{:S(2)}) %copy-start) | copy-done | bytes 524312
  25.2 1.2 %copy-done.1 = bf16[2048,256]{1,0:T(8,128)(2,1)S(1)} copy-done((bf16[2048,256]{1,0:T(8,128)(2,1)S(1)}, bf16[2048,256]{1,0:T(8,128)(2,1)}, u32[]{:S(2)}) %copy-start.1) | copy-done | bytes 1048600
  26.4 1.2 %copy-done.2 = bf16[2048,256]{1,0:T(8,128)(2,1)S(1)} copy-done((bf16[2048,256]{1,0:T(8,128)(2,1)S(1)}, bf16[2048,256]{1,0:T(8,128)(2,1)}, u32[]{:S(2)}) %copy-start.2) | copy-done | bytes 1048600
  27.6 1.0 %copy-done.3 = bf16[2048,128]{1,0:T(8,128)(2,1)S(1)} copy-done((bf16[2048,128]{1,0:T(8,128)(2,1)S(1)}, bf16[2048,128]{1,0:T(8,128)(2,1)}, u32[]{:S(2)}) %copy-start.3) | copy-done | bytes 524312
  28.7 3.0 %near.1.st_ref = f32[16,16,256]{2,1,0:T(8,128)S(1)} custom-call(bf16[2048,256]{1,0:T(8,128)(2,1)S(1)} %copy-done.1, bf16[2048,256]{1,0:T(8,128)(2,1)S(1)} %copy-done.2, bf16[2048,128]{1,0:T(8,128)(2,1)S(1)} %copy-done, bf16[2048,128]{1,0:T(8,128)(2,1)S(1)} %copy-done.3, bf16[2,128,128]{2,1,0:T(8,128)(2,1)S(1)} %collective-permute-done.low_ref, ...), custom_call_target="tpu_custom_call" | custom-call | flops 805306368 | bytes 4194304 | tf_op jit(solution)/shard_map/near/pallas_call | solution.py:565
  31.7 3.4 %collective-permute-start.2 = (bf16[8,160,128]{2,1,0:T(8,128)(2,1)S(1)}, bf16[8,160,128]{2,1,0:T(8,128)(2,1)S(1)}, u32[]{:S(2)}, u32[]{:S(2)}) collective-permute-start(bf16[8,160,128]{2,1,0:T(8,128)(2,1)S(1)} %all-to-all-done.1.mine_ref), channel_id=1, source_target_pairs={{0,1},{1,0},{2,3},{3,2},{4,5},{5,4},{6,7},{7,6},{8,9},{9,8},{10,11... | collective-permute-start | bytes 983048 | tf_op jit(solution)/shard_map/ppermute | solution.py:583
  35.1 1.7 %broadcast_select_fusion = (bf16[2048,256]{1,0:T(8,128)(2,1)S(1)}, bf16[2048,256]{1,0:T(8,128)(2,1)S(1)}) fusion(bf16[2048,256]{1,0:T(8,128)(2,1)} %g_ref.3, pred[]{:T(512)S(6)} %lt.3, bf16[2048,256]{1,0:T(8,128)(2,1)} %q_ref.3), kind=kLoop, calls=%fused_computation | loop fusion | flops 1048576 | bytes 4194305 | tf_op jit(solution)/shard_map/jit(_where)/select_n | solution.py:582
  37.5 9.5 %far.1 = (bf16[80,640,256]{2,1,0:T(8,128)(2,1)}, f32[1600,8,256]{2,1,0:T(8,128)}, bf16[12,2,32,128]{3,2,1,0:T(8,128)(2,1)S(1)}, bf16[12,2,32,128]{3,2,1,0:T(8,12...) custom-call(s32[3,16]{1,0:T(4,128)S(1)} %bitcast.3, ...), custom_call_target="tpu_custom_call" | custom-call | flops 3355443200 | bytes 8388608 | tf_op jit(solution)/shard_map/far/pallas_call | solution.py:587
  47.0 1.3 %collective-permute-start.5 = (bf16[12,2,32,128]{3,2,1,0:T(8,128)(2,1)S(1)}, bf16[12,2,32,128]{3,2,1,0:T(8,128)(2,1)S(1)}, u32[]{:S(2)}, u32[]{:S(2)}) collective-permute-start(bf16[12,2,32,128]{3,2,1,0:T(8,128)(2,1)S(1)} %get-tuple-element.61), channel_id=1, source_target_pairs={{0,3},{1,2},{2,1},{3,0},{4,7},{5,6},{6,5},{7,4},{8,11},{9,10},{10,... | collective-permute-start | bytes 589832 | tf_op jit(solution)/shard_map/ppermute | solution.py:645
  49.0 8.1 %close.1 = (bf16[16,384,256]{2,1,0:T(8,128)(2,1)}, bf16[16,2,64,128]{3,2,1,0:T(8,128)(2,1)}, bf16[16,2,64,128]{3,2,1,0:T(8,128)(2,1)}) custom-call(bf16[2048,256]{1,0:T(8,128)(2,1)} %q_ref.3, bf16[2048,256]{1,0:T(8,128)(2,1)} %g_ref.3, bf16[2048,128]{1,0:T(8,128)(2,1)} %k_ref.11, bf16[2048,128]{1,0:T(8,128)(2,1)} %v_ref.7, bf16[2,128,128]{2,1,0:T(8,128)(2,1)} %copy-done.6, ...), custom_call_target="tpu_custom_call" | custom-call | flops 1610612736 | bytes 8388608 | tf_op jit(solution)/shard_map/close/pallas_call | solution.py:615
  58.6 5.1 %all-to-all-start.2 = ((bf16[8,6,32,128]{3,2,1,0:T(8,128)(2,1)}), bf16[8,6,32,128]{3,2,1,0:T(8,128)(2,1)S(1)}, u32[]{:S(2)}, u32[]{:S(2)}) async-start(bf16[8,6,32,128]{3,2,1,0:T(8,128)(2,1)} %get-tuple-element.66), calls=%async_computation.2 | async-start | bytes 786432 | tf_op jit(solution)/shard_map/all_to_all | solution.py:687
  64.9 1.3 %collective-permute-start.9 = (bf16[16,2,32,128]{3,2,1,0:T(8,128)(2,1)S(1)}, bf16[16,2,32,128]{3,2,1,0:T(8,128)(2,1)S(1)}, u32[]{:S(2)}, u32[]{:S(2)}) collective-permute-start(bf16[16,2,32,128]{3,2,1,0:T(8,128)(2,1)S(1)} %get-tuple-element.77), channel_id=1, source_target_pairs={{0,2},{1,3},{2,0},{3,1},{4,6},{5,7},{6,4},{7,5},{8,10},{9,11},{10,... | collective-permute-start | bytes 786440 | tf_op jit(solution)/shard_map/ppermute | solution.py:641
  66.2 4.3 %collective-permute-start.7 = (bf16[2,32,128]{2,1,0:T(8,128)(2,1)S(1)}, bf16[2,32,128]{2,1,0:T(8,128)(2,1)S(1)}, u32[]{:S(2)}, u32[]{:S(2)}) collective-permute-start(bf16[2,32,128]{2,1,0:T(8,128)(2,1)S(1)} %get-tuple-element.73), channel_id=1, source_target_pairs={{4,8},{8,4},{12,16},{16,12},{20,24},{24,20},{5,9},{9,5},{13,17},{1... | collective-permute-start | bytes 49160 | tf_op jit(solution)/shard_map/ppermute | solution.py:689
  70.5 5.2 %queries.2.refs_0_ = bf16[2048,256]{1,0:T(8,128)(2,1)} custom-call(s32[48]{0:T(128)} %get-tuple-element.67.owners, bf16[2048,128]{1,0:T(8,128)(2,1)} %k_ref.11, bf16[2,128,128]{2,1,0:T(8,128)(2,1)} %copy-done.6, bf16[2,128,128]{2,1,0:T(8,128)(2,1)} %copy-done.7, bf16[8,160,128]{2,1,0:T(8,128)(2,1)} %copy-done.4, bf16[8,160,128]{2,1,0:T(8,128)(2,1)} %copy-done.5, ...), custom_call_target="tpu_custom_call" | custom-call | flops 536870912 | bytes 4194304 | tf_op jit(solution)/shard_map/queries/pallas_call | solution.py:666
  76.9 2.7 %collective-permute-start.11 = (bf16[16,2,32,128]{3,2,1,0:T(8,128)(2,1)S(1)}, bf16[16,2,32,128]{3,2,1,0:T(8,128)(2,1)S(1)}, u32[]{:S(2)}, u32[]{:S(2)}) collective-permute-start(bf16[16,2,32,128]{3,2,1,0:T(8,128)(2,1)S(1)} %settle.1.refs_0_), channel_id=1, source_target_pairs={{0,1},{1,0},{2,3},{3,2},{4,5},{5,4},{6,7},{7,6},{8,9},{9,8},{10,11... | collective-permute-start | bytes 786440 | tf_op jit(solution)/shard_map/ppermute | solution.py:707
  79.5 5.2 %queries.3 = bf16[2048,256]{1,0:T(8,128)(2,1)} custom-call(s32[48]{0:T(128)} %get-tuple-element.67.owners, bf16[2048,128]{1,0:T(8,128)(2,1)} %k_ref.11, bf16[2,128,128]{2,1,0:T(8,128)(2,1)} %copy-done.6, bf16[2,128,128]{2,1,0:T(8,128)(2,1)} %copy-done.7, bf16[8,160,128]{2,1,0:T(8,128)(2,1)} %copy-done.4, ...), custom_call_target="tpu_custom_call", output_to_operand_aliasing={{}: (8, {})} | custom-call | flops 536870912 | bytes 4194304 | tf_op jit(solution)/shard_map/queries/pallas_call | solution.py:666
  85.4 1.2 %collective-permute-done.12.refs_3_ = bf16[16,2,32,128]{3,2,1,0:T(8,128)(2,1)S(1)} collective-permute-done((bf16[16,2,32,128]{3,2,1,0:T(8,128)(2,1)S(1)}, bf16[16,2,32,128]{3,2,1,0:T(8,128)(2,1)S(1)}, u32[]{:S(2)}, u32[]{:S(2)}) %collective-permute-start.12) | collective-permute-done | bytes 262176 | tf_op jit(solution)/shard_map/ppermute | solution.py:707
  86.5 1.1 %join.1 = (bf16[2048,128]{1,0:T(8,128)(2,1)}, bf16[2048,128]{1,0:T(8,128)(2,1)}) custom-call(bf16[16,2,32,128]{3,2,1,0:T(8,128)(2,1)S(1)} %settle.1.refs_0_, bf16[16,2,32,128]{3,2,1,0:T(8,128)(2,1)S(1)} %collective-permute-done.11.refs_1_, bf16[16,2,32,128]{3,2,1,0:T(8,128)(2,1)S(1)} %collective-permute-done.10.refs_2_, ...), custom_call_target="tpu_custom_call" | custom-call | tf_op jit(solution)/shard_map/join/pallas_call | solution.py:708
  (46 shorter events, 6.6 us)
Async XLA Ops:
  3.0 12.2 %all-to-all-start = ((bf16[8,48,128]{2,1,0:T(8,128)(2,1)}), bf16[8,48,128]{2,1,0:T(8,128)(2,1)S(1)}, u32[]{:S(2)}, u32[]{:S(2)}) async-start(bf16[8,48,128]{2,1,0:T(8,128)(2,1)} %get-tuple-element.44), calls=%async_computation | async-start | bytes 196608 | tf_op jit(solution)/shard_map/all_to_all | solution.py:541
  8.8 4.3 %collective-permute-start = (bf16[2,128,128]{2,1,0:T(8,128)(2,1)}, bf16[2,128,128]{2,1,0:T(8,128)(2,1)S(1)}, u32[]{:S(2)}, u32[]{:S(2)}) collective-permute-start(bf16[2,128,128]{2,1,0:T(8,128)(2,1)} %get-tuple-element.45), channel_id=1, source_target_pairs={{0,4},{4,0},{8,12},{12,8},{16,20},{20,16},{24,28},{28,24},{1,5},{5... | collective-permute-start | bytes 196616 | tf_op jit(solution)/shard_map/ppermute | solution.py:545
  8.8 6.4 %collective-permute-start.1 = (bf16[2,128,128]{2,1,0:T(8,128)(2,1)}, bf16[2,128,128]{2,1,0:T(8,128)(2,1)S(1)}, u32[]{:S(2)}, u32[]{:S(2)}) collective-permute-start(bf16[2,128,128]{2,1,0:T(8,128)(2,1)} %get-tuple-element.46), channel_id=1, source_target_pairs={{4,8},{8,4},{12,16},{16,12},{20,24},{24,20},{5,9},{9,5},{13,17},{1... | collective-permute-start | bytes 196616 | tf_op jit(solution)/shard_map/ppermute | solution.py:546
  13.1 35.9 %copy-start.6 = (bf16[2,128,128]{2,1,0:T(8,128)(2,1)}, bf16[2,128,128]{2,1,0:T(8,128)(2,1)S(1)}, u32[]{:S(2)}) copy-start(bf16[2,128,128]{2,1,0:T(8,128)(2,1)S(1)} %collective-permute-done.low_ref) | copy-start | bytes 196612
  15.2 33.8 %copy-start.7 = (bf16[2,128,128]{2,1,0:T(8,128)(2,1)}, bf16[2,128,128]{2,1,0:T(8,128)(2,1)S(1)}, u32[]{:S(2)}) copy-start(bf16[2,128,128]{2,1,0:T(8,128)(2,1)S(1)} %collective-permute-done.1.high_ref) | copy-start | bytes 196612
  18.7 13.0 %all-to-all-start.1 = ((bf16[8,160,128]{2,1,0:T(8,128)(2,1)}), bf16[8,160,128]{2,1,0:T(8,128)(2,1)S(1)}, u32[]{:S(2)}, u32[]{:S(2)}) async-start(bf16[8,160,128]{2,1,0:T(8,128)(2,1)} %get-tuple-element.50), calls=%async_computation.1 | async-start | bytes 655360 | tf_op jit(solution)/shard_map/all_to_all | solution.py:558
  25.2 1.2 %copy-start.1 = (bf16[2048,256]{1,0:T(8,128)(2,1)S(1)}, bf16[2048,256]{1,0:T(8,128)(2,1)}, u32[]{:S(2)}) copy-start(bf16[2048,256]{1,0:T(8,128)(2,1)} %q_ref.3) | copy-start | bytes 3145732
  26.4 1.2 %copy-start.2 = (bf16[2048,256]{1,0:T(8,128)(2,1)S(1)}, bf16[2048,256]{1,0:T(8,128)(2,1)}, u32[]{:S(2)}) copy-start(bf16[2048,256]{1,0:T(8,128)(2,1)} %g_ref.3) | copy-start | bytes 3145732
  31.7 25.4 %copy-start.4 = (bf16[8,160,128]{2,1,0:T(8,128)(2,1)}, bf16[8,160,128]{2,1,0:T(8,128)(2,1)S(1)}, u32[]{:S(2)}) copy-start(bf16[8,160,128]{2,1,0:T(8,128)(2,1)S(1)} %all-to-all-done.1.mine_ref) | copy-start | bytes 983044
  31.7 5.1 %collective-permute-start.2 = (bf16[8,160,128]{2,1,0:T(8,128)(2,1)S(1)}, bf16[8,160,128]{2,1,0:T(8,128)(2,1)S(1)}, u32[]{:S(2)}, u32[]{:S(2)}) collective-permute-start(bf16[8,160,128]{2,1,0:T(8,128)(2,1)S(1)} %all-to-all-done.1.mine_ref), channel_id=1, source_target_pairs={{0,1},{1,0},{2,3},{3,2},{4,5},{5,4},{6,7},{7,6},{8,9},{9,8},{10,11... | collective-permute-start | bytes 983048 | tf_op jit(solution)/shard_map/ppermute | solution.py:583
  36.8 20.2 %copy-start.5 = (bf16[8,160,128]{2,1,0:T(8,128)(2,1)}, bf16[8,160,128]{2,1,0:T(8,128)(2,1)S(1)}, u32[]{:S(2)}) copy-start(bf16[8,160,128]{2,1,0:T(8,128)(2,1)S(1)} %collective-permute-done.2.other_ref) | copy-start | bytes 983044
  47.0 10.0 %collective-permute-start.5 = (bf16[12,2,32,128]{3,2,1,0:T(8,128)(2,1)S(1)}, bf16[12,2,32,128]{3,2,1,0:T(8,128)(2,1)S(1)}, u32[]{:S(2)}, u32[]{:S(2)}) collective-permute-start(bf16[12,2,32,128]{3,2,1,0:T(8,128)(2,1)S(1)} %get-tuple-element.61), channel_id=1, source_target_pairs={{0,3},{1,2},{2,1},{3,0},{4,7},{5,6},{6,5},{7,4},{8,11},{9,10},{10,... | collective-permute-start | bytes 589832 | tf_op jit(solution)/shard_map/ppermute | solution.py:645
  48.4 9.2 %collective-permute-start.3 = (bf16[12,2,32,128]{3,2,1,0:T(8,128)(2,1)S(1)}, bf16[12,2,32,128]{3,2,1,0:T(8,128)(2,1)S(1)}, u32[]{:S(2)}, u32[]{:S(2)}) collective-permute-start(bf16[12,2,32,128]{3,2,1,0:T(8,128)(2,1)S(1)} %get-tuple-element.59), channel_id=1, source_target_pairs={{0,1},{1,0},{2,3},{3,2},{4,5},{5,4},{6,7},{7,6},{8,9},{9,8},{10,11... | collective-permute-start | bytes 589832 | tf_op jit(solution)/shard_map/ppermute | solution.py:645
  48.7 9.1 %collective-permute-start.4 = (bf16[12,2,32,128]{3,2,1,0:T(8,128)(2,1)S(1)}, bf16[12,2,32,128]{3,2,1,0:T(8,128)(2,1)S(1)}, u32[]{:S(2)}, u32[]{:S(2)}) collective-permute-start(bf16[12,2,32,128]{3,2,1,0:T(8,128)(2,1)S(1)} %get-tuple-element.60), channel_id=1, source_target_pairs={{0,2},{1,3},{2,0},{3,1},{4,6},{5,7},{6,4},{7,5},{8,10},{9,11},{10,... | collective-permute-start | bytes 589832 | tf_op jit(solution)/shard_map/ppermute | solution.py:645
  57.1 6.7 %collective-permute-start.8 = (bf16[16,2,64,128]{3,2,1,0:T(8,128)(2,1)}, bf16[16,2,64,128]{3,2,1,0:T(8,128)(2,1)S(1)}, u32[]{:S(2)}, u32[]{:S(2)}) collective-permute-start(bf16[16,2,64,128]{3,2,1,0:T(8,128)(2,1)} %get-tuple-element.75), channel_id=1, source_target_pairs={{0,1},{1,0},{2,3},{3,2},{4,5},{5,4},{6,7},{7,6},{8,9},{9,8},{10,11... | collective-permute-start | bytes 1572872 | tf_op jit(solution)/shard_map/ppermute | solution.py:630
  58.6 17.0 %all-to-all-start.2 = ((bf16[8,6,32,128]{3,2,1,0:T(8,128)(2,1)}), bf16[8,6,32,128]{3,2,1,0:T(8,128)(2,1)S(1)}, u32[]{:S(2)}, u32[]{:S(2)}) async-start(bf16[8,6,32,128]{3,2,1,0:T(8,128)(2,1)} %get-tuple-element.66), calls=%async_computation.2 | async-start | bytes 786432 | tf_op jit(solution)/shard_map/all_to_all | solution.py:687
  64.9 10.8 %collective-permute-start.9 = (bf16[16,2,32,128]{3,2,1,0:T(8,128)(2,1)S(1)}, bf16[16,2,32,128]{3,2,1,0:T(8,128)(2,1)S(1)}, u32[]{:S(2)}, u32[]{:S(2)}) collective-permute-start(bf16[16,2,32,128]{3,2,1,0:T(8,128)(2,1)S(1)} %get-tuple-element.77), channel_id=1, source_target_pairs={{0,2},{1,3},{2,0},{3,1},{4,6},{5,7},{6,4},{7,5},{8,10},{9,11},{10,... | collective-permute-start | bytes 786440 | tf_op jit(solution)/shard_map/ppermute | solution.py:641
  66.2 9.5 %collective-permute-start.6 = (bf16[2,32,128]{2,1,0:T(8,128)(2,1)S(1)}, bf16[2,32,128]{2,1,0:T(8,128)(2,1)S(1)}, u32[]{:S(2)}, u32[]{:S(2)}) collective-permute-start(bf16[2,32,128]{2,1,0:T(8,128)(2,1)S(1)} %get-tuple-element.72), channel_id=1, source_target_pairs={{0,4},{4,0},{8,12},{12,8},{16,20},{20,16},{24,28},{28,24},{1,5},{5... | collective-permute-start | bytes 49160 | tf_op jit(solution)/shard_map/ppermute | solution.py:688
  66.2 9.5 %collective-permute-start.7 = (bf16[2,32,128]{2,1,0:T(8,128)(2,1)S(1)}, bf16[2,32,128]{2,1,0:T(8,128)(2,1)S(1)}, u32[]{:S(2)}, u32[]{:S(2)}) collective-permute-start(bf16[2,32,128]{2,1,0:T(8,128)(2,1)S(1)} %get-tuple-element.73), channel_id=1, source_target_pairs={{4,8},{8,4},{12,16},{16,12},{20,24},{24,20},{5,9},{9,5},{13,17},{1... | collective-permute-start | bytes 49160 | tf_op jit(solution)/shard_map/ppermute | solution.py:689
  70.5 5.2 %copy-start.10 = (s32[2]{0:T(128)S(1)}, s32[2]{0:T(128)}, u32[]{:S(2)}) copy-start(s32[2]{0:T(128)} %global_blocks.5) | copy-start | bytes 28
  70.5 5.2 %copy-start.11 = (s32[8]{0:T(128)S(1)}, s32[8]{0:T(128)}, u32[]{:S(2)}) copy-start(s32[8]{0:T(128)} %get-tuple-element.70.requested) | copy-start | bytes 100
  76.5 8.2 %collective-permute-start.10 = (bf16[16,2,32,128]{3,2,1,0:T(8,128)(2,1)S(1)}, bf16[16,2,32,128]{3,2,1,0:T(8,128)(2,1)S(1)}, u32[]{:S(2)}, u32[]{:S(2)}) collective-permute-start(bf16[16,2,32,128]{3,2,1,0:T(8,128)(2,1)S(1)} %settle.1.refs_0_), channel_id=1, source_target_pairs={{0,2},{1,3},{2,0},{3,1},{4,6},{5,7},{6,4},{7,5},{8,10},{9,11},{10,... | collective-permute-start | bytes 786440 | tf_op jit(solution)/shard_map/ppermute | solution.py:703
  76.9 8.5 %collective-permute-start.11 = (bf16[16,2,32,128]{3,2,1,0:T(8,128)(2,1)S(1)}, bf16[16,2,32,128]{3,2,1,0:T(8,128)(2,1)S(1)}, u32[]{:S(2)}, u32[]{:S(2)}) collective-permute-start(bf16[16,2,32,128]{3,2,1,0:T(8,128)(2,1)S(1)} %settle.1.refs_0_), channel_id=1, source_target_pairs={{0,1},{1,0},{2,3},{3,2},{4,5},{5,4},{6,7},{7,6},{8,9},{9,8},{10,11... | collective-permute-start | bytes 786440 | tf_op jit(solution)/shard_map/ppermute | solution.py:707
  84.7 1.8 %collective-permute-start.12 = (bf16[16,2,32,128]{3,2,1,0:T(8,128)(2,1)S(1)}, bf16[16,2,32,128]{3,2,1,0:T(8,128)(2,1)S(1)}, u32[]{:S(2)}, u32[]{:S(2)}) collective-permute-start(bf16[16,2,32,128]{3,2,1,0:T(8,128)(2,1)S(1)} %collective-permute-done.10.refs_2_), channel_id=1, source_target_pairs={{0,1},{1,0},{2,3},{3,2},{4,5},{5,4},{6,7},{7,6},{8,9},{9,8},{10,11... | collective-permute-start | bytes 786440 | tf_op jit(solution)/shard_map/ppermute | solution.py:707
  (5 other events, 4.5 us)

commit v7 on v6

--- a/solution.py
+++ b/solution.py
@@ -64,7 +64,7 @@
 
 
 def ask_kernel(
-    global_blocks, random_blocks, random_ref, k_ref, v_ref, out_ref, low_ref, high_ref, owners, rows, sems
+    global_blocks, random_ref, k_ref, v_ref, out_ref, low_ref, high_ref, rows, sems
 ):
     tokens = k_ref.shape[0]
     blocks = tokens // BLOCK
@@ -98,9 +98,6 @@
         return carry
 
     lax.fori_loop(0, peers, mark, 0, unroll=min(peers, 8))
-    for b in range(blocks):
-        for r in range(R):
-            owners[b * R + r] = lax.div(random_blocks[r, b], blocks)
     for copy in copies:
         copy.wait()
     out_ref[:slices, MARKS:, :] = rows[...].reshape(slices, size, DH)
@@ -437,7 +434,7 @@
 
 
 def queries_kernel(
-    first, owners, k_ref, low_ref, high_ref, mine_ref, other_ref, dsw_ref, dsf_ref, *refs
+    first, random_blocks, k_ref, low_ref, high_ref, mine_ref, other_ref, dsw_ref, dsf_ref, *refs
 ):
     *_, dq_ref, k_all, kt_all = refs
     blocks = k_ref.shape[0] // BLOCK
@@ -472,7 +469,7 @@
     for u in range(per):
         b = first + step * per + u
         panels = [b + w for w in range(WINDOW)]
-        panels += [first_random + owners[b * R + r] for r in range(R)]
+        panels += [first_random + lax.div(random_blocks[r, b], blocks) for r in range(R)]
         panels += [first_global + j for j in range(G)]
         turned = [kt_all[i] for i in panels]
         dqt = mm(jnp.concatenate(turned[:WINDOW], axis=1), dsw_ref[u], NN)
@@ -521,23 +518,22 @@
 
     edge = (2, BLOCK, DH)
     _, size = glob_slices(seq_count)
-    asking, to_low, to_high, owners = pl.pallas_call(
+    asking, to_low, to_high = pl.pallas_call(
         ask_kernel,
         out_shape=(
             sds((seq_count, MARKS + size, DH), bf16),
             sds(edge, bf16),
             sds(edge, bf16),
-            sds((blocks * R,), jnp.int32),
         ),
-        in_specs=[smem, smem, vmem, hbm, hbm],
-        out_specs=(vmem, vmem, vmem, smem),
+        in_specs=[smem, vmem, hbm, hbm],
+        out_specs=(vmem, vmem, vmem),
         scratch_shapes=[
             pltpu.VMEM((2 * G * HALF, DH), bf16),
             pltpu.SemaphoreType.DMA((2 * G + 4,)),
         ],
         compiler_params=large,
         name="ask",
-    )(global_blocks, random_blocks.T, random_blocks.T, key_vectors, value_vectors)
+    )(global_blocks, random_blocks.T, key_vectors, value_vectors)
     asked = lax.all_to_all(asking, "seq", split_axis=0, concat_axis=0, tiled=True)
 
     low_pairs = [(i, i ^ 1) for i in range(seq_count)]
@@ -681,7 +677,7 @@
                 flops=LISTED * unit // 2, bytes_accessed=4 * MIB, transcendentals=0
             ),
             name="queries",
-        )(owners, key_vectors, low, high, mine, other, dsw, dsf, *done)
+        )(random_blocks.T, key_vectors, low, high, mine, other, dsw, dsf, *done)
 
     query_grad = queries(0, dsw, ())
     back = lax.all_to_all(terms, "seq", split_axis=0, concat_axis=0, tiled=True)

time: 88.6 us -> 88.7 us (level)
  no operation moved by 1% of the time
where the time goes in v7:
time: 88.7 us; the launch traced here: 87.6 us
  Pallas kernels  39 us (44%)
  starting transfers between devices  35.6 us (40%)
  local copies, waits for them, and re-layouts  6.95 us (8%)
  waiting for transfers between devices  3.55 us (4%)
  other arithmetic  1.68 us (2%)
    pallas_call x2, Pallas kernels, queries(): pl.pallas_call(functools.partial(queries_kernel, shift * per), out_shape=...  10.4 us
    pallas_call x1, Pallas kernels, body(): pl.pallas_call(far_kernel, out_shape=(sds((blocks * SPARE, FAR * BLOCK, l...  9.52 us
    pallas_call x1, Pallas kernels, body(): pl.pallas_call(close_kernel, out_shape=(sds((blocks, WINDOW * BLOCK, lane...  8.05 us
    unnamed x26, local copies, waits for them, and re-layouts  6.95 us
    all_to_all x1, starting transfers between devices, body(): lax.all_to_all(asking, 'seq', split_axis=0, concat_axis=0, tiled=True)  5.79 us
    all_to_all x1, starting transfers between devices, body(): lax.all_to_all(served, 'seq', split_axis=0, concat_axis=0, tiled=True)  5.42 us
    all_to_all x1, starting transfers between devices, body(): back = lax.all_to_all(terms, 'seq', split_axis=0, concat_axis=0, tiled=True)  5.12 us
    ppermute x1, starting transfers between devices, body(): from_high = lax.ppermute(to_high, 'seq', high_pairs)  4.25 us
  transfers between devices with their start and end apart: 16, of which 3 were waited for; matrix products, arithmetic and copies ran while one was open for 2% of the time, Pallas kernels for 26%

profile of v7, /device:TPU:5, one launch (start us, length us, event | category | flops | bytes accessed | tf_op | source)
XLA Modules:
  0.0 87.6 jit_solution(16838978817827556890)
XLA Ops:
  0.6 2.3 %ask.1 = (bf16[8,48,128]{2,1,0:T(8,128)(2,1)}, bf16[2,128,128]{2,1,0:T(8,128)(2,1)}, bf16[2,128,128]{2,1,0:T(8,128)(2,1)}) custom-call(s32[2]{0:T(128)} %global_blocks.5, s32[3,16]{1,0:T(4,128)} %bitcast.1, bf16[2048,128]{1,0:T(8,128)(2,1)} %k_ref.11, bf16[2048,128]{1,0:T(8,128)(2,1)} %v_ref.7), custom_call_target="tpu_custom_call" | custom-call | tf_op jit(solution)/shard_map/ask/pallas_call | solution.py:521
  3.0 5.8 %all-to-all-start = ((bf16[8,48,128]{2,1,0:T(8,128)(2,1)}), bf16[8,48,128]{2,1,0:T(8,128)(2,1)S(1)}, u32[]{:S(2)}, u32[]{:S(2)}) async-start(bf16[8,48,128]{2,1,0:T(8,128)(2,1)} %get-tuple-element.43), calls=%async_computation | async-start | bytes 196608 | tf_op jit(solution)/shard_map/all_to_all | solution.py:537
  8.8 4.2 %collective-permute-start.1 = (bf16[2,128,128]{2,1,0:T(8,128)(2,1)}, bf16[2,128,128]{2,1,0:T(8,128)(2,1)S(1)}, u32[]{:S(2)}, u32[]{:S(2)}) collective-permute-start(bf16[2,128,128]{2,1,0:T(8,128)(2,1)} %get-tuple-element.45), channel_id=1, source_target_pairs={{4,8},{8,4},{12,16},{16,12},{20,24},{24,20},{5,9},{9,5},{13,17},{1... | collective-permute-start | bytes 196616 | tf_op jit(solution)/shard_map/ppermute | solution.py:542
  13.0 2.1 %collective-permute-done.1.high_ref = bf16[2,128,128]{2,1,0:T(8,128)(2,1)S(1)} collective-permute-done((bf16[2,128,128]{2,1,0:T(8,128)(2,1)}, bf16[2,128,128]{2,1,0:T(8,128)(2,1)S(1)}, u32[]{:S(2)}, u32[]{:S(2)}) %collective-permute-start.1) | collective-permute-done | bytes 65568 | tf_op jit(solution)/shard_map/ppermute | solution.py:542
  15.8 2.8 %serve.1 = (bf16[8,160,128]{2,1,0:T(8,128)(2,1)}, s32[8]{0:T(128)}) custom-call(s32[2]{0:T(128)} %global_blocks.5, bf16[8,48,128]{2,1,0:T(8,128)(2,1)} %copy-done.12, bf16[2048,128]{1,0:T(8,128)(2,1)} %k_ref.11, bf16[2048,128]{1,0:T(8,128)(2,1)} %v_ref.7), custom_call_target="tpu_custom_call" | custom-call | tf_op jit(solution)/shard_map/serve/pallas_call | solution.py:545
  18.7 5.4 %all-to-all-start.1 = ((bf16[8,160,128]{2,1,0:T(8,128)(2,1)}), bf16[8,160,128]{2,1,0:T(8,128)(2,1)S(1)}, u32[]{:S(2)}, u32[]{:S(2)}) async-start(bf16[8,160,128]{2,1,0:T(8,128)(2,1)} %get-tuple-element.49), calls=%async_computation.1 | async-start | bytes 655360 | tf_op jit(solution)/shard_map/all_to_all | solution.py:554
  24.1 1.0 %copy-done = bf16[2048,128]{1,0:T(8,128)(2,1)S(1)} copy-done((bf16[2048,128]{1,0:T(8,128)(2,1)S(1)}, bf16[2048,128]{1,0:T(8,128)(2,1)}, u32[]{:S(2)}) %copy-start) | copy-done | bytes 524312
  25.1 1.2 %copy-done.1 = bf16[2048,256]{1,0:T(8,128)(2,1)S(1)} copy-done((bf16[2048,256]{1,0:T(8,128)(2,1)S(1)}, bf16[2048,256]{1,0:T(8,128)(2,1)}, u32[]{:S(2)}) %copy-start.1) | copy-done | bytes 1048600
  26.4 1.2 %copy-done.2 = bf16[2048,256]{1,0:T(8,128)(2,1)S(1)} copy-done((bf16[2048,256]{1,0:T(8,128)(2,1)S(1)}, bf16[2048,256]{1,0:T(8,128)(2,1)}, u32[]{:S(2)}) %copy-start.2) | copy-done | bytes 1048600
  27.6 1.0 %copy-done.3 = bf16[2048,128]{1,0:T(8,128)(2,1)S(1)} copy-done((bf16[2048,128]{1,0:T(8,128)(2,1)S(1)}, bf16[2048,128]{1,0:T(8,128)(2,1)}, u32[]{:S(2)}) %copy-start.3) | copy-done | bytes 524312
  28.6 3.0 %near.1.st_ref = f32[16,16,256]{2,1,0:T(8,128)S(1)} custom-call(bf16[2048,256]{1,0:T(8,128)(2,1)S(1)} %copy-done.1, bf16[2048,256]{1,0:T(8,128)(2,1)S(1)} %copy-done.2, bf16[2048,128]{1,0:T(8,128)(2,1)S(1)} %copy-done, bf16[2048,128]{1,0:T(8,128)(2,1)S(1)} %copy-done.3, bf16[2,128,128]{2,1,0:T(8,128)(2,1)S(1)} %collective-permute-done.low_ref, ...), custom_call_target="tpu_custom_call" | custom-call | flops 805306368 | bytes 4194304 | tf_op jit(solution)/shard_map/near/pallas_call | solution.py:561
  31.6 3.4 %collective-permute-start.2 = (bf16[8,160,128]{2,1,0:T(8,128)(2,1)S(1)}, bf16[8,160,128]{2,1,0:T(8,128)(2,1)S(1)}, u32[]{:S(2)}, u32[]{:S(2)}) collective-permute-start(bf16[8,160,128]{2,1,0:T(8,128)(2,1)S(1)} %all-to-all-done.1.mine_ref), channel_id=1, source_target_pairs={{0,1},{1,0},{2,3},{3,2},{4,5},{5,4},{6,7},{7,6},{8,9},{9,8},{10,11... | collective-permute-start | bytes 983048 | tf_op jit(solution)/shard_map/ppermute | solution.py:579
  35.1 1.7 %broadcast_select_fusion = (bf16[2048,256]{1,0:T(8,128)(2,1)S(1)}, bf16[2048,256]{1,0:T(8,128)(2,1)S(1)}) fusion(bf16[2048,256]{1,0:T(8,128)(2,1)} %g_ref.3, pred[]{:T(512)S(6)} %lt.3, bf16[2048,256]{1,0:T(8,128)(2,1)} %q_ref.3), kind=kLoop, calls=%fused_computation | loop fusion | flops 1048576 | bytes 4194305 | tf_op jit(solution)/shard_map/jit(_where)/select_n | solution.py:578
  37.5 9.5 %far.1 = (bf16[80,640,256]{2,1,0:T(8,128)(2,1)}, f32[1600,8,256]{2,1,0:T(8,128)}, bf16[12,2,32,128]{3,2,1,0:T(8,128)(2,1)S(1)}, bf16[12,2,32,128]{3,2,1,0:T(8,12...) custom-call(s32[3,16]{1,0:T(4,128)S(1)} %bitcast.4, ...), custom_call_target="tpu_custom_call" | custom-call | flops 3355443200 | bytes 8388608 | tf_op jit(solution)/shard_map/far/pallas_call | solution.py:583
  47.0 1.3 %collective-permute-start.5 = (bf16[12,2,32,128]{3,2,1,0:T(8,128)(2,1)S(1)}, bf16[12,2,32,128]{3,2,1,0:T(8,128)(2,1)S(1)}, u32[]{:S(2)}, u32[]{:S(2)}) collective-permute-start(bf16[12,2,32,128]{3,2,1,0:T(8,128)(2,1)S(1)} %get-tuple-element.60), channel_id=1, source_target_pairs={{0,3},{1,2},{2,1},{3,0},{4,7},{5,6},{6,5},{7,4},{8,11},{9,10},{10,... | collective-permute-start | bytes 589832 | tf_op jit(solution)/shard_map/ppermute | solution.py:641
  48.9 8.1 %close.1 = (bf16[16,384,256]{2,1,0:T(8,128)(2,1)}, bf16[16,2,64,128]{3,2,1,0:T(8,128)(2,1)}, bf16[16,2,64,128]{3,2,1,0:T(8,128)(2,1)}) custom-call(bf16[2048,256]{1,0:T(8,128)(2,1)} %q_ref.3, bf16[2048,256]{1,0:T(8,128)(2,1)} %g_ref.3, bf16[2048,128]{1,0:T(8,128)(2,1)} %k_ref.11, bf16[2048,128]{1,0:T(8,128)(2,1)} %v_ref.7, bf16[2,128,128]{2,1,0:T(8,128)(2,1)} %copy-done.6, ...), custom_call_target="tpu_custom_call" | custom-call | flops 1610612736 | bytes 8388608 | tf_op jit(solution)/shard_map/close/pallas_call | solution.py:611
  58.6 5.1 %all-to-all-start.2 = ((bf16[8,6,32,128]{3,2,1,0:T(8,128)(2,1)}), bf16[8,6,32,128]{3,2,1,0:T(8,128)(2,1)S(1)}, u32[]{:S(2)}, u32[]{:S(2)}) async-start(bf16[8,6,32,128]{3,2,1,0:T(8,128)(2,1)} %get-tuple-element.65), calls=%async_computation.2 | async-start | bytes 786432 | tf_op jit(solution)/shard_map/all_to_all | solution.py:683
  64.9 1.3 %collective-permute-start.9 = (bf16[16,2,32,128]{3,2,1,0:T(8,128)(2,1)S(1)}, bf16[16,2,32,128]{3,2,1,0:T(8,128)(2,1)S(1)}, u32[]{:S(2)}, u32[]{:S(2)}) collective-permute-start(bf16[16,2,32,128]{3,2,1,0:T(8,128)(2,1)S(1)} %get-tuple-element.75), channel_id=1, source_target_pairs={{0,2},{1,3},{2,0},{3,1},{4,6},{5,7},{6,4},{7,5},{8,10},{9,11},{10,... | collective-permute-start | bytes 786440 | tf_op jit(solution)/shard_map/ppermute | solution.py:637
  66.2 4.3 %collective-permute-start.7 = (bf16[2,32,128]{2,1,0:T(8,128)(2,1)S(1)}, bf16[2,32,128]{2,1,0:T(8,128)(2,1)S(1)}, u32[]{:S(2)}, u32[]{:S(2)}) collective-permute-start(bf16[2,32,128]{2,1,0:T(8,128)(2,1)S(1)} %get-tuple-element.71), channel_id=1, source_target_pairs={{4,8},{8,4},{12,16},{16,12},{20,24},{24,20},{5,9},{9,5},{13,17},{1... | collective-permute-start | bytes 49160 | tf_op jit(solution)/shard_map/ppermute | solution.py:685
  70.4 5.2 %queries.2.refs_0_ = bf16[2048,256]{1,0:T(8,128)(2,1)} custom-call(s32[3,16]{1,0:T(4,128)} %bitcast.2, bf16[2048,128]{1,0:T(8,128)(2,1)} %k_ref.11, bf16[2,128,128]{2,1,0:T(8,128)(2,1)} %copy-done.6, bf16[2,128,128]{2,1,0:T(8,128)(2,1)} %copy-done.7, bf16[8,160,128]{2,1,0:T(8,128)(2,1)} %copy-done.4, bf16[8,160,128]{2,1,0:T(8,128)(2,1)} %copy-done.5, ...), custom_call_target="tpu_custom_call" | custom-call | flops 536870912 | bytes 4194304 | tf_op jit(solution)/shard_map/queries/pallas_call | solution.py:662
  76.9 2.7 %collective-permute-start.11 = (bf16[16,2,32,128]{3,2,1,0:T(8,128)(2,1)S(1)}, bf16[16,2,32,128]{3,2,1,0:T(8,128)(2,1)S(1)}, u32[]{:S(2)}, u32[]{:S(2)}) collective-permute-start(bf16[16,2,32,128]{3,2,1,0:T(8,128)(2,1)S(1)} %settle.1.refs_0_), channel_id=1, source_target_pairs={{0,1},{1,0},{2,3},{3,2},{4,5},{5,4},{6,7},{7,6},{8,9},{9,8},{10,11... | collective-permute-start | bytes 786440 | tf_op jit(solution)/shard_map/ppermute | solution.py:703
  79.5 5.2 %queries.3 = bf16[2048,256]{1,0:T(8,128)(2,1)} custom-call(s32[3,16]{1,0:T(4,128)} %bitcast.3, bf16[2048,128]{1,0:T(8,128)(2,1)} %k_ref.11, bf16[2,128,128]{2,1,0:T(8,128)(2,1)} %copy-done.6, bf16[2,128,128]{2,1,0:T(8,128)(2,1)} %copy-done.7, bf16[8,160,128]{2,1,0:T(8,128)(2,1)} %copy-done.4, ...), custom_call_target="tpu_custom_call", output_to_operand_aliasing={{}: (8, {})} | custom-call | flops 536870912 | bytes 4194304 | tf_op jit(solution)/shard_map/queries/pallas_call | solution.py:662
  85.4 1.2 %collective-permute-done.12.refs_3_ = bf16[16,2,32,128]{3,2,1,0:T(8,128)(2,1)S(1)} collective-permute-done((bf16[16,2,32,128]{3,2,1,0:T(8,128)(2,1)S(1)}, bf16[16,2,32,128]{3,2,1,0:T(8,128)(2,1)S(1)}, u32[]{:S(2)}, u32[]{:S(2)}) %collective-permute-start.12) | collective-permute-done | bytes 262176 | tf_op jit(solution)/shard_map/ppermute | solution.py:703
  86.5 1.1 %join.1 = (bf16[2048,128]{1,0:T(8,128)(2,1)}, bf16[2048,128]{1,0:T(8,128)(2,1)}) custom-call(bf16[16,2,32,128]{3,2,1,0:T(8,128)(2,1)S(1)} %settle.1.refs_0_, bf16[16,2,32,128]{3,2,1,0:T(8,128)(2,1)S(1)} %collective-permute-done.11.refs_1_, bf16[16,2,32,128]{3,2,1,0:T(8,128)(2,1)S(1)} %collective-permute-done.10.refs_2_, ...), custom_call_target="tpu_custom_call" | custom-call | tf_op jit(solution)/shard_map/join/pallas_call | solution.py:704
  (46 shorter events, 6.6 us)
Async XLA Ops:
  3.0 12.2 %all-to-all-start = ((bf16[8,48,128]{2,1,0:T(8,128)(2,1)}), bf16[8,48,128]{2,1,0:T(8,128)(2,1)S(1)}, u32[]{:S(2)}, u32[]{:S(2)}) async-start(bf16[8,48,128]{2,1,0:T(8,128)(2,1)} %get-tuple-element.43), calls=%async_computation | async-start | bytes 196608 | tf_op jit(solution)/shard_map/all_to_all | solution.py:537
  8.8 4.3 %collective-permute-start = (bf16[2,128,128]{2,1,0:T(8,128)(2,1)}, bf16[2,128,128]{2,1,0:T(8,128)(2,1)S(1)}, u32[]{:S(2)}, u32[]{:S(2)}) collective-permute-start(bf16[2,128,128]{2,1,0:T(8,128)(2,1)} %get-tuple-element.44), channel_id=1, source_target_pairs={{0,4},{4,0},{8,12},{12,8},{16,20},{20,16},{24,28},{28,24},{1,5},{5... | collective-permute-start | bytes 196616 | tf_op jit(solution)/shard_map/ppermute | solution.py:541
  8.8 6.4 %collective-permute-start.1 = (bf16[2,128,128]{2,1,0:T(8,128)(2,1)}, bf16[2,128,128]{2,1,0:T(8,128)(2,1)S(1)}, u32[]{:S(2)}, u32[]{:S(2)}) collective-permute-start(bf16[2,128,128]{2,1,0:T(8,128)(2,1)} %get-tuple-element.45), channel_id=1, source_target_pairs={{4,8},{8,4},{12,16},{16,12},{20,24},{24,20},{5,9},{9,5},{13,17},{1... | collective-permute-start | bytes 196616 | tf_op jit(solution)/shard_map/ppermute | solution.py:542
  13.0 35.9 %copy-start.6 = (bf16[2,128,128]{2,1,0:T(8,128)(2,1)}, bf16[2,128,128]{2,1,0:T(8,128)(2,1)S(1)}, u32[]{:S(2)}) copy-start(bf16[2,128,128]{2,1,0:T(8,128)(2,1)S(1)} %collective-permute-done.low_ref) | copy-start | bytes 196612
  15.2 33.7 %copy-start.7 = (bf16[2,128,128]{2,1,0:T(8,128)(2,1)}, bf16[2,128,128]{2,1,0:T(8,128)(2,1)S(1)}, u32[]{:S(2)}) copy-start(bf16[2,128,128]{2,1,0:T(8,128)(2,1)S(1)} %collective-permute-done.1.high_ref) | copy-start | bytes 196612
  18.7 13.0 %all-to-all-start.1 = ((bf16[8,160,128]{2,1,0:T(8,128)(2,1)}), bf16[8,160,128]{2,1,0:T(8,128)(2,1)S(1)}, u32[]{:S(2)}, u32[]{:S(2)}) async-start(bf16[8,160,128]{2,1,0:T(8,128)(2,1)} %get-tuple-element.49), calls=%async_computation.1 | async-start | bytes 655360 | tf_op jit(solution)/shard_map/all_to_all | solution.py:554
  25.1 1.2 %copy-start.1 = (bf16[2048,256]{1,0:T(8,128)(2,1)S(1)}, bf16[2048,256]{1,0:T(8,128)(2,1)}, u32[]{:S(2)}) copy-start(bf16[2048,256]{1,0:T(8,128)(2,1)} %q_ref.3) | copy-start | bytes 3145732
  26.3 1.2 %copy-start.2 = (bf16[2048,256]{1,0:T(8,128)(2,1)S(1)}, bf16[2048,256]{1,0:T(8,128)(2,1)}, u32[]{:S(2)}) copy-start(bf16[2048,256]{1,0:T(8,128)(2,1)} %g_ref.3) | copy-start | bytes 3145732
  31.6 25.3 %copy-start.4 = (bf16[8,160,128]{2,1,0:T(8,128)(2,1)}, bf16[8,160,128]{2,1,0:T(8,128)(2,1)S(1)}, u32[]{:S(2)}) copy-start(bf16[8,160,128]{2,1,0:T(8,128)(2,1)S(1)} %all-to-all-done.1.mine_ref) | copy-start | bytes 983044
  31.6 5.1 %collective-permute-start.2 = (bf16[8,160,128]{2,1,0:T(8,128)(2,1)S(1)}, bf16[8,160,128]{2,1,0:T(8,128)(2,1)S(1)}, u32[]{:S(2)}, u32[]{:S(2)}) collective-permute-start(bf16[8,160,128]{2,1,0:T(8,128)(2,1)S(1)} %all-to-all-done.1.mine_ref), channel_id=1, source_target_pairs={{0,1},{1,0},{2,3},{3,2},{4,5},{5,4},{6,7},{7,6},{8,9},{9,8},{10,11... | collective-permute-start | bytes 983048 | tf_op jit(solution)/shard_map/ppermute | solution.py:579
  36.8 20.2 %copy-start.5 = (bf16[8,160,128]{2,1,0:T(8,128)(2,1)}, bf16[8,160,128]{2,1,0:T(8,128)(2,1)S(1)}, u32[]{:S(2)}) copy-start(bf16[8,160,128]{2,1,0:T(8,128)(2,1)S(1)} %collective-permute-done.2.other_ref) | copy-start | bytes 983044
  47.0 10.0 %collective-permute-start.5 = (bf16[12,2,32,128]{3,2,1,0:T(8,128)(2,1)S(1)}, bf16[12,2,32,128]{3,2,1,0:T(8,128)(2,1)S(1)}, u32[]{:S(2)}, u32[]{:S(2)}) collective-permute-start(bf16[12,2,32,128]{3,2,1,0:T(8,128)(2,1)S(1)} %get-tuple-element.60), channel_id=1, source_target_pairs={{0,3},{1,2},{2,1},{3,0},{4,7},{5,6},{6,5},{7,4},{8,11},{9,10},{10,... | collective-permute-start | bytes 589832 | tf_op jit(solution)/shard_map/ppermute | solution.py:641
  48.3 9.2 %collective-permute-start.3 = (bf16[12,2,32,128]{3,2,1,0:T(8,128)(2,1)S(1)}, bf16[12,2,32,128]{3,2,1,0:T(8,128)(2,1)S(1)}, u32[]{:S(2)}, u32[]{:S(2)}) collective-permute-start(bf16[12,2,32,128]{3,2,1,0:T(8,128)(2,1)S(1)} %get-tuple-element.58), channel_id=1, source_target_pairs={{0,1},{1,0},{2,3},{3,2},{4,5},{5,4},{6,7},{7,6},{8,9},{9,8},{10,11... | collective-permute-start | bytes 589832 | tf_op jit(solution)/shard_map/ppermute | solution.py:641
  48.7 9.1 %collective-permute-start.4 = (bf16[12,2,32,128]{3,2,1,0:T(8,128)(2,1)S(1)}, bf16[12,2,32,128]{3,2,1,0:T(8,128)(2,1)S(1)}, u32[]{:S(2)}, u32[]{:S(2)}) collective-permute-start(bf16[12,2,32,128]{3,2,1,0:T(8,128)(2,1)S(1)} %get-tuple-element.59), channel_id=1, source_target_pairs={{0,2},{1,3},{2,0},{3,1},{4,6},{5,7},{6,4},{7,5},{8,10},{9,11},{10,... | collective-permute-start | bytes 589832 | tf_op jit(solution)/shard_map/ppermute | solution.py:641
  57.0 6.7 %collective-permute-start.8 = (bf16[16,2,64,128]{3,2,1,0:T(8,128)(2,1)}, bf16[16,2,64,128]{3,2,1,0:T(8,128)(2,1)S(1)}, u32[]{:S(2)}, u32[]{:S(2)}) collective-permute-start(bf16[16,2,64,128]{3,2,1,0:T(8,128)(2,1)} %get-tuple-element.73), channel_id=1, source_target_pairs={{0,1},{1,0},{2,3},{3,2},{4,5},{5,4},{6,7},{7,6},{8,9},{9,8},{10,11... | collective-permute-start | bytes 1572872 | tf_op jit(solution)/shard_map/ppermute | solution.py:626
  58.6 17.1 %all-to-all-start.2 = ((bf16[8,6,32,128]{3,2,1,0:T(8,128)(2,1)}), bf16[8,6,32,128]{3,2,1,0:T(8,128)(2,1)S(1)}, u32[]{:S(2)}, u32[]{:S(2)}) async-start(bf16[8,6,32,128]{3,2,1,0:T(8,128)(2,1)} %get-tuple-element.65), calls=%async_computation.2 | async-start | bytes 786432 | tf_op jit(solution)/shard_map/all_to_all | solution.py:683
  64.9 10.8 %collective-permute-start.9 = (bf16[16,2,32,128]{3,2,1,0:T(8,128)(2,1)S(1)}, bf16[16,2,32,128]{3,2,1,0:T(8,128)(2,1)S(1)}, u32[]{:S(2)}, u32[]{:S(2)}) collective-permute-start(bf16[16,2,32,128]{3,2,1,0:T(8,128)(2,1)S(1)} %get-tuple-element.75), channel_id=1, source_target_pairs={{0,2},{1,3},{2,0},{3,1},{4,6},{5,7},{6,4},{7,5},{8,10},{9,11},{10,... | collective-permute-start | bytes 786440 | tf_op jit(solution)/shard_map/ppermute | solution.py:637
  66.1 9.5 %collective-permute-start.6 = (bf16[2,32,128]{2,1,0:T(8,128)(2,1)S(1)}, bf16[2,32,128]{2,1,0:T(8,128)(2,1)S(1)}, u32[]{:S(2)}, u32[]{:S(2)}) collective-permute-start(bf16[2,32,128]{2,1,0:T(8,128)(2,1)S(1)} %get-tuple-element.70), channel_id=1, source_target_pairs={{0,4},{4,0},{8,12},{12,8},{16,20},{20,16},{24,28},{28,24},{1,5},{5... | collective-permute-start | bytes 49160 | tf_op jit(solution)/shard_map/ppermute | solution.py:684
  66.2 9.5 %collective-permute-start.7 = (bf16[2,32,128]{2,1,0:T(8,128)(2,1)S(1)}, bf16[2,32,128]{2,1,0:T(8,128)(2,1)S(1)}, u32[]{:S(2)}, u32[]{:S(2)}) collective-permute-start(bf16[2,32,128]{2,1,0:T(8,128)(2,1)S(1)} %get-tuple-element.71), channel_id=1, source_target_pairs={{4,8},{8,4},{12,16},{16,12},{20,24},{24,20},{5,9},{9,5},{13,17},{1... | collective-permute-start | bytes 49160 | tf_op jit(solution)/shard_map/ppermute | solution.py:685
  70.4 5.3 %copy-start.10 = (s32[2]{0:T(128)S(1)}, s32[2]{0:T(128)}, u32[]{:S(2)}) copy-start(s32[2]{0:T(128)} %global_blocks.5) | copy-start | bytes 28
  70.4 5.3 %copy-start.11 = (s32[8]{0:T(128)S(1)}, s32[8]{0:T(128)}, u32[]{:S(2)}) copy-start(s32[8]{0:T(128)} %get-tuple-element.68.requested) | copy-start | bytes 100
  76.5 8.2 %collective-permute-start.10 = (bf16[16,2,32,128]{3,2,1,0:T(8,128)(2,1)S(1)}, bf16[16,2,32,128]{3,2,1,0:T(8,128)(2,1)S(1)}, u32[]{:S(2)}, u32[]{:S(2)}) collective-permute-start(bf16[16,2,32,128]{3,2,1,0:T(8,128)(2,1)S(1)} %settle.1.refs_0_), channel_id=1, source_target_pairs={{0,2},{1,3},{2,0},{3,1},{4,6},{5,7},{6,4},{7,5},{8,10},{9,11},{10,... | collective-permute-start | bytes 786440 | tf_op jit(solution)/shard_map/ppermute | solution.py:699
  76.9 8.5 %collective-permute-start.11 = (bf16[16,2,32,128]{3,2,1,0:T(8,128)(2,1)S(1)}, bf16[16,2,32,128]{3,2,1,0:T(8,128)(2,1)S(1)}, u32[]{:S(2)}, u32[]{:S(2)}) collective-permute-start(bf16[16,2,32,128]{3,2,1,0:T(8,128)(2,1)S(1)} %settle.1.refs_0_), channel_id=1, source_target_pairs={{0,1},{1,0},{2,3},{3,2},{4,5},{5,4},{6,7},{7,6},{8,9},{9,8},{10,11... | collective-permute-start | bytes 786440 | tf_op jit(solution)/shard_map/ppermute | solution.py:703
  84.7 1.8 %collective-permute-start.12 = (bf16[16,2,32,128]{3,2,1,0:T(8,128)(2,1)S(1)}, bf16[16,2,32,128]{3,2,1,0:T(8,128)(2,1)S(1)}, u32[]{:S(2)}, u32[]{:S(2)}) collective-permute-start(bf16[16,2,32,128]{3,2,1,0:T(8,128)(2,1)S(1)} %collective-permute-done.10.refs_2_), channel_id=1, source_target_pairs={{0,1},{1,0},{2,3},{3,2},{4,5},{5,4},{6,7},{7,6},{8,9},{9,8},{10,11... | collective-permute-start | bytes 786440 | tf_op jit(solution)/shard_map/ppermute | solution.py:703
  (5 other events, 4.5 us)
